TPU v7x, 128 devices: a whole 4x4x4 slice. The times are simulated.
128 devices in a mesh: ctx: 8 (over z, core), tp: 16 (over y, x).
Axes of the slice: x: 4, y: 4, z: 4, core: 2. Of those that a mesh axis runs over, the one named last changes fastest.
Arguments:
- hidden: bfloat16 [4, 2048, 2048], P(None, 'ctx'), may hold values from -6 to 6
- segments: int32 [4, 2048], replicated, may hold values from 0 to 3, as said below
- key_attendable: int32 [4, 2048], replicated, may hold values 0 or 1
- attention_gain: bfloat16 [2048], replicated, may hold values from 0.5 to 1.5
- feedforward_gain: bfloat16 [2048], replicated, may hold values from 0.5 to 1.5
- attend_frozen: bfloat16 [3, 2048, 2048], P(None, None, 'tp'), may hold values from -0.125 to 0.125
- output_frozen: bfloat16 [2048, 2048], P('tp'), may hold values from -0.125 to 0.125
- expand_frozen: bfloat16 [2, 2048, 5632], P(None, None, 'tp'), may hold values from -0.125 to 0.125
- reduce_frozen: bfloat16 [5632, 2048], P('tp'), may hold values from -0.078125 to 0.078125
- attend_lower: float32 [3, 2048, 16], replicated, may hold values from -0.125 to 0.125
- attend_upper: float32 [3, 16, 2048], P(None, None, 'tp'), may hold values from -0.6 to 0.6
- attend_magnitude: float32 [3, 2048], P(None, 'tp'), may hold values from 0.8 to 1.6
- output_lower: float32 [2048, 16], P('tp'), may hold values from -0.125 to 0.125
- output_upper: float32 [16, 2048], replicated, may hold values from -0.6 to 0.6
- output_magnitude: float32 [2048], replicated, may hold values from 6 to 14
- expand_lower: float32 [2, 2048, 16], replicated, may hold values from -0.125 to 0.125
- expand_upper: float32 [2, 16, 5632], P(None, None, 'tp'), may hold values from -0.6 to 0.6
- expand_magnitude: float32 [2, 5632], P(None, 'tp'), may hold values from 0.8 to 1.6
- reduce_lower: float32 [5632, 16], P('tp'), may hold values from -0.078125 to 0.078125
- reduce_upper: float32 [16, 2048], replicated, may hold values from -0.6 to 0.6
- reduce_magnitude: float32 [2048], replicated, may hold values from 0.8 to 2
- cotangent: bfloat16 [4, 2048, 2048], P(None, 'ctx'), may hold values from -6 to 6
Outputs:
- block_output: bfloat16 [4, 2048, 2048], P(None, 'ctx')
- hidden_grad: float32 [4, 2048, 2048], P(None, 'ctx')
- attend_lower_grad: float32 [3, 2048, 16], replicated
- attend_upper_grad: float32 [3, 16, 2048], P(None, None, 'tp')
- attend_magnitude_grad: float32 [3, 2048], P(None, 'tp')
- output_lower_grad: float32 [2048, 16], P('tp')
- output_upper_grad: float32 [16, 2048], replicated
- output_magnitude_grad: float32 [2048], replicated
- expand_lower_grad: float32 [2, 2048, 16], replicated
- expand_upper_grad: float32 [2, 16, 5632], P(None, None, 'tp')
- expand_magnitude_grad: float32 [2, 5632], P(None, 'tp')
- reduce_lower_grad: float32 [5632, 16], P('tp')
- reduce_upper_grad: float32 [16, 2048], replicated
- reduce_magnitude_grad: float32 [2048], replicated
Inputs may be any that keep to these rules, and one draw needn't show every extreme that they name: `segments`: ids never fall along a row; in every row one segment starts within the first 256 positions and ends within the last 256.
All inputs are finite; a program needn't handle non-finite values.
Results may differ from a plain program's by a relative error of at most 0.015.
The roundings to bfloat16 on the way count: a program that leaves them out, or rounds other values in their place, can miss the bound.
Values may be sent and summed in bfloat16 or wider, within the bound.
A program may use at most 256 MiB of HBM per device.

v0:
```python
import jax
import jax.numpy as jnp
from jax import lax
from jax.sharding import PartitionSpec as P

HD = 128
SEGS = 4


epsilon = 1e-05
adapter_scale = 2.0
rotary_base = 10000.0
top_precision = lax.Precision.HIGHEST


def merge_local(base_weights, down_factor, up_factor):
    return base_weights.astype(jnp.float32) + adapter_scale * jnp.dot(
        down_factor, up_factor, precision=top_precision
    )


def rotate(tensor, cosine, sine_part):
    half_width = tensor.shape[-1] // 2
    turned = jnp.concatenate([-tensor[..., half_width:], tensor[..., :half_width]], axis=-1)
    return tensor * cosine + turned * sine_part


def unrotate(grads_in, cosine, sine_part):
    half_width = grads_in.shape[-1] // 2
    weighted = grads_in * sine_part
    turned = jnp.concatenate([weighted[..., half_width:], -weighted[..., :half_width]], axis=-1)
    return grads_in * cosine + turned


def rms_back(tensor, inverse, scaling, grads_in):
    scaled = grads_in * scaling
    return inverse * scaled - tensor * inverse**3 * jnp.mean(
        tensor * scaled, axis=-1, keepdims=True
    )


def adapter_grads(dweight, combined_weight, magnitude, column, down_factor, up_factor, summed):
    combined_gradient = dweight * (magnitude / column) - combined_weight * (
        magnitude * summed / column**3
    )
    down_factor_gradient = adapter_scale * jnp.dot(
        combined_gradient, up_factor.T, precision=top_precision
    )
    up_factor_gradient = adapter_scale * jnp.dot(
        down_factor.T, combined_gradient, precision=top_precision
    )
    return (down_factor_gradient, up_factor_gradient, summed / column)


def on_device(
    hidden,
    segments,
    key_attendable,
    attention_gain,
    feedforward_gain,
    attend_frozen,
    output_frozen,
    expand_frozen,
    reduce_frozen,
    attend_lower,
    attend_upper,
    attend_magnitude,
    output_lower,
    output_upper,
    output_magnitude,
    expand_lower,
    expand_upper,
    expand_magnitude,
    reduce_lower,
    reduce_upper,
    reduce_magnitude,
    cotangent,
):
    batch_rows, tokens_here, model_width = hidden.shape
    length = segments.shape[1]
    local_width = attend_frozen.shape[2]
    heads_here = local_width // HD
    flat_count = batch_rows * tokens_here
    offset = lax.axis_index("ctx") * tokens_here
    score_scale = HD ** (-0.5)
    joined_attend = [
        merge_local(attend_frozen[member], attend_lower[member], attend_upper[member])
        for member in range(3)
    ]
    column_attend = [
        jnp.sqrt(jnp.sum(combined_weight * combined_weight, axis=0))
        for combined_weight in joined_attend
    ]
    weight_attend = [
        (joined_attend[member] * (attend_magnitude[member] / column_attend[member])).astype(
            jnp.bfloat16
        )
        for member in range(3)
    ]
    joined_expand = [
        merge_local(expand_frozen[member], expand_lower[member], expand_upper[member])
        for member in range(2)
    ]
    column_expand = [
        jnp.sqrt(jnp.sum(combined_weight * combined_weight, axis=0))
        for combined_weight in joined_expand
    ]
    weight_expand = [
        (joined_expand[member] * (expand_magnitude[member] / column_expand[member])).astype(
            jnp.bfloat16
        )
        for member in range(2)
    ]
    joined_out = merge_local(output_frozen, output_lower, output_upper)
    joined_reduce = merge_local(reduce_frozen, reduce_lower, reduce_upper)
    square_out, square_reduce = lax.psum(
        (jnp.sum(joined_out * joined_out, axis=0), jnp.sum(joined_reduce * joined_reduce, axis=0)),
        "tp",
    )
    column_out = jnp.sqrt(square_out)
    column_reduce = jnp.sqrt(square_reduce)
    weight_out = (joined_out * (output_magnitude / column_out)).astype(jnp.bfloat16)
    weight_reduce = (joined_reduce * (reduce_magnitude / column_reduce)).astype(jnp.bfloat16)
    levels = jnp.arange(SEGS, dtype=jnp.int32)
    below_count = jnp.sum(
        (segments[:, None, :] < levels[None, :, None]).astype(jnp.float32), axis=2
    )
    seg_begin = jnp.sum(
        (segments[:, :, None] == levels[None, None, :]).astype(jnp.float32)
        * below_count[:, None, :],
        axis=2,
    )
    places = jnp.arange(length).astype(jnp.float32)[None, :] - seg_begin
    places_here = lax.dynamic_slice_in_dim(places, offset, tokens_here, 1)
    frequency = rotary_base ** (-(2.0 * jnp.arange(HD // 2).astype(jnp.float32)) / HD)
    angles = places_here[:, :, None] * frequency[None, None, :]
    angles = jnp.concatenate([angles, angles], axis=-1)[:, :, None, :]
    cosine = jnp.cos(angles)
    sine_part = jnp.sin(angles)
    query_segment = lax.dynamic_slice_in_dim(segments, offset, tokens_here, 1)
    query_spot = offset + jnp.arange(tokens_here, dtype=jnp.int32)
    key_spot = jnp.arange(length, dtype=jnp.int32)
    diagonal = key_spot[None, None, :] == query_spot[None, :, None]
    allowed = (
        (query_segment[:, :, None] == segments[:, None, :])
        & (key_spot[None, None, :] <= query_spot[None, :, None])
        & ((key_attendable[:, None, :] == 1) | diagonal)
    )
    allowed = allowed[:, None]

    def split_heads(tensor):
        return tensor.reshape(batch_rows, tokens_here, heads_here, HD)

    gain_one = attention_gain.astype(jnp.float32)
    gain_two = feedforward_gain.astype(jnp.float32)
    inputs = hidden.astype(jnp.float32).reshape(flat_count, model_width)
    inverse_one = lax.rsqrt(jnp.mean(inputs * inputs, axis=-1, keepdims=True) + epsilon)
    normed_one = (inputs * inverse_one * gain_one).astype(jnp.bfloat16)
    queries = rotate(
        split_heads(jnp.dot(normed_one, weight_attend[0], preferred_element_type=jnp.float32)),
        cosine,
        sine_part,
    ).astype(jnp.bfloat16)
    keys_here = rotate(
        split_heads(jnp.dot(normed_one, weight_attend[1], preferred_element_type=jnp.float32)),
        cosine,
        sine_part,
    ).astype(jnp.bfloat16)
    values_here = split_heads(
        jnp.dot(normed_one, weight_attend[2], preferred_element_type=jnp.float32)
    ).astype(jnp.bfloat16)
    all_keys, all_values = (
        lax.all_gather(keys_here, "ctx", axis=1, tiled=True),
        lax.all_gather(values_here, "ctx", axis=1, tiled=True),
    )

    def scores_from(key_block):
        raw_scores = (
            jnp.einsum("rqhd,rkhd->rhqk", queries, key_block, preferred_element_type=jnp.float32)
            * score_scale
        )
        return jnp.where(allowed, raw_scores, -1e30)

    scores = scores_from(all_keys)
    row_peak = jnp.max(scores, axis=-1, keepdims=True)
    powers = jnp.exp(scores - row_peak)
    sum_total = jnp.sum(powers, axis=-1, keepdims=True)
    attention_probs = powers / sum_total
    log_total = row_peak + jnp.log(sum_total)
    probs_low = attention_probs.astype(jnp.bfloat16)
    mixed_heads = jnp.einsum(
        "rhqk,rkhd->rqhd", probs_low, all_values, preferred_element_type=jnp.float32
    )
    mixed_heads = mixed_heads.astype(jnp.bfloat16).reshape(flat_count, local_width)
    resid = inputs + lax.psum(
        jnp.dot(mixed_heads, weight_out, preferred_element_type=jnp.float32), "tp"
    )
    inverse_two = lax.rsqrt(jnp.mean(resid * resid, axis=-1, keepdims=True) + epsilon)
    normed_two = (resid * inverse_two * gain_two).astype(jnp.bfloat16)
    gate_proj = jnp.dot(normed_two, weight_expand[0], preferred_element_type=jnp.float32)
    up_proj = jnp.dot(normed_two, weight_expand[1], preferred_element_type=jnp.float32)
    sigmoid_gate = jax.nn.sigmoid(gate_proj)
    activated = (gate_proj * sigmoid_gate * up_proj).astype(jnp.bfloat16)
    feedforward = lax.psum(
        jnp.dot(activated, weight_reduce, preferred_element_type=jnp.float32), "tp"
    )
    block_output = (
        (resid + feedforward).astype(jnp.bfloat16).reshape(batch_rows, tokens_here, model_width)
    )
    grad_low = cotangent.reshape(flat_count, model_width)
    grad_full = grad_low.astype(jnp.float32)
    dweight_reduce = jnp.dot(activated.T, grad_low, preferred_element_type=jnp.float32)
    d_act = jnp.dot(grad_low, weight_reduce.T, preferred_element_type=jnp.float32)
    d_gate = (d_act * up_proj * sigmoid_gate * (1.0 + gate_proj * (1.0 - sigmoid_gate))).astype(
        jnp.bfloat16
    )
    d_up = (d_act * gate_proj * sigmoid_gate).astype(jnp.bfloat16)
    dweight_gate = jnp.dot(normed_two.T, d_gate, preferred_element_type=jnp.float32)
    dweight_up = jnp.dot(normed_two.T, d_up, preferred_element_type=jnp.float32)
    d_two_part = jnp.dot(d_gate, weight_expand[0].T, preferred_element_type=jnp.float32) + jnp.dot(
        d_up, weight_expand[1].T, preferred_element_type=jnp.float32
    )
    d_two = lax.psum(d_two_part, "tp")
    d_resid = grad_full + rms_back(resid, inverse_two, gain_two, d_two)
    d_resid_low = d_resid.astype(jnp.bfloat16)
    dweight_out = jnp.dot(mixed_heads.T, d_resid_low, preferred_element_type=jnp.float32)
    d_mixed = split_heads(
        jnp.dot(d_resid_low, weight_out.T, preferred_element_type=jnp.float32).astype(jnp.bfloat16)
    )
    keys_back, values_back = (
        lax.all_gather(keys_here, "ctx", axis=1, tiled=True),
        lax.all_gather(values_here, "ctx", axis=1, tiled=True),
    )
    probs_back = jnp.exp(scores_from(keys_back) - log_total)
    probs_back_low = probs_back.astype(jnp.bfloat16)
    d_probs = jnp.einsum(
        "rqhd,rkhd->rhqk", d_mixed, values_back, preferred_element_type=jnp.float32
    )
    row_delta = jnp.sum(d_probs * probs_back, axis=-1, keepdims=True)
    d_scores = (probs_back * (d_probs - row_delta)).astype(jnp.bfloat16)
    d_queries = (
        jnp.einsum("rhqk,rkhd->rqhd", d_scores, keys_back, preferred_element_type=jnp.float32)
        * score_scale
    )
    d_keys_all = (
        jnp.einsum("rhqk,rqhd->rkhd", d_scores, queries, preferred_element_type=jnp.float32)
        * score_scale
    )
    d_values_all = jnp.einsum(
        "rhqk,rqhd->rkhd", probs_back_low, d_mixed, preferred_element_type=jnp.float32
    )
    d_keys, d_values = (
        lax.psum_scatter(d_keys_all, "ctx", scatter_dimension=1, tiled=True),
        lax.psum_scatter(d_values_all, "ctx", scatter_dimension=1, tiled=True),
    )
    query_low = (
        unrotate(d_queries, cosine, sine_part).astype(jnp.bfloat16).reshape(flat_count, local_width)
    )
    key_low = (
        unrotate(d_keys, cosine, sine_part).astype(jnp.bfloat16).reshape(flat_count, local_width)
    )
    value_low = d_values.astype(jnp.bfloat16).reshape(flat_count, local_width)
    grads_low = [query_low, key_low, value_low]
    dweight_attend = [
        jnp.dot(normed_one.T, grads_low[member], preferred_element_type=jnp.float32)
        for member in range(3)
    ]
    d_one_part = jnp.dot(query_low, weight_attend[0].T, preferred_element_type=jnp.float32)
    d_one_part = d_one_part + jnp.dot(
        key_low, weight_attend[1].T, preferred_element_type=jnp.float32
    )
    d_one_part = d_one_part + jnp.dot(
        value_low, weight_attend[2].T, preferred_element_type=jnp.float32
    )
    d_one = lax.psum(d_one_part, "tp")
    hidden_grad = (d_resid + rms_back(inputs, inverse_one, gain_one, d_one)).reshape(
        batch_rows, tokens_here, model_width
    )
    attend_parts = [
        adapter_grads(
            dweight_attend[member],
            joined_attend[member],
            attend_magnitude[member],
            column_attend[member],
            attend_lower[member],
            attend_upper[member],
            jnp.sum(dweight_attend[member] * joined_attend[member], axis=0),
        )
        for member in range(3)
    ]
    dweight_expand = [dweight_gate, dweight_up]
    expand_parts = [
        adapter_grads(
            dweight_expand[member],
            joined_expand[member],
            expand_magnitude[member],
            column_expand[member],
            expand_lower[member],
            expand_upper[member],
            jnp.sum(dweight_expand[member] * joined_expand[member], axis=0),
        )
        for member in range(2)
    ]
    summed_out, summed_reduce = lax.psum(
        (
            jnp.sum(dweight_out * joined_out, axis=0),
            jnp.sum(dweight_reduce * joined_reduce, axis=0),
        ),
        "tp",
    )
    out_lower_grad, out_upper_grad, out_magnitude_grad = adapter_grads(
        dweight_out,
        joined_out,
        output_magnitude,
        column_out,
        output_lower,
        output_upper,
        summed_out,
    )
    red_lower_grad, red_upper_grad, red_magnitude_grad = adapter_grads(
        dweight_reduce,
        joined_reduce,
        reduce_magnitude,
        column_reduce,
        reduce_lower,
        reduce_upper,
        summed_reduce,
    )
    attend_upper_part = jnp.stack([piece[1] for piece in attend_parts])
    attend_magnitude_part = jnp.stack([piece[2] for piece in attend_parts])
    attend_lower_part = jnp.stack([piece[0] for piece in attend_parts])
    expand_upper_part = jnp.stack([piece[1] for piece in expand_parts])
    expand_magnitude_part = jnp.stack([piece[2] for piece in expand_parts])
    expand_lower_part = jnp.stack([piece[0] for piece in expand_parts])
    (
        attend_upper_grad,
        attend_magnitude_grad,
        output_lower_grad,
        output_magnitude_grad,
        expand_upper_grad,
        expand_magnitude_grad,
        reduce_lower_grad,
        reduce_magnitude_grad,
    ) = lax.psum(
        (
            attend_upper_part,
            attend_magnitude_part,
            out_lower_grad,
            out_magnitude_grad,
            expand_upper_part,
            expand_magnitude_part,
            red_lower_grad,
            red_magnitude_grad,
        ),
        "ctx",
    )
    attend_lower_grad, output_upper_grad, expand_lower_grad, reduce_upper_grad = lax.psum(
        (attend_lower_part, out_upper_grad, expand_lower_part, red_upper_grad), ("ctx", "tp")
    )
    return (
        block_output,
        hidden_grad,
        attend_lower_grad,
        attend_upper_grad,
        attend_magnitude_grad,
        output_lower_grad,
        output_upper_grad,
        output_magnitude_grad,
        expand_lower_grad,
        expand_upper_grad,
        expand_magnitude_grad,
        reduce_lower_grad,
        reduce_upper_grad,
        reduce_magnitude_grad,
    )


def solution(mesh):
    placed = (
        P(None, "ctx", None),
        P(),
        P(),
        P(),
        P(),
        P(None, None, "tp"),
        P("tp", None),
        P(None, None, "tp"),
        P("tp", None),
        P(),
        P(None, None, "tp"),
        P(None, "tp"),
        P("tp", None),
        P(),
        P(),
        P(),
        P(None, None, "tp"),
        P(None, "tp"),
        P("tp", None),
        P(),
        P(),
        P(None, "ctx", None),
    )
    return jax.shard_map(
        on_device,
        mesh=mesh,
        in_specs=placed,
        out_specs=(
            P(None, "ctx", None),
            P(None, "ctx", None),
            P(),
            P(None, None, "tp"),
            P(None, "tp"),
            P("tp", None),
            P(),
            P(),
            P(),
            P(None, None, "tp"),
            P(None, "tp"),
            P("tp", None),
            P(),
            P(),
        ),
        check_vma=False,
    )
```

profile of v0, /device:TPU:0, one launch (start us, length us, event | category | flops | bytes accessed | tf_op | source)
XLA Modules:
  0.0 1040.4 jit_solution(10751264294596890120)
XLA Ops:
  27.4 4.1 fusion.60
  40.4 41.3 %psum.140 = f32[2048]{0:T(1024)S(1)} all-reduce(f32[2048]{0:T(1024)S(1)} %get-tuple-element.87), channel_id=1, replica_groups=mesh['ctx'=8,'tp'=16] {'tp'}, use_global_device_ids=true, to_apply=%region_9.0 | all-reduce | flops 2048 | bytes 16384 | tf_op jit(solution)/shard_map/psum | solution.py:116
  88.8 4.6 fusion.137
  98.7 5.9 fusion.49
  104.8 4.5 fusion.72
  111.2 5.3 multiply_reduce_fusion.7
  116.5 4.3 multiply_reduce_fusion.8
  124.7 123.4 %all-reduce.10.cloned.1.call-done = f32[1024,2048]{1,0:T(8,128)} async-done(((f32[1024,2048]{1,0:T(8,128)}), f32[1024,2048]{1,0:T(8,128)}) %all-reduce.10.cloned.1.call-update) | async-done | bytes 8388624 | tf_op jit(solution)/shard_map/psum | solution.py:195
  248.1 5.9 multiply_reduce_fusion.2
  264.9 3.9 multiply_reduce_fusion.3
  268.9 38.8 %psum.142 = f32[2048]{0:T(1024)S(1)} all-reduce(f32[2048]{0:T(1024)S(1)} %get-tuple-element.15), channel_id=1, replica_groups=mesh['ctx'=8,'tp'=16] {'tp'}, use_global_device_ids=true, to_apply=%region_15.16 | all-reduce | flops 2048 | bytes 16384 | tf_op jit(solution)/shard_map/psum | solution.py:116
  307.7 5.3 multiply_convert_fusion.5
  315.5 6.0 convolution_add_fusion
  322.2 137.1 %all-reduce.12.cloned.1.call-done = f32[1024,2048]{1,0:T(8,128)} async-done(((f32[1024,2048]{1,0:T(8,128)}), f32[1024,2048]{1,0:T(8,128)}) %all-reduce.12.cloned.1.call-update) | async-done | bytes 8388624 | tf_op jit(solution)/shard_map/psum | solution.py:223
  459.3 8.6 multiply_reduce_fusion.1
  468.0 8.7 subtract_add_fusion
  480.0 3.6 fusion.15
  485.2 4.4 multiply_reduce_fusion
  489.7 4.9 multiply_convert_fusion
  496.6 3.7 multiply_bitcast_fusion
  502.2 6.9 fusion.55
  509.1 11.9 %reduce-scatter.5.cloned.1.call-done = f32[4,256,1,128]{1,3,0,2:T(8,128)} async-done(((f32[4,2048,1,128]{1,3,0,2:T(8,128)}), f32[4,256,1,128]{1,3,0,2:T(8,128)}) %reduce-scatter.5.cloned.1.call-update) | async-done | bytes 524304 | tf_op jit(solution)/shard_map/reduce_scatter | solution.py:254
  524.6 36.3 %reduce-scatter.3.cloned.1.call-done = f32[4,256,1,128]{3,1,0,2:T(8,128)} async-done(((f32[4,2048,1,128]{3,1,0,2:T(8,128)}), f32[4,256,1,128]{3,1,0,2:T(8,128)}) %reduce-scatter.3.cloned.1.call-update) | async-done | bytes 524304 | tf_op jit(solution)/shard_map/reduce_scatter | solution.py:253
  560.9 5.6 fusion.66
  572.4 4.6 add_add_fusion
  577.7 5.2 multiply_reduce_fusion.4
  598.5 77.1 %all-reduce.1 = (f32[2048]{0:T(1024)S(1)}, f32[2048]{0:T(1024)S(1)}) all-reduce(f32[2048]{0:T(1024)S(1)} %get-tuple-element.105, f32[2048]{0:T(1024)S(1)} %copy-done.87), channel_id=1, replica_groups=mesh['ctx'=8,'tp'=16] {'tp'}, use_global_device_ids=true, to_apply=%region_31.32 | all-reduce | flops 4096 | bytes 32768 | tf_op jit(solution)/shard_map/psum | solution.py:304
  701.1 97.0 %all-reduce.16.cloned.1.call-done = (f32[1024,2048]{1,0:T(8,128)}, f32[1024,2048]{1,0:T(8,128)}) async-done(((f32[1024,2048]{1,0:T(8,128)}, f32[1024,2048]{1,0:T(8,128)}), (f32[1024,2048]{1,0:T(8,128)}, f32[1024,2048]{1,0:T(8,128)})) %all-reduce.16.cloned.1.call-update) | async-done | bytes 16777232 | tf_op jit(solution)/shard_map/psum | solution.py:204
  798.2 6.0 fusion.8
  804.2 17.2 %fusion.7 = (f32[1024,2048]{1,0:T(8,128)}, bf16[1024,2048]{1,0:T(8,128)(2,1)}) fusion(f32[1024,2048]{1,0:T(8,128)} %copy-done.9, bf16[4,256,2048]{2,1,0:T(8,128)(2,1)S(1)} %copy-done.4, f32[1024,2048]{1,0:T(8,128)} %get-tuple-element.27, f32[1024]{0:T(1024)S(1)} %broadcast_multiply_fusion.1, f32[1024]{0:T(1024)S(1)} %multiply_multiply_fusion.2, ...), kind=kLoop, calls=%fused_computation.13 | loop fusion | flops 20971520 | bytes 50352128 | tf_op jit(solution)/shard_map/add | solution.py:276
  821.4 40.7 %all-reduce.18.cloned.1.call-done = (f32[3,16,128]{2,1,0:T(8,128)}, f32[3,128]{1,0:T(4,128)}, f32[128,16]{0,1:T(8,128)}, f32[2048]{0:T(1024)}, f32[2,16,352]{2,1...) async-done(((f32[3,16,128]{2,1,0:T(8,128)}, f32[3,128]{1,0:T(4,128)}, f32[128,16]{0,1:T(8,128)}, f32[2048]{0:T(1024)}, f32[2,16,352]{2,1,0:T(8,128)}, ...) | async-done | bytes 121104 | tf_op jit(solution)/shard_map/psum | solution.py:344
  862.2 154.2 %all-reduce.14.cloned.1.call-done = (f32[3,2048,16]{1,2,0:T(8,128)}, f32[16,2048]{1,0:T(8,128)}, f32[2,2048,16]{1,2,0:T(8,128)}, f32[16,2048]{1,0:T(8,128)}) async-done(((f32[3,2048,16]{1,2,0:T(8,128)}, f32[16,2048]{1,0:T(8,128)}, f32[2,2048,16]{1,2,0:T(8,128)}, f32[16,2048]{1,0:T(8,128)}), (f32[3,2048,16]{1,2,0:T(8,128)}, f32[16,2048]{1,0:T(8,128)}, f32[2,2048,16]{1,2,0:T(8,128)}, ...) | async-done | bytes 917520 | tf_op jit(solution)/shard_map/psum | solution.py:357
  (358 shorter events, 137.3 us)
Async XLA Ops:
  7.2 114.9 %copy-start = (f32[16,2048]{1,0:T(8,128)S(1)}, f32[16,2048]{1,0:T(8,128)}, u32[]{:S(2)}) copy-start(f32[16,2048]{1,0:T(8,128)} %param.41) | copy-start | bytes 393220
  7.2 81.5 %all-gather.4.cloned.1.call-start = ((), (), s32[]{:S(2)}) async-start(), calls=%async_computation.2 | async-start | bytes 2359296 | tf_op jit(solution)/shard_map/all_gather | solution.py:173
  10.2 24.9 %copy-start.20 = (f32[2048,128]{1,0:T(8,128)}, f32[2048,128]{1,0:T(8,128)S(1)}, u32[]{:S(2)}) copy-start(f32[2048,128]{1,0:T(8,128)S(1)} %get-tuple-element.82) | copy-start | bytes 3145732
  17.0 64.8 %copy-start.26 = (f32[2048,128]{1,0:T(8,128)}, f32[2048,128]{1,0:T(8,128)S(1)}, u32[]{:S(2)}) copy-start(f32[2048,128]{1,0:T(8,128)S(1)} %get-tuple-element.84) | copy-start | bytes 3145732
  22.0 13.2 %copy-start.99 = (f32[128]{0:T(128)}, f32[128]{0:T(128)S(1)}, u32[]{:S(2)}) copy-start(f32[128]{0:T(128)S(1)} %get-tuple-element.72) | copy-start | bytes 1540
  22.0 59.8 %copy-start.101 = (f32[128]{0:T(128)}, f32[128]{0:T(128)S(1)}, u32[]{:S(2)}) copy-start(f32[128]{0:T(128)S(1)} %get-tuple-element.73) | copy-start | bytes 1540
  31.6 66.5 %all-gather.6.cloned.1.call-start = ((), (), s32[]{:S(2)}) async-start(), calls=%async_computation.7 | async-start | bytes 2359296 | tf_op jit(solution)/shard_map/all_gather | solution.py:174
  37.2 44.6 %copy-start.82 = (f32[2048]{0:T(1024)S(1)}, f32[2048]{0:T(1024)}, u32[]{:S(2)}) copy-start(f32[2048]{0:T(1024)} %param.36) | copy-start | bytes 24580
  39.2 208.9 %all-reduce.10.cloned.1.call-start = ((), (), s32[]{:S(2)}) async-start(), calls=%async_computation.3 | async-start | bytes 16777216 | tf_op jit(solution)/shard_map/psum | solution.py:195
  40.4 64.4 %copy-start.29 = (f32[128,2048]{1,0:T(8,128)}, f32[128,2048]{1,0:T(8,128)S(1)}, u32[]{:S(2)}) copy-start(f32[128,2048]{1,0:T(8,128)S(1)} %get-tuple-element.88) | copy-start | bytes 3145732
  109.4 349.9 %all-reduce.12.cloned.1.call-start = ((), (), s32[]{:S(2)}) async-start(), calls=%async_computation.4 | async-start | bytes 16777216 | tf_op jit(solution)/shard_map/psum | solution.py:223
  111.2 142.7 %copy-start.65 = (f32[2048]{0:T(1024)}, f32[2048]{0:T(1024)S(1)}, u32[]{:S(2)}) copy-start(f32[2048]{0:T(1024)S(1)} %convert_element_type.199) | copy-start | bytes 24580
  122.1 190.9 %copy-start.78 = (f32[352]{0:T(512)}, f32[352]{0:T(512)S(1)}, u32[]{:S(2)}) copy-start(f32[352]{0:T(512)S(1)} %get-tuple-element.18) | copy-start | bytes 4228
  122.1 193.4 %copy-start.76 = (f32[352]{0:T(512)}, f32[352]{0:T(512)S(1)}, u32[]{:S(2)}) copy-start(f32[352]{0:T(512)S(1)} %get-tuple-element.19) | copy-start | bytes 4228
  124.7 183.0 %copy-start.10 = (f32[352,2048]{1,0:T(8,128)}, f32[352,2048]{1,0:T(8,128)S(1)}, u32[]{:S(2)}) copy-start(f32[352,2048]{1,0:T(8,128)S(1)} %fusion.18) | copy-start | bytes 8650756
  264.9 42.7 %copy-start.84 = (f32[2048]{0:T(1024)S(1)}, f32[2048]{0:T(1024)}, u32[]{:S(2)}) copy-start(f32[2048]{0:T(1024)} %param.42) | copy-start | bytes 24580
  321.5 137.8 %copy-start.66 = (f32[2048]{0:T(1024)S(1)}, f32[2048]{0:T(1024)}, u32[]{:S(2)}) copy-start(f32[2048]{0:T(1024)} %copy-done.65) | copy-start | bytes 24580
  321.5 199.5 %reduce-scatter.5.cloned.1.call-start = ((), (), s32[]{:S(2)}) async-start(), calls=%async_computation.6 | async-start | bytes 4718592 | tf_op jit(solution)/shard_map/reduce_scatter | solution.py:254
  468.0 12.0 %slice-start = ((s8[8388608]{0:T(1024)(128)(4,1)}), s8[4194304]{0:T(1024)(128)(4,1)S(1)}, s32[]{:S(2)}) async-start(s8[8388608]{0:T(1024)(128)(4,1)} %bitcast.307), calls=%async_computation.11 | async-start | bytes 8388608
  468.0 12.0 %slice-start.1 = ((s8[8388608]{0:T(1024)(128)(4,1)}), s8[4194304]{0:T(1024)(128)(4,1)S(1)}, s32[]{:S(2)}) async-start(s8[8388608]{0:T(1024)(128)(4,1)} %bitcast.307), calls=%async_computation.12 | async-start | bytes 8388608
  483.7 77.2 %reduce-scatter.3.cloned.1.call-start = ((), (), s32[]{:S(2)}) async-start(), calls=%async_computation.5 | async-start | bytes 4718592 | tf_op jit(solution)/shard_map/reduce_scatter | solution.py:253
  500.3 60.5 %copy-start.35 = (f32[4,256,1,64]{3,1,0,2:T(8,128)S(1)}, f32[4,256,1,64]{3,1,0,2:T(8,128)}, u32[]{:S(2)}) copy-start(f32[4,256,1,64]{3,1,0,2:T(8,128)} %copy-done.34) | copy-start | bytes 786436
  500.3 297.9 %all-reduce.16.cloned.1.call-start = ((), (), s32[]{:S(2)}) async-start(), calls=%async_computation.9 | async-start | bytes 33554432 | tf_op jit(solution)/shard_map/psum | solution.py:204
  577.0 285.2 %all-reduce.18.cloned.1.call-start = ((), (), s32[]{:S(2)}) async-start(), calls=%async_computation.10 | async-start | bytes 256000 | tf_op jit(solution)/shard_map/psum | solution.py:344
  596.7 78.9 %copy-start.71 = (f32[2048]{0:T(1024)S(1)}, f32[2048]{0:T(1024)}, u32[]{:S(2)}) copy-start(f32[2048]{0:T(1024)} %copy-done.70) | copy-start | bytes 24580
  596.7 78.9 %copy-start.83 = (f32[2048]{0:T(1024)S(1)}, f32[2048]{0:T(1024)}, u32[]{:S(2)}) copy-start(f32[2048]{0:T(1024)} %param.36) | copy-start | bytes 24580
  596.7 79.5 %copy-start.73 = (f32[2048]{0:T(1024)S(1)}, f32[2048]{0:T(1024)}, u32[]{:S(2)}) copy-start(f32[2048]{0:T(1024)} %copy-done.72) | copy-start | bytes 24580
  596.7 79.5 %copy-start.85 = (f32[2048]{0:T(1024)S(1)}, f32[2048]{0:T(1024)}, u32[]{:S(2)}) copy-start(f32[2048]{0:T(1024)} %param.42) | copy-start | bytes 24580
  596.7 80.1 %copy-start.58 = (f32[16,2048]{1,0:T(8,128)S(1)}, f32[16,2048]{1,0:T(8,128)}, u32[]{:S(2)}) copy-start(f32[16,2048]{1,0:T(8,128)} %param.35) | copy-start | bytes 393220
  596.7 83.3 %copy-start.81 = (f32[128,16]{0,1:T(8,128)S(1)}, f32[128,16]{0,1:T(8,128)}, u32[]{:S(2)}) copy-start(f32[128,16]{0,1:T(8,128)} %param.34) | copy-start | bytes 24580
  696.7 101.5 %copy-start.60 = (f32[2048]{0:T(1024)S(1)}, f32[2048]{0:T(1024)}, u32[]{:S(2)}) copy-start(f32[2048]{0:T(1024)} %copy-done.59) | copy-start | bytes 24580
  700.3 316.1 %all-reduce.14.cloned.1.call-start = ((), (), s32[]{:S(2)}) async-start(), calls=%async_computation.8 | async-start | bytes 1835008 | tf_op jit(solution)/shard_map/psum | solution.py:357
  (98 other events, 366.3 us)
Sparse Core Ops, SparseCore 0:
  31.7 27.8 all-gather.3
  61.9 25.7 all-gather.5
  109.5 138.4 all-reduce.9
  321.6 137.6 all-reduce.11
  483.8 37.1 reduce-scatter.4
  523.8 36.9 reduce-scatter.2
  577.1 221.0 all-reduce.15
  802.3 59.8 all-reduce.17
  869.6 146.7 all-reduce.13
where the time goes:
time: 1050 us; the launch traced here: 1040 us
  waiting for transfers between devices  601 us (57%)
  blocking collectives  157 us (15%)
  matrix products  142 us (14%)
  other arithmetic  81.8 us (8%)
  local copies, waits for them, and re-layouts  40.9 us (4%)
  between operations  15.9 us (2%)
    psum x1, waiting for transfers between devices, on_device(): lax.psum((attend_lower_part, out_upper_grad, expand_lower_part, red_upper...  154 us
    psum x1, waiting for transfers between devices, on_device(): d_two = lax.psum(d_two_part, 'tp')  137 us
    psum x1, waiting for transfers between devices, on_device(): lax.psum(jnp.dot(mixed_heads, weight_out, preferred_element_type=jnp.floa...  123 us
    psum x1, waiting for transfers between devices, on_device(): lax.psum(jnp.dot(activated, weight_reduce, preferred_element_type=jnp.flo...  97 us
    psum x2, blocking collectives, on_device(): lax.psum((jnp.sum(joined_out * joined_out, axis=0), jnp.sum(joined_reduce...  80.1 us
    psum x1, blocking collectives, on_device(): lax.psum((jnp.sum(dweight_out * joined_out, axis=0), jnp.sum(dweight_redu...  77.1 us
    psum x1, waiting for transfers between devices, on_device(): lax.psum((attend_upper_part, attend_magnitude_part, out_lower_grad, out_m...  40.7 us
    unnamed x255, local copies, waits for them, and re-layouts  38.3 us
  transfers between devices with their start and end apart: 9, of which 7 were waited for; matrix products, arithmetic and copies ran while one was open for 12% of the time, Pallas kernels for 0%

commit v1 on v0

v1 whole, which is shorter than its diff:
```python
import jax
import jax.numpy as jnp
from jax import lax
from jax.experimental import pallas as pl
from jax.experimental.pallas import tpu as pltpu
from jax.sharding import PartitionSpec as P

HD = 128
SEGS = 4
X = 4
Y = 4
Z = 4

epsilon = 1e-05
adapter_scale = 2.0
rotary_base = 10000.0
F32 = jnp.float32
BF16 = jnp.bfloat16


def roll_blocks(a, axis, start):
    n = a.shape[axis]
    return lax.dynamic_slice_in_dim(jnp.concatenate([a, a], axis=axis), start, n, axis)


def halves(a):
    high = lax.reduce_precision(a, 8, 7)
    return high.astype(BF16), (a - high).astype(BF16)


def dot32(a, b, dims):
    return lax.dot_general(a, b, (dims, ((), ())), preferred_element_type=F32)


def exact_dot(bf, full, dims):
    high, low = halves(full)
    return dot32(bf, high, dims) + dot32(bf, low, dims)


def exact_dot_left(full, bf, dims):
    high, low = halves(full)
    return dot32(high, bf, dims) + dot32(low, bf, dims)


def rotate(tensor, cosine, sine_part):
    half_width = tensor.shape[-1] // 2
    turned = jnp.concatenate([-tensor[..., half_width:], tensor[..., :half_width]], axis=-1)
    return tensor * cosine + turned * sine_part


MESH = pl.DeviceIdType.MESH
ANY = pl.BlockSpec(memory_space=pl.ANY)
VM = pl.BlockSpec(memory_space=pltpu.VMEM)
NEAR_LAST = (2, 1, 3)


def place():
    ctx = lax.axis_index("ctx")
    tp = lax.axis_index("tp")
    return ctx // 2, ctx % 2, tp // X, tp % X


def device(dz=0, dc=0, dy=0, dx=0):
    z, core, y, x = place()
    return (((z + dz) % Z) * 2 + (core + dc) % 2, ((y + dy) % Y) * X + (x + dx) % X)


def greet(devices):
    barrier = pltpu.get_barrier_semaphore()
    for d in devices:
        pl.semaphore_signal(barrier, inc=1, device_id=d, device_id_type=MESH)
    pl.semaphore_wait(barrier, len(devices))


def send(src, dst, send_sem, recv_sem, to):
    copy = pltpu.make_async_remote_copy(
        src_ref=src,
        dst_ref=dst,
        send_sem=send_sem,
        recv_sem=recv_sem,
        device_id=to,
        device_id_type=MESH,
    )
    copy.start()
    return copy


def keep(src, dst, sem):
    copy = pltpu.make_async_copy(src, dst, sem)
    copy.start()
    return copy


def dma(*shape):
    return pltpu.SemaphoreType.DMA(shape)


def call(kernel, outs, in_specs, out_specs, scratch, number, flops, moved):
    return pl.pallas_call(
        kernel,
        out_shape=outs,
        in_specs=in_specs,
        out_specs=out_specs,
        scratch_shapes=scratch,
        cost_estimate=pl.CostEstimate(flops=flops, bytes_accessed=moved, transcendentals=0),
        compiler_params=pltpu.CompilerParams(
            collective_id=number, has_side_effects=True, vmem_limit_bytes=58 * 2**20
        ),
    )


def mask_of(begin, spot_q, key_tag, key_spot):
    return ((key_tag >= begin) & (key_tag <= spot_q)) | (key_spot == spot_q)


KB = 512


def tiles(total, size):
    return [(s, min(size, total - s)) for s in range(0, total, size)]


PIECES = 3


def relay_plan(weights, send_a, recv_a, send_b, recv_b, send_s, recv_s, cols):
    def begin(p, own, start, size):
        return [
            send(own, weights(1, start, size), send_a.at[p, 0], recv_a.at[p, 0], device(dx=1)),
            send(own, weights(3, start, size), send_a.at[p, 1], recv_a.at[p, 1], device(dx=3)),
        ]

    def relay(p, copies, start, size):
        half = size // 2
        more = []
        for k, (slot, at, to) in enumerate(((1, start, 1), (3, start + half, 3))):
            copies[k].wait_recv()
            more.append(
                send(
                    weights(slot, at, half), weights(2, at, half),
                    send_b.at[p, k], recv_b.at[p, k], device(dx=to),
                )
            )
            there = weights(slot, start, size)
            more.append(send(there, there, send_s.at[p, k], recv_s.at[p, k], device(dc=1)))
        return more

    def relay_far(p, more, start, size):
        more[0].wait_recv()
        more[2].wait_recv()
        there = weights(2, start, size)
        return send(there, there, send_s.at[p, 2], recv_s.at[p, 2], device(dc=1))

    def finish(copies, more, last):
        more[1].wait_recv()
        more[3].wait_recv()
        last.wait_recv()
        for copy in copies + more + [last]:
            copy.wait_send()

    return begin, relay, relay_far, finish


def front_kernel(
    hid_ref, gain_ref, fa_ref, la_ref, ua_ref, maga_ref, thin_ref, fw_ref, aw_ref, bw_ref,
    mage_ref, mago_ref, el_ref, small_ref, cos_ref, sin_ref, begin_ref, tag_ref,
    mixed_out, soft_out, log_out, kv_out, weights_out, wq_out, q_out, pre_out, thr_out,
    cola_out, cole_out, sq_out, ina_out, ine_out, ino_out, n1_out, small_out,
    kv_all, score, soft, logs, mixed, mixed_x, joined, w_own, wq_all, normed, kv_own, small,
    sq_x, sq_y, sq_one, ja,
    kv_send, kv_recv, sib_send, sib_recv, a_send, a_recv, b_send, b_recv, ws_send, ws_recv,
    m_send, m_recv, sq_send, sq_recv, sm_send, sm_recv, local, n_local,
):
    z, core, y, x = place()
    me = z * 2 + core
    rows, here, width = hid_ref.shape
    length = Z * 2 * here
    count = fw_ref.shape[0]
    ff = (count - HD) // 3
    piece = here // Y
    cols = pl.ds(pl.multiple_of(core * (width // 2), width // 2), width // 2)
    greet(
        [device(dx=d) for d in (1, 2, 3)]
        + [device(dy=d) for d in (1, 2, 3)]
        + [device(dz=d) for d in (1, 2, 3)]
        + [device(dc=1)]
    )

    def join(matrix, start, size, at):
        low = dot32(aw_ref[start : start + size], bw_ref[matrix, :, at], ((1,), (0,)))
        return fw_ref[start : start + size, at].astype(F32) + adapter_scale * low

    for s, size in tiles(width, 512):
        at = slice(s, s + size)
        one = join(0, 0, HD, at)
        two = join(3, HD + 2 * ff, ff, at)
        sq_one[0:1, at] = jnp.sum(one * one, axis=0, keepdims=True)
        sq_one[1:2, at] = jnp.sum(two * two, axis=0, keepdims=True)
    sq_copies = [
        send(sq_one, sq_x.at[d - 1], sq_send.at[0, d - 1], sq_recv.at[0, d - 1], device(dx=d))
        for d in NEAR_LAST
    ]

    def there(slot, start, size):
        return weights_out.at[slot, pl.ds(start, size), cols]

    begin, relay, relay_far, finish = relay_plan(
        there, a_send, a_recv, b_send, b_recv, ws_send, ws_recv, cols
    )
    where = ((HD, ff), (HD + ff, ff), (0, HD))
    sent, more, last = {}, {}, {}
    for m in range(2):
        start = HD + m * ff
        total = jnp.zeros((ff, 1), F32)
        for s, size in tiles(width, 512):
            at = slice(s, s + size)
            value = join(1 + m, start, ff, at)
            joined[:, at] = value
            total = total + jnp.sum(value * value, axis=1, keepdims=True)
        column = jnp.sqrt(total)
        cole_out[m * ff : (m + 1) * ff] = column
        magnitude = mage_ref[m * ff : (m + 1) * ff]
        ratio = magnitude / column
        for s, size in tiles(width, 512):
            at = slice(s, s + size)
            w_own[start : start + ff, at] = (joined[:, at] * ratio).astype(BF16)
        sent[m] = begin(m, w_own.at[pl.ds(start, ff), cols], start, ff)
        inner = dot32(w_own[start : start + ff], el_ref[...], ((1,), (0,)))
        ine_out[m * ff : (m + 1) * ff] = inner / ratio
        source = small_ref[0:ff, m * 16 : (m + 1) * 16]
        small[0:ff, m * 16 : (m + 1) * 16] = (source * ratio).astype(BF16)
        small[0:ff, (3 + m) * 16 : (4 + m) * 16] = (source / (magnitude * column)).astype(BF16)
    small[0:ff, 32:48] = small_ref[0:ff, 32:48].astype(BF16)
    small[0:ff, 80:] = jnp.zeros((ff, HD - 80), BF16)
    small[ff:] = small_ref[ff:].astype(BF16)
    sm_copies = [
        send(small, small_out.at[d], sm_send.at[d - 1], sm_recv.at[d - 1], device(dx=d))
        for d in NEAR_LAST
    ]
    own = [keep(small, small_out.at[0], local.at[0])]
    for copy in sq_copies:
        copy.wait()
    sq_one[...] += sq_x[0] + sq_x[1] + sq_x[2]
    sq_copies = [
        send(sq_one, sq_y.at[d - 1], sq_send.at[1, d - 1], sq_recv.at[1, d - 1], device(dy=d))
        for d in NEAR_LAST
    ]
    for m in range(3):
        total = jnp.zeros((1, HD), F32)
        for s, size in tiles(width, 512):
            at = slice(s, s + size)
            value = fa_ref[m, at].astype(F32) + adapter_scale * dot32(
                la_ref[m, at], ua_ref[m], ((1,), (0,))
            )
            ja[at] = value
            total = total + jnp.sum(value * value, axis=0, keepdims=True)
        column = jnp.sqrt(total)
        cola_out[m : m + 1] = column
        ratio = maga_ref[m : m + 1] / column
        wq_all[:, m * HD : (m + 1) * HD] = (ja[...] * ratio).astype(BF16)
        inner = dot32(la_ref[m], ja[...].astype(BF16), ((0,), (0,)))
        ina_out[m] = inner[0:16] + inner[32:48]
    own.append(keep(wq_all, wq_out, local.at[1]))
    kv_copies, sib_copies, n_copies = [], [], []
    gain = gain_ref[...]
    for r in range(rows):
        inputs = hid_ref[r].astype(F32)
        inverse = lax.rsqrt(jnp.mean(inputs * inputs, axis=1, keepdims=True) + epsilon)
        if r >= 2:
            n_copies[r - 2].wait()
        normed[r % 2] = (inputs * inverse * gain).astype(BF16)
        n_copies.append(keep(normed.at[r % 2], n1_out.at[r], n_local.at[r]))
        pre = dot32(normed[r % 2], wq_all[...], ((1,), (0,)))
        pre_out[r] = pre
        thin = dot32(normed[r % 2], thin_ref[...], ((1,), (0,)))
        thr_out[r] = thin
        cosine, sine = cos_ref[r], sin_ref[r]
        q_out[r] = rotate(pre[:, :HD], cosine, sine).astype(BF16)
        kv_own[r, :, :HD] = rotate(pre[:, HD : 2 * HD], cosine, sine).astype(BF16)
        kv_own[r, :, HD:] = pre[:, 2 * HD :].astype(BF16)
        for d in NEAR_LAST:
            kv_copies.append(
                send(
                    kv_own.at[r], kv_all.at[me, r], kv_send.at[r, d - 1], kv_recv.at[r, d - 1],
                    device(dz=d),
                )
            )
        sib_copies.append(
            send(kv_own.at[r], kv_all.at[me, r], sib_send.at[r, 0], sib_recv.at[r, 0], device(dc=1))
        )
    own.append(keep(kv_own, kv_all.at[me], local.at[2]))
    for copy in sq_copies:
        copy.wait()
    squares = sq_one[...] + (sq_y[0] + sq_y[1] + sq_y[2])
    sq_out[...] = squares
    ratios = mago_ref[...] / jnp.sqrt(squares)
    for s, size in tiles(width, 512):
        at = slice(s, s + size)
        one = join(0, 0, HD, at)
        two = join(3, HD + 2 * ff, ff, at)
        w_own[0:HD, at] = (one * ratios[0:1, at]).astype(BF16)
        w_own[HD + 2 * ff :, at] = (two * ratios[1:2, at]).astype(BF16)
        ino_out[0:16, at] = dot32(small[ff:], one.astype(BF16), ((0,), (0,)))[0:16]
        ino_out[16:32, at] = dot32(small[0:ff], two.astype(BF16), ((0,), (0,)))[32:48]
    sent[2] = begin(2, w_own.at[pl.ds(0, HD), cols], 0, HD)
    own.append(keep(w_own, weights_out.at[0], local.at[3]))
    more[0] = relay(0, sent[0], *where[0])

    def pass_kv(r):
        for k, d in enumerate(NEAR_LAST):
            kv_copies[3 * r + k].wait_recv()
            slot = ((z + Z - d) % Z) * 2 + core
            at = kv_all.at[slot, r]
            sib_copies.append(send(at, at, sib_send.at[r, d], sib_recv.at[r, d], device(dc=1)))

    for r in range(rows):
        pass_kv(r)
    more[1] = relay(1, sent[1], *where[1])
    own[2].wait()
    for copy in sib_copies:
        copy.wait_recv()
    own.append(keep(kv_all, kv_out, local.at[4]))
    spot_q = lax.broadcasted_iota(jnp.int32, (here, 1), 0) + me * here
    m_copies = []
    for i in (2, 1, 3, 0):
        row = (x + i) % X
        query = q_out[row]
        first = begin_ref[row]
        peak = jnp.full((here, 1), -1e30, F32)
        for b in range(length // KB):
            keys = jnp.concatenate(
                [kv_all[b * (KB // here) + k, row, :, :HD] for k in range(KB // here)], axis=0
            )
            raw = dot32(query, keys, ((1,), (1,))) * (HD**-0.5)
            key_spot = lax.broadcasted_iota(jnp.int32, (1, KB), 1) + b * KB
            ok = mask_of(first, spot_q, tag_ref[row, :, b * KB : (b + 1) * KB], key_spot)
            raw = jnp.where(ok, raw, -1e30)
            score[:, b * KB : (b + 1) * KB] = raw
            peak = jnp.maximum(peak, jnp.max(raw, axis=1, keepdims=True))
        total = jnp.zeros((here, 1), F32)
        gathered = jnp.zeros((here, HD), F32)
        for b in range(length // KB):
            power = jnp.exp(score[:, b * KB : (b + 1) * KB] - peak)
            total = total + jnp.sum(power, axis=1, keepdims=True)
            values = jnp.concatenate(
                [kv_all[b * (KB // here) + k, row, :, HD:] for k in range(KB // here)], axis=0
            )
            gathered = gathered + dot32(power.astype(BF16), values, ((1,), (0,)))
        soft[row] = gathered / total
        logs[row] = peak + jnp.log(total)
        for j in range(Y):
            mixed[i, j * piece : (j + 1) * piece] = soft[
                row, pl.ds(pl.multiple_of(((y + j) % Y) * piece, piece), piece)
            ].astype(BF16)
        if i:
            m_copies.append(
                send(mixed.at[i], mixed_x.at[i], m_send.at[i - 1], m_recv.at[i - 1], device(dx=i))
            )
        else:
            mixed_x[0] = mixed[0]
        if i == 2:
            more[2] = relay(2, sent[2], *where[2])
        if i == 3:
            last[0] = relay_far(0, more[0], *where[0])
    own.append(keep(soft, soft_out, local.at[5]))
    own.append(keep(logs, log_out, local.at[6]))
    last[1] = relay_far(1, more[1], *where[1])
    last[2] = relay_far(2, more[2], *where[2])
    for copy in m_copies:
        copy.wait()
    own.append(keep(mixed_x, mixed_out, local.at[7]))
    for copy in kv_copies + sib_copies:
        copy.wait_send()
    for copy in sm_copies:
        copy.wait()
    for p in range(PIECES):
        finish(sent[p], more[p], last[p])
    for copy in n_copies[rows - 2 :]:
        copy.wait()
    own.pop(2)
    for copy in own:
        copy.wait()


def front(
    hidden, gain, fa, la, ua, maga, thin, fw, aw, bw, mage, mago, el, small, cos, sin, begin, tag
):
    rows, here, width = hidden.shape
    count = fw.shape[0]
    ff = (count - HD) // 3
    length = 2 * Z * here
    s = jax.ShapeDtypeStruct
    return call(
        front_kernel,
        (
            s((X, here, HD), BF16),
            s((rows, here, HD), F32),
            s((rows, here, 1), F32),
            s((2 * Z, rows, here, 2 * HD), BF16),
            s((X, count, width), BF16),
            s((width, 3 * HD), BF16),
            s((rows, here, HD), BF16),
            s((rows, here, 3 * HD), F32),
            s((rows, here, HD), F32),
            s((3, HD), F32),
            s((2 * ff, 1), F32),
            s((2, width), F32),
            s((3, 16, HD), F32),
            s((2 * ff, HD), F32),
            s((32, width), F32),
            s((rows, here, width), BF16),
            s((X, ff + HD, HD), BF16),
        ),
        [VM] * 18,
        (ANY,) * 6 + (VM,) * 9 + (ANY, ANY),
        [
            pltpu.VMEM((2 * Z, rows, here, 2 * HD), BF16),
            pltpu.VMEM((here, length), F32),
            pltpu.VMEM((rows, here, HD), F32),
            pltpu.VMEM((rows, here, 1), F32),
            pltpu.VMEM((X, here, HD), BF16),
            pltpu.VMEM((X, here, HD), BF16),
            pltpu.VMEM((ff, width), F32),
            pltpu.VMEM((count, width), BF16),
            pltpu.VMEM((width, 3 * HD), BF16),
            pltpu.VMEM((2, here, width), BF16),
            pltpu.VMEM((rows, here, 2 * HD), BF16),
            pltpu.VMEM((ff + HD, HD), BF16),
            pltpu.VMEM((3, 2, width), F32),
            pltpu.VMEM((3, 2, width), F32),
            pltpu.VMEM((2, width), F32),
            pltpu.VMEM((width, HD), F32),
            dma(rows, 3), dma(rows, 3), dma(rows, 4), dma(rows, 4),
            dma(PIECES, 2), dma(PIECES, 2), dma(PIECES, 2), dma(PIECES, 2),
            dma(PIECES, 3), dma(PIECES, 3),
            dma(3), dma(3), dma(2, 3), dma(2, 3), dma(3), dma(3), dma(8), dma(rows),
        ],
        0,
        2 * 2 * rows * here * length * HD + 2 * rows * here * width * 4 * HD,
        32 * 2**20,
    )(hidden, gain, fa, la, ua, maga, thin, fw, aw, bw, mage, mago, el, small, cos, sin, begin, tag)


def feed_kernel(
    mixed_ref, hid_ref, gain_ref, cot_ref, weights_ref, small_ref, el_ref, upper_ref, mago_ref,
    sq_ref,
    resid_grad_out, block_out, dmix_out, early_out, columns_out, lower_out,
    out_w, gate_w, up_w, down_w, normed, low, act, dgate, dup, sends, recvs, acc, resid_s, mags,
    load, s_send, s_recv, a_send, a_recv, b_send, b_recv, ws_send, ws_recv,
):
    z, core, y, x = place()
    width = hid_ref.shape[1]
    piece = hid_ref.shape[0]
    here = cot_ref.shape[0]
    ff = gate_w.shape[0] // X
    cols = pl.ds(pl.multiple_of(core * (width // 2), width // 2), width // 2)
    down_rows = pl.ds(HD + 2 * ff, ff)
    loads = [[], [], [], []]
    for w, (dst, start, size) in enumerate(((out_w, 0, HD), (gate_w, HD, ff), (up_w, HD + ff, ff))):
        for i in range(X):
            loads[w].append(
                keep(
                    weights_ref.at[i, pl.ds(start, size)], dst.at[pl.ds(i * size, size)],
                    load.at[w, i],
                )
            )
    loads[3].append(keep(weights_ref.at[0, down_rows], down_w.at[pl.ds(0, ff)], load.at[3, 0]))
    greet(
        [device(dy=d) for d in (1, 2, 3)] + [device(dx=1), device(dx=3), device(dc=1)]
    )

    def there(slot, start, size):
        return down_w.at[pl.ds(slot * ff + start, size), cols]

    begin, relay, relay_far, finish = relay_plan(
        there, a_send, a_recv, b_send, b_recv, ws_send, ws_recv, cols
    )
    sent = begin(0, weights_ref.at[0, down_rows, cols], 0, ff)

    def loaded(w):
        for copy in loads[w]:
            copy.wait()

    def start_scatter(k):
        return [
            send(
                sends.at[k, d - 1], recvs.at[k, d - 1], s_send.at[k, d - 1], s_recv.at[k, d - 1],
                device(dy=d),
            )
            for d in NEAR_LAST
        ]

    def put(k, part, start, size):
        acc[k, :, start : start + size] = part[:piece]
        for d in range(1, Y):
            sends[k, d - 1, :, start : start + size] = part[d * piece : (d + 1) * piece].astype(BF16)

    def summed(k, copies):
        for copy in copies:
            copy.wait()
        return acc[k] + (
            recvs[k, 0].astype(F32) + recvs[k, 1].astype(F32) + recvs[k, 2].astype(F32)
        )

    def start_gather(buffer, k):
        return [
            send(
                buffer.at[pl.ds(0, piece)], buffer.at[pl.ds((Y - d) * piece, piece)],
                s_send.at[k, d - 1], s_recv.at[k, d - 1], device(dy=d),
            )
            for d in NEAR_LAST
        ]

    loaded(0)
    mixed_cat = jnp.concatenate([mixed_ref[i] for i in range(X)], axis=1)
    for start, size in tiles(width, 512):
        put(0, dot32(mixed_cat, out_w[:, start : start + size], ((1,), (0,))), start, size)
    copies = start_scatter(0)
    ratios = mago_ref[...] / jnp.sqrt(sq_ref[...])
    upper_o = (upper_ref[0:16] * ratios[0:1]).astype(BF16)
    upper_d = (upper_ref[16:32] * ratios[1:2]).astype(BF16)
    through_down = dot32(cot_ref[...], upper_d, ((1,), (1,))).astype(BF16)
    small = jnp.concatenate([small_ref[i, 0:ff] for i in range(X)], axis=0)
    small_o = jnp.concatenate([small_ref[i, ff:] for i in range(X)], axis=0)
    from_mixed = dot32(mixed_cat, small_o, ((1,), (0,)))[:, 0:16].astype(BF16)
    attended = summed(0, copies)
    acc[0] = attended
    gain = gain_ref[...]
    resid = hid_ref[...].astype(F32) + attended
    inverse = lax.rsqrt(jnp.mean(resid * resid, axis=1, keepdims=True) + epsilon)
    resid_s[...] = resid
    normed[0:piece] = (resid * inverse * gain).astype(BF16)
    copies = start_gather(normed, 3)
    more = relay(0, sent, 0, ff)
    loaded(1)
    loaded(2)
    loaded(3)
    for copy in copies:
        copy.wait()
    far = relay_far(0, more, 0, ff)
    finish(sent, more, far)
    for start, size in tiles(X * ff, 256):
        at = slice(start, start + size)
        gate = dot32(normed[...], gate_w[at], ((1,), (1,)))
        up = dot32(normed[...], up_w[at], ((1,), (1,)))
        d_act = dot32(cot_ref[...], down_w[at], ((1,), (1,)))
        sig = 1.0 / (1.0 + jnp.exp(-gate))
        gated = gate * sig
        act[:, at] = (gated * up).astype(BF16)
        d_gate = (d_act * up * sig * (1.0 + gate * (1.0 - sig))).astype(BF16)
        d_up = (d_act * gated).astype(BF16)
        dgate[:, at] = d_gate
        dup[:, at] = d_up
        mags[0:1, at] = jnp.sum(d_gate.astype(F32) * gate, axis=0, keepdims=True)
        mags[1:2, at] = jnp.sum(d_up.astype(F32) * up, axis=0, keepdims=True)
    for start, size in tiles(width, 512):
        at = slice(start, start + size)
        part = dot32(dgate[...], gate_w[:, at], ((1,), (0,)))
        part = part + dot32(dup[...], up_w[:, at], ((1,), (0,)))
        put(1, part, start, size)
    two_copies = start_scatter(1)
    for start, size in tiles(width, 512):
        at = slice(start, start + size)
        put(2, dot32(act[...], down_w[:, at], ((1,), (0,))), start, size)
    ff_copies = start_scatter(2)
    through = dot32(normed[...], el_ref[...], ((1,), (0,)))
    through = (through[:, 0:32] + through[:, 32:64]).astype(BF16)
    gate_down = dot32(dgate[...], small, ((1,), (0,)))[:, 0:16].astype(BF16)
    up_down = dot32(dup[...], small, ((1,), (0,)))[:, 16:32].astype(BF16)
    from_act = dot32(act[...], small, ((1,), (0,)))[:, 32:48].astype(BF16)
    small_t = jnp.transpose(small.astype(F32))
    pull_gate = (small_t[48:64] * mags[0:1]).astype(BF16)
    pull_up = (small_t[64:80] * mags[1:2]).astype(BF16)

    def columns(row, value):
        for i in range(X):
            columns_out[i, row : row + value.shape[0]] = value[:, i * ff : (i + 1) * ff]

    columns(0, dot32(through[:, 0:16], dgate[...], ((0,), (0,))))
    columns(16, dot32(through[:, 16:32], dup[...], ((0,), (0,))))
    columns(32, dot32(through_down, act[...], ((0,), (0,))))
    columns(48, jnp.concatenate([mags[...], jnp.zeros((6, X * ff), F32)], axis=0))
    early_out[0:16] = dot32(gate_down, normed[...], ((0,), (0,))) - dot32(
        pull_gate, gate_w[...], ((1,), (0,))
    )
    early_out[16:32] = dot32(up_down, normed[...], ((0,), (0,))) - dot32(
        pull_up, up_w[...], ((1,), (0,))
    )
    early_out[48:64] = dot32(from_act, cot_ref[...], ((0,), (0,)))
    d_two = summed(1, two_copies)
    resid = resid_s[...]
    inverse = lax.rsqrt(jnp.mean(resid * resid, axis=1, keepdims=True) + epsilon)
    scaled = d_two * gain
    cot_own = cot_ref[0:piece].astype(F32)
    d_resid = cot_own + (
        inverse * scaled
        - resid * (inverse * inverse * inverse) * jnp.mean(resid * scaled, axis=1, keepdims=True)
    )
    resid_grad_out[...] = d_resid
    own_low = d_resid.astype(BF16)
    low[0:piece] = own_low
    copies = start_gather(low, 4)
    mag_out = jnp.sum(own_low.astype(F32) * acc[0], axis=0, keepdims=True)
    feedforward = summed(2, ff_copies)
    block_out[...] = (resid_s[...] + feedforward).astype(BF16)
    mag_down = jnp.sum(cot_own * feedforward, axis=0, keepdims=True)
    early_out[64:80] = jnp.concatenate(
        [mag_out, mag_down, jnp.zeros((14, width), F32)], axis=0
    )
    for copy in copies:
        copy.wait()
    d_mixed = dot32(low[...], out_w[...], ((1,), (1,))).astype(BF16)
    for i in range(X):
        dmix_out[i] = d_mixed[:, i * HD : (i + 1) * HD]
    through_out = dot32(low[...], upper_o, ((1,), (1,))).astype(BF16)
    value = dot32(through_out, mixed_cat, ((0,), (0,)))
    for i in range(X):
        lower_out[i] = value[:, i * HD : (i + 1) * HD]
    early_out[32:48] = dot32(from_mixed, low[...], ((0,), (0,)))


def feed(mixed_x, hid_own, gain, cot_row, weights, small_x, el, upper, mago, squares):
    here, width = cot_row.shape
    piece = here // Y
    hidden = (weights.shape[1] - HD) // 3 * X
    s = jax.ShapeDtypeStruct
    return call(
        feed_kernel,
        (
            s((piece, width), F32),
            s((piece, width), BF16),
            s((X, here, HD), BF16),
            s((80, width), F32),
            s((X, 56, hidden // X), F32),
            s((X, 16, HD), F32),
        ),
        [VM, VM, VM, VM, ANY, VM, VM, VM, VM, VM],
        (VM,) * 6,
        [
            pltpu.VMEM((X * HD, width), BF16),
            pltpu.VMEM((hidden, width), BF16),
            pltpu.VMEM((hidden, width), BF16),
            pltpu.VMEM((hidden, width), BF16),
            pltpu.VMEM((here, width), BF16),
            pltpu.VMEM((here, width), BF16),
            pltpu.VMEM((here, hidden), BF16),
            pltpu.VMEM((here, hidden), BF16),
            pltpu.VMEM((here, hidden), BF16),
            pltpu.VMEM((3, Y - 1, piece, width), BF16),
            pltpu.VMEM((3, Y - 1, piece, width), BF16),
            pltpu.VMEM((3, piece, width), F32),
            pltpu.VMEM((piece, width), F32),
            pltpu.VMEM((2, hidden), F32),
            dma(4, X), dma(5, 3), dma(5, 3), dma(1, 2), dma(1, 2), dma(1, 2), dma(1, 2),
            dma(1, 3), dma(1, 3),
        ],
        1,
        2 * here * hidden * width * 6,
        32 * 2**20,
    )(mixed_x, hid_own, gain, cot_row, weights, small_x, el, upper, mago, squares)


def attend_back_kernel(
    q_ref, kv_ref, dmix_ref, soft_ref, log_ref, begin_ref, tag_ref, cos_ref, sin_ref, block_ref,
    grads_out, block_out,
    kv_all, dmix_all, dmix_abs, part, own, sib_s, sib_r, z_own, z_s, z_r, dq_s,
    d_send, d_recv, b_send, b_recv, sib_send, sib_recv, z_send, z_recv, local,
):
    z, core, y, x = place()
    me = z * 2 + core
    rows, here = q_ref.shape[0], q_ref.shape[1]
    piece, width = block_ref.shape
    half = width // 2
    load = keep(kv_ref, kv_all, local.at[0])
    greet(
        [device(dx=d) for d in (1, 2, 3)]
        + [device(dy=d) for d in (1, 2, 3)]
        + [device(dz=d) for d in (1, 2, 3)]
        + [device(dc=1)]
    )
    d_copies = [
        send(
            dmix_ref.at[X - d], dmix_all.at[x], d_send.at[d - 1], d_recv.at[d - 1], device(dx=d)
        )
        for d in NEAR_LAST
    ]
    own_mix = keep(dmix_ref.at[0], dmix_all.at[x], local.at[1])
    tokens = pl.ds(pl.multiple_of(y * piece, piece), piece)
    left, right = pl.ds(0, half), pl.ds(half, half)
    own_block = keep(block_ref, block_out.at[x, tokens], local.at[2])
    block_one = []
    for d in NEAR_LAST:
        block_one.append(
            send(
                block_ref.at[:, left], block_out.at[x, tokens, left],
                b_send.at[0, d - 1], b_recv.at[0, d - 1], device(dx=d),
            )
        )
        block_one.append(
            send(
                block_ref.at[:, right], block_out.at[x, tokens, right],
                b_send.at[1, d - 1], b_recv.at[1, d - 1], device(dy=d),
            )
        )
    load.wait()
    own_mix.wait()
    for copy in d_copies:
        copy.wait()
    spot_q = lax.broadcasted_iota(jnp.int32, (here, 1), 0) + me * here
    sib_copies, z_copies, block_two = [], [], []

    def pass_on(r):
        sib_copies[r].wait()
        z_own[r] = own[r, z] + sib_r[r, z].astype(F32)
        for d in NEAR_LAST:
            to = (z + d) % Z
            z_s[r, d - 1] = (own[r, to] + sib_r[r, to].astype(F32)).astype(BF16)
            z_copies.append(
                send(
                    z_s.at[r, d - 1], z_r.at[r, d - 1], z_send.at[r, d - 1], z_recv.at[r, d - 1],
                    device(dz=d),
                )
            )

    def back(a, r):
        cosine, sine = cos_ref[r], sin_ref[r]
        weighted = a * sine
        turned = jnp.concatenate([weighted[:, HD // 2 :], -weighted[:, : HD // 2]], axis=1)
        return a * cosine + turned

    for r in range(rows):
        for j in range(Y):
            dmix_abs[pl.ds(pl.multiple_of(((y + j) % Y) * piece, piece), piece)] = dmix_all[
                r, j * piece : (j + 1) * piece
            ]
        query = q_ref[r]
        grad = dmix_abs[...]
        delta = jnp.sum(grad.astype(F32) * soft_ref[r], axis=1, keepdims=True)
        begin = begin_ref[r]
        log = log_ref[r]
        d_query = jnp.zeros((here, HD), F32)
        for b in range(Z):
            keys = jnp.concatenate([kv_all[2 * b + k, r, :, :HD] for k in range(2)], axis=0)
            values = jnp.concatenate([kv_all[2 * b + k, r, :, HD:] for k in range(2)], axis=0)
            raw = dot32(query, keys, ((1,), (1,))) * (HD**-0.5)
            key_spot = lax.broadcasted_iota(jnp.int32, (1, KB), 1) + b * KB
            ok = mask_of(begin, spot_q, tag_ref[r, :, b * KB : (b + 1) * KB], key_spot)
            probs = jnp.exp(jnp.where(ok, raw, -1e30) - log)
            d_probs = dot32(grad, values, ((1,), (1,)))
            d_scores = (probs * (d_probs - delta)).astype(BF16)
            d_query = d_query + dot32(d_scores, keys, ((1,), (0,)))
            d_keys = dot32(d_scores, query, ((0,), (0,))) * (HD**-0.5)
            d_values = dot32(probs.astype(BF16), grad, ((0,), (0,)))
            for k in range(2):
                part[b, k, :, :HD] = d_keys[k * here : (k + 1) * here]
                part[b, k, :, HD:] = d_values[k * here : (k + 1) * here]
        dq_s[r] = d_query * (HD**-0.5)
        for b in range(Z):
            sib_s[r, b] = part[b, 1 - core].astype(BF16)
            own[r, b] = part[b, core]
        sib_copies.append(
            send(sib_s.at[r], sib_r.at[r], sib_send.at[r], sib_recv.at[r], device(dc=1))
        )
        grads_out[r, :, :HD] = back(dq_s[r], r).astype(BF16)
        if r:
            pass_on(r - 1)
        if r == 1:
            own_block.wait()
            for copy in block_one:
                copy.wait()
            for d in NEAR_LAST:
                spread = block_out.at[:, tokens, left]
                block_two.append(
                    send(
                        spread, spread, b_send.at[2, d - 1], b_recv.at[2, d - 1], device(dy=d)
                    )
                )
                spread = block_out.at[x, :, right]
                block_two.append(
                    send(
                        spread, spread, b_send.at[3, d - 1], b_recv.at[3, d - 1], device(dx=d)
                    )
                )
    pass_on(rows - 1)
    for r in range(rows):
        for copy in z_copies[3 * r : 3 * r + 3]:
            copy.wait()
        total = z_own[r] + (
            z_r[r, 0].astype(F32) + z_r[r, 1].astype(F32) + z_r[r, 2].astype(F32)
        )
        grads_out[r, :, HD : 2 * HD] = back(total[:, :HD], r).astype(BF16)
        grads_out[r, :, 2 * HD :] = total[:, HD:].astype(BF16)
    for copy in block_two:
        copy.wait()


def attend_back(queries, kv, dmix, soft, log, begin, tag, cosine, sine, block):
    rows, here, _ = queries.shape
    piece, width = block.shape
    return call(
        attend_back_kernel,
        (
            jax.ShapeDtypeStruct((rows, here, 3 * HD), BF16),
            jax.ShapeDtypeStruct((rows, here, width), BF16),
        ),
        [VM, ANY, VM, VM, VM, VM, VM, VM, VM, VM],
        (VM, ANY),
        [
            pltpu.VMEM((2 * Z, rows, here, 2 * HD), BF16),
            pltpu.VMEM((rows, here, HD), BF16),
            pltpu.VMEM((here, HD), BF16),
            pltpu.VMEM((Z, 2, here, 2 * HD), F32),
            pltpu.VMEM((rows, Z, here, 2 * HD), F32),
            pltpu.VMEM((rows, Z, here, 2 * HD), BF16),
            pltpu.VMEM((rows, Z, here, 2 * HD), BF16),
            pltpu.VMEM((rows, here, 2 * HD), F32),
            pltpu.VMEM((rows, Z - 1, here, 2 * HD), BF16),
            pltpu.VMEM((rows, Z - 1, here, 2 * HD), BF16),
            pltpu.VMEM((rows, here, HD), F32),
            dma(3), dma(3), dma(4, 3), dma(4, 3), dma(rows), dma(rows), dma(rows, 3), dma(rows, 3),
            dma(3),
        ],
        2,
        2 * 5 * rows * here * 2 * Z * here * HD,
        32 * 2**20,
    )(queries, kv, dmix, soft, log, begin, tag, cosine, sine, block)


def input_grad_kernel(
    grads_ref, weight_ref, hid_ref, gain_ref, dres_ref,
    grad_out,
    rel, send_l, send_r, recv_l, recv_r, acc_l, acc_r, send_2, recv_2, d_one, spread,
    s_one, r_one, s_two, r_two, s_gat, r_gat, local,
):
    z, core, y, x = place()
    rows, here, deep = grads_ref.shape
    piece, width = hid_ref.shape
    half = width // 2
    for i in range(X):
        for j in range(Y):
            rel[i, j] = grads_ref[
                (x + i) % X, pl.ds(pl.multiple_of(((y + j) % Y) * piece, piece), piece)
            ]
    greet([device(dx=d) for d in (1, 2, 3)] + [device(dy=d) for d in (1, 2, 3)])
    one = []
    for d in (2, 1, 3, 0):
        lhs_l = rel[d].reshape(here, deep)
        lhs_r = jnp.concatenate([rel[i, d] for i in range(X)], axis=0)
        for start, size in tiles(half, 512):
            at = slice(start, start + size)
            part = dot32(lhs_l, weight_ref[at], ((1,), (1,)))
            if d:
                send_l[d - 1, :, at] = part.astype(BF16)
            else:
                acc_l[:, at] = part
        if d:
            one.append(
                send(send_l.at[d - 1], recv_l.at[d - 1], s_one.at[0, d - 1], r_one.at[0, d - 1],
                     device(dx=d))
            )
        for start, size in tiles(half, 512):
            at = slice(start, start + size)
            part = dot32(lhs_r, weight_ref[half + start : half + start + size], ((1,), (1,)))
            if d:
                send_r[d - 1, :, at] = part.astype(BF16)
            else:
                acc_r[:, at] = part
        if d:
            one.append(
                send(send_r.at[d - 1], recv_r.at[d - 1], s_one.at[1, d - 1], r_one.at[1, d - 1],
                     device(dy=d))
            )
    for copy in one:
        copy.wait()
    two = []
    for k, (acc, recv) in enumerate(((acc_l, recv_l), (acc_r, recv_r))):
        for d in (2, 1, 3, 0):
            at = slice(d * piece, (d + 1) * piece)
            part = acc[at] + (
                recv[0, at].astype(F32) + recv[1, at].astype(F32) + recv[2, at].astype(F32)
            )
            if d:
                send_2[k, d - 1] = part.astype(BF16)
                two.append(
                    send(send_2.at[k, d - 1], recv_2.at[k, d - 1], s_two.at[k, d - 1],
                         r_two.at[k, d - 1], device(dx=d) if k else device(dy=d))
                )
            else:
                d_one[:, k * half : (k + 1) * half] = part
    for copy in two:
        copy.wait()
    for k in range(2):
        d_one[:, k * half : (k + 1) * half] += (
            recv_2[k, 0].astype(F32) + recv_2[k, 1].astype(F32) + recv_2[k, 2].astype(F32)
        )
    inputs = hid_ref[...].astype(F32)
    inverse = lax.rsqrt(jnp.mean(inputs * inputs, axis=1, keepdims=True) + epsilon)
    scaled = d_one[...] * gain_ref[...]
    result = dres_ref[...] + (
        inverse * scaled
        - inputs * (inverse * inverse * inverse) * jnp.mean(inputs * scaled, axis=1, keepdims=True)
    )
    tokens = pl.ds(pl.multiple_of(y * piece, piece), piece)
    left, right = pl.ds(0, half), pl.ds(half, half)
    spread[x, tokens] = result.astype(BF16)
    gat = []
    for d in NEAR_LAST:
        for k, (cut, to) in enumerate(((left, device(dx=d)), (right, device(dy=d)))):
            at = spread.at[x, tokens, cut]
            gat.append(send(at, at, s_gat.at[k, d - 1], r_gat.at[k, d - 1], to))
    for copy in gat:
        copy.wait()
    gat = []
    for d in NEAR_LAST:
        at = spread.at[:, tokens, left]
        gat.append(send(at, at, s_gat.at[2, d - 1], r_gat.at[2, d - 1], device(dy=d)))
        at = spread.at[x, :, right]
        gat.append(send(at, at, s_gat.at[3, d - 1], r_gat.at[3, d - 1], device(dx=d)))
    for copy in gat:
        copy.wait()
    out = keep(spread, grad_out, local.at[0])
    out.wait()


def input_grad(grads, weight, hid_own, gain, d_resid):
    rows, here, deep = grads.shape
    piece, width = hid_own.shape
    half = width // 2
    return call(
        input_grad_kernel,
        jax.ShapeDtypeStruct((rows, here, width), BF16),
        [VM] * 5,
        ANY,
        [
            pltpu.VMEM((X, Y, piece, deep), BF16),
            pltpu.VMEM((3, here, half), BF16),
            pltpu.VMEM((3, here, half), BF16),
            pltpu.VMEM((3, here, half), BF16),
            pltpu.VMEM((3, here, half), BF16),
            pltpu.VMEM((here, half), F32),
            pltpu.VMEM((here, half), F32),
            pltpu.VMEM((2, 3, piece, half), BF16),
            pltpu.VMEM((2, 3, piece, half), BF16),
            pltpu.VMEM((piece, width), F32),
            pltpu.VMEM((rows, here, width), BF16),
            dma(2, 3), dma(2, 3), dma(2, 3), dma(2, 3), dma(4, 3), dma(4, 3), dma(1),
        ],
        3,
        2 * rows * here * deep * width,
        16 * 2**20,
    )(grads, weight, hid_own, gain, d_resid)


def sums_kernel(
    all_ref, block_ref, lower_ref, ctx_ref,
    all_out, block_out, ctx_out,
    c_r, z_s, z_r, x_s, x_r, y_s, y_r, gath, bx_r, lx_r, b_one, b_two, e_one, e_two, e_z, b_z,
    ss, rs,
):
    z, core, y, x = place()
    n, width = all_ref.shape
    nc, nz = n // 2, n // 2 // Z
    wx, wy = width // X, width // X // Y
    rank = lower_ref.shape[1]
    greet(
        [device(dx=d) for d in (1, 2, 3)]
        + [device(dy=d) for d in (1, 2, 3)]
        + [device(dz=d) for d in (1, 2, 3)]
        + [device(dc=1)]
    )

    def go(k, d, src, dst, to):
        return send(src, dst, ss.at[k, d], rs.at[k, d], to)

    def ds(index, size):
        return pl.ds(pl.multiple_of(index * size, size), size)

    def done(copies):
        for copy in copies:
            copy.wait()

    first = [go(0, 0, all_ref.at[ds(1 - core, nc)], c_r, device(dc=1))]
    slots = []
    for d in NEAR_LAST:
        slots.append(go(1, d, block_ref.at[X - d], bx_r.at[d - 1], device(dx=d)))
        slots.append(go(2, d, lower_ref.at[X - d], lx_r.at[d - 1], device(dx=d)))
    done(first)
    z_s[...] = all_ref[ds(core, nc)] + c_r[...]
    zc = [go(3, d, z_s.at[ds((z + d) % Z, nz)], z_r.at[d - 1], device(dz=d)) for d in NEAR_LAST]
    done(slots)
    b_one[...] = block_ref[0] + (bx_r[0] + bx_r[1] + bx_r[2])
    e_one[:rank] = lower_ref[0] + (lx_r[0] + lx_r[1] + lx_r[2])
    e_one[rank:] = ctx_ref[...]
    cc = [
        go(4, 0, b_one, b_two, device(dc=1)),
        go(5, 0, e_one, e_two, device(dc=1)),
    ]
    done(cc)
    b_two[...] += b_one[...]
    e_two[...] += e_one[...]
    cz = []
    for d in NEAR_LAST:
        cz.append(go(6, d, b_two, b_z.at[d - 1], device(dz=d)))
        cz.append(go(7, d, e_two, e_z.at[d - 1], device(dz=d)))
    done(zc)
    x_s[...] = z_s[ds(z, nz)] + (z_r[0] + z_r[1] + z_r[2])
    xc = [go(8, d, x_s.at[:, ds((x + d) % X, wx)], x_r.at[d - 1], device(dx=d)) for d in NEAR_LAST]
    done(xc)
    y_s[...] = x_s[:, ds(x, wx)] + (x_r[0] + x_r[1] + x_r[2])
    yc = [go(9, d, y_s.at[:, ds((y + d) % Y, wy)], y_r.at[d - 1], device(dy=d)) for d in NEAR_LAST]
    done(yc)
    mine = ds(core * Z + z, nz)
    at_y = x * Y + y
    gath[mine, ds(at_y, wy)] = y_s[:, ds(y, wy)] + (y_r[0] + y_r[1] + y_r[2])
    spot = gath.at[mine, ds(at_y, wy)]
    done([go(10, d, spot, spot, device(dy=d)) for d in NEAR_LAST])
    spot = gath.at[mine, ds(x, wx)]
    done([go(11, d, spot, spot, device(dx=d)) for d in NEAR_LAST])
    spot = gath.at[mine]
    done([go(12, d, spot, spot, device(dz=d)) for d in NEAR_LAST])
    spot = gath.at[ds(core, nc)]
    done([go(13, 0, spot, spot, device(dc=1))])
    all_out[...] = gath[...]
    done(cz)
    block_out[...] = b_two[...] + (b_z[0] + b_z[1] + b_z[2])
    ctx_out[...] = e_two[...] + (e_z[0] + e_z[1] + e_z[2])


def sums(everywhere, block, lower, local):
    n, width = everywhere.shape
    _, bn, bw = block.shape
    rank = lower.shape[1]
    en = local.shape[0] + rank
    nc, nz = n // 2, n // 2 // Z
    wx, wy = width // X, width // X // Y
    return call(
        sums_kernel,
        (
            jax.ShapeDtypeStruct((n, width), F32),
            jax.ShapeDtypeStruct((bn, bw), F32),
            jax.ShapeDtypeStruct((en, HD), F32),
        ),
        [VM] * 4,
        (VM,) * 3,
        [
            pltpu.VMEM((nc, width), F32),
            pltpu.VMEM((nc, width), F32),
            pltpu.VMEM((3, nz, width), F32),
            pltpu.VMEM((nz, width), F32),
            pltpu.VMEM((3, nz, wx), F32),
            pltpu.VMEM((nz, wx), F32),
            pltpu.VMEM((3, nz, wy), F32),
            pltpu.VMEM((n, width), F32),
            pltpu.VMEM((3, bn, bw), F32),
            pltpu.VMEM((3, rank, HD), F32),
            pltpu.VMEM((bn, bw), F32),
            pltpu.VMEM((bn, bw), F32),
            pltpu.VMEM((en, HD), F32),
            pltpu.VMEM((en, HD), F32),
            pltpu.VMEM((3, en, HD), F32),
            pltpu.VMEM((3, bn, bw), F32),
            dma(14, 4), dma(14, 4),
        ],
        4,
        2**20,
        2**22,
    )(everywhere, block, lower, local)


def on_device(
    hidden,
    segments,
    key_attendable,
    attention_gain,
    feedforward_gain,
    attend_frozen,
    output_frozen,
    expand_frozen,
    reduce_frozen,
    attend_lower,
    attend_upper,
    attend_magnitude,
    output_lower,
    output_upper,
    output_magnitude,
    expand_lower,
    expand_upper,
    expand_magnitude,
    reduce_lower,
    reduce_upper,
    reduce_magnitude,
    cotangent,
):
    rows, here, width = hidden.shape
    length = segments.shape[1]
    ff = reduce_frozen.shape[0]
    flat = rows * here
    piece = here // Y
    rank = output_lower.shape[1]
    ctx = lax.axis_index("ctx")
    tp = lax.axis_index("tp")
    y, x = tp // X, tp % X
    offset = ctx * here
    share = 1.0 / (2 * Z)

    def left_factor(a):
        high, low = halves(a)
        return jnp.concatenate([high, high, low], axis=-1)

    def right_factor(a):
        high, low = halves(a)
        return jnp.concatenate([high, low, high], axis=-2)

    fw = jnp.concatenate(
        [output_frozen, expand_frozen[0].T, expand_frozen[1].T, reduce_frozen], axis=0
    )
    expand_upper_t = expand_upper.transpose(0, 2, 1)
    aw = left_factor(
        jnp.concatenate([output_lower, expand_upper_t[0], expand_upper_t[1], reduce_lower], axis=0)
    )
    bw = right_factor(
        jnp.stack([output_upper, expand_lower[0].T, expand_lower[1].T, reduce_upper], axis=0)
    )
    la = left_factor(attend_lower)
    ua = right_factor(attend_upper)
    flat_lower = attend_lower.transpose(1, 0, 2).reshape(width, 3 * rank)
    high, low = halves(flat_lower)
    thin = jnp.concatenate([high, low, jnp.zeros((width, HD - 6 * rank), BF16)], axis=1)
    flat_lower = expand_lower.transpose(1, 0, 2).reshape(width, 2 * rank)
    high, low = halves(flat_lower)
    el = jnp.concatenate([high, low, jnp.zeros((width, HD - 4 * rank), BF16)], axis=1)
    small = jnp.concatenate([expand_upper_t[0], expand_upper_t[1], reduce_lower], axis=1)
    small = jnp.concatenate(
        [
            jnp.pad(small, ((0, 0), (0, HD - 3 * rank))),
            jnp.pad(output_lower, ((0, 0), (0, HD - rank))),
        ],
        axis=0,
    )
    mago = jnp.stack([output_magnitude, reduce_magnitude])
    upper = jnp.concatenate([output_upper, reduce_upper], axis=0)

    levels = jnp.arange(SEGS, dtype=jnp.int32)
    below_count = jnp.sum((segments[:, None, :] < levels[None, :, None]).astype(F32), axis=2)
    segments_here = lax.dynamic_slice_in_dim(segments, offset, here, 1)
    begin_here = jnp.sum(
        (segments_here[:, :, None] == levels[None, None, :]).astype(F32) * below_count[:, None, :],
        axis=2,
    )
    spot_here = offset + jnp.arange(here, dtype=jnp.int32)
    places = spot_here.astype(F32)[None, :] - begin_here
    frequency = rotary_base ** (-(2.0 * jnp.arange(HD // 2).astype(F32)) / HD)
    frequency = jnp.concatenate([frequency, frequency])
    angles = places[:, :, None] * frequency[None, None, :]
    cosine, sine_part = jnp.cos(angles), jnp.sin(angles)
    spots = jnp.arange(length, dtype=jnp.int32)[None]
    key_tag = jnp.where(key_attendable == 1, spots, -1)[:, None, :]
    begin = begin_here.astype(jnp.int32)[:, :, None]
    gain_one = attention_gain.astype(F32)
    gain_two = feedforward_gain.astype(F32)

    def take_row(a):
        mine = lax.dynamic_index_in_dim(a, x, 0, keepdims=False)
        return roll_blocks(mine.reshape(Y, piece, width), 0, y)

    (
        mixed_parts,
        soft,
        log_total,
        all_pairs,
        weights_x,
        weight_attend,
        queries,
        pre,
        through_three,
        column_attend,
        column_expand,
        squares,
        inner_attend,
        inner_expand,
        inner_both,
        normed_one,
        small_x,
    ) = front(
        hidden,
        gain_one[None],
        attend_frozen,
        la,
        ua,
        attend_magnitude,
        thin,
        fw,
        aw,
        bw,
        expand_magnitude.reshape(2 * ff, 1),
        mago,
        el,
        small,
        cosine,
        sine_part,
        begin,
        key_tag,
    )
    hid_own = take_row(hidden)[0]
    cot_row = take_row(cotangent).reshape(here, width)
    d_resid, block_own, d_mixed_parts, early, block_x, lower_out = feed(
        mixed_parts, hid_own, gain_two[None], cot_row, weights_x, small_x, el, upper, mago, squares
    )
    grads_low, block_output = attend_back(
        queries,
        all_pairs,
        d_mixed_parts,
        soft,
        log_total,
        begin,
        key_tag,
        cosine,
        sine_part,
        block_own,
    )
    hidden_grad = input_grad(grads_low, weight_attend, hid_own, gain_one[None], d_resid)
    hidden_grad = hidden_grad.astype(F32)
    pre = pre.reshape(flat, 3 * HD)
    through_three = through_three.reshape(flat, HD)
    normed_one = normed_one.reshape(flat, width)

    late = []
    local = []
    mags = []
    through_three = through_three[:, : 3 * rank] + through_three[:, 3 * rank : 6 * rank]
    flat_grads = grads_low.reshape(flat, 3, HD)
    flat_pre = pre.reshape(flat, 3, HD)
    downs = []
    for m in range(3):
        grad = flat_grads[:, m]
        ratio = attend_magnitude[m] / column_attend[m]
        mag = jnp.sum(grad.astype(F32) * flat_pre[:, m], axis=0)
        mags.append(mag / attend_magnitude[m])
        pull = attend_magnitude[m] * (mags[m] * column_attend[m]) / column_attend[m] ** 3
        upper_part = exact_dot_left(
            through_three[:, m * rank : (m + 1) * rank], grad, ((0,), (0,))
        )
        local.append(adapter_scale * (upper_part * ratio - inner_attend[m] * pull))
        downs.append(exact_dot(grad, attend_upper[m] * ratio, ((1,), (1,))))
        pulled = attend_upper[m] * pull
        outer = exact_dot_left(pulled, attend_frozen[m], ((1,), (1,)))
        outer = outer + adapter_scale * jnp.dot(
            jnp.dot(pulled, attend_upper[m].T, precision=lax.Precision.HIGHEST),
            attend_lower[m].T,
            precision=lax.Precision.HIGHEST,
        )
        late.append(outer)
    late = exact_dot_left(jnp.concatenate(downs, axis=1), normed_one, ((0,), (0,))) - (
        jnp.concatenate(late, axis=0)
    )
    local = jnp.concatenate(local + [jnp.stack(mags), jnp.zeros((5, HD), F32)], axis=0)
    everywhere, block_x, small_ctx = sums(
        jnp.concatenate(
            [early, inner_both * share, late, jnp.zeros((32, width), F32)], axis=0
        ),
        block_x,
        lower_out,
        local,
    )
    lower_out, local = small_ctx[:rank], small_ctx[rank:]
    late = adapter_scale * everywhere[7 * rank : 10 * rank]
    early = everywhere[: 7 * rank]

    attend_lower_grad = late.reshape(3, rank, width).transpose(0, 2, 1)
    attend_upper_grad = local[: 3 * rank].reshape(3, rank, HD)
    attend_magnitude_grad = local[3 * rank : 3 * rank + 3]
    column_expand = column_expand.reshape(2, ff)
    inner_expand = inner_expand.reshape(2, ff, HD)
    inner_expand = inner_expand[..., : 2 * rank] + inner_expand[..., 2 * rank : 4 * rank]
    expand_magnitude_grad = block_x[3 * rank : 3 * rank + 2] / expand_magnitude
    pull_expand = expand_magnitude * expand_magnitude_grad / column_expand**2
    ratio_expand = expand_magnitude / column_expand
    expand_upper_grad = jnp.stack(
        [
            adapter_scale
            * (
                block_x[m * rank : (m + 1) * rank] * ratio_expand[m]
                - inner_expand[m, :, m * rank : (m + 1) * rank].T * pull_expand[m]
            )
            for m in range(2)
        ]
    )
    expand_lower_grad = adapter_scale * early[: 2 * rank].reshape(2, rank, width).transpose(0, 2, 1)
    columns = jnp.sqrt(squares)
    magnitude_grads = early[4 * rank : 4 * rank + 2] / mago
    pulls = mago * magnitude_grads / squares
    ratios = mago / columns
    output_magnitude_grad = magnitude_grads[0]
    reduce_magnitude_grad = magnitude_grads[1]
    output_upper_grad = adapter_scale * (
        early[2 * rank : 3 * rank] * ratios[0] - early[5 * rank : 6 * rank] * pulls[0]
    )
    reduce_upper_grad = adapter_scale * (
        early[3 * rank : 4 * rank] * ratios[1] - early[6 * rank : 7 * rank] * pulls[1]
    )

    def pulled_rows(frozen, lower, upper, pull):
        pulled = upper * pull
        rows_part = exact_dot(frozen, pulled, ((1,), (1,)))
        return rows_part + adapter_scale * jnp.dot(
            lower,
            jnp.dot(upper, pulled.T, precision=lax.Precision.HIGHEST),
            precision=lax.Precision.HIGHEST,
        )

    output_lower_grad = adapter_scale * (
        lower_out.T - pulled_rows(output_frozen, output_lower, output_upper, pulls[0])
    )
    reduce_lower_grad = adapter_scale * (
        block_x[2 * rank : 3 * rank].T
        - pulled_rows(reduce_frozen, reduce_lower, reduce_upper, pulls[1])
    )
    return (
        block_output,
        hidden_grad,
        attend_lower_grad,
        attend_upper_grad,
        attend_magnitude_grad,
        output_lower_grad,
        output_upper_grad,
        output_magnitude_grad,
        expand_lower_grad,
        expand_upper_grad,
        expand_magnitude_grad,
        reduce_lower_grad,
        reduce_upper_grad,
        reduce_magnitude_grad,
    )


def solution(mesh):
    placed = (
        P(None, "ctx", None),
        P(),
        P(),
        P(),
        P(),
        P(None, None, "tp"),
        P("tp", None),
        P(None, None, "tp"),
        P("tp", None),
        P(),
        P(None, None, "tp"),
        P(None, "tp"),
        P("tp", None),
        P(),
        P(),
        P(),
        P(None, None, "tp"),
        P(None, "tp"),
        P("tp", None),
        P(),
        P(),
        P(None, "ctx", None),
    )
    return jax.shard_map(
        on_device,
        mesh=mesh,
        in_specs=placed,
        out_specs=(
            P(None, "ctx", None),
            P(None, "ctx", None),
            P(),
            P(None, None, "tp"),
            P(None, "tp"),
            P("tp", None),
            P(),
            P(),
            P(),
            P(None, None, "tp"),
            P(None, "tp"),
            P("tp", None),
            P(),
            P(),
        ),
        check_vma=False,
    )
```

time: 1050 us -> 416 us (0.40)
  waiting for transfers between devices: 601 us -> 0 us
  Pallas kernels: 0 us -> 325 us
  blocking collectives: 157 us -> 0 us
  matrix products: 142 us -> 13.9 us
  other arithmetic: 81.8 us -> 34.4 us
  between operations: 15.9 us -> 1.49 us
    psum x5 -> x0, waiting for transfers between devices: 553 us -> none  [the longest x1 154 us: on_device(): lax.psum((attend_lower_part, out_upper_grad, expand_lower_part, red_upper...]
    pallas_call x0 -> x5, Pallas kernels: none -> 325 us  [the longest x1 83.6 us: feed(): call(feed_kernel, (s((piece, width), F32), s((piece, width), BF16), s((X,...]
    psum x3 -> x0, blocking collectives: 157 us -> none  [the longest x2 80.1 us: on_device(): lax.psum((jnp.sum(joined_out * joined_out, axis=0), jnp.sum(joined_reduce...]
    dot_general x48 -> x34, matrix products: 142 us -> 13.9 us  [the longest x24 10.5 us: dot32(): return lax.dot_general(a, b, (dims, ((), ())), preferred_element_type=F32)]
    reduce_scatter x2 -> x0, waiting for transfers between devices: 48.2 us -> none  [the longest x1 36.3 us: on_device(): lax.psum_scatter(d_keys_all, 'ctx', scatter_dimension=1, tiled=True)]
    unnamed x255 -> x86, local copies, waits for them, and re-layouts: 38.3 us -> 8.85 us
    add x4 -> x2, other arithmetic: 25.9 us -> 0.22 us  [the longest x1 0.2 us: on_device(): through_three[:, :3 * rank] + through_three[:, 3 * rank:6 * rank]]
    reduce_sum x7 -> x5, other arithmetic: 25.6 us -> 2.75 us  [the longest x3 2.53 us: on_device(): mag = jnp.sum(grad.astype(F32) * flat_pre[:, m], axis=0)]
  transfers between devices with their start and end apart: 9 -> 0, of which waited for: 7 -> 0; matrix products, arithmetic and copies ran while one was open for 12% -> 0% of each run, Pallas kernels for 0% -> 0%
where the time goes in v1:
time: 416 us; the launch traced here: 410 us
  Pallas kernels  325 us (78%)
  local copies, waits for them, and re-layouts  35.2 us (8%)
  other arithmetic  34.4 us (8%)
  matrix products  13.9 us (3%)
    pallas_call x1, Pallas kernels, feed(): call(feed_kernel, (s((piece, width), F32), s((piece, width), BF16), s((X,...  83.6 us
    pallas_call x1, Pallas kernels, front(): call(front_kernel, (s((X, here, HD), BF16), s((rows, here, HD), F32), s((...  81.8 us
    pallas_call x1, Pallas kernels, input_grad(): call(input_grad_kernel, jax.ShapeDtypeStruct((rows, here, width), BF16),...  73.6 us
    pallas_call x1, Pallas kernels, sums(): call(sums_kernel, (jax.ShapeDtypeStruct((n, width), F32), jax.ShapeDtypeS...  43.9 us
    pallas_call x1, Pallas kernels, attend_back(): call(attend_back_kernel, (jax.ShapeDtypeStruct((rows, here, 3 * HD), BF16...  42.6 us
    dot_general x24, matrix products, dot32(): return lax.dot_general(a, b, (dims, ((), ())), preferred_element_type=F32)  10.5 us
    unnamed x86, local copies, waits for them, and re-layouts  8.85 us

profile of v1, /device:TPU:0, one launch (start us, length us, event | category | flops | bytes accessed | tf_op | source)
XLA Modules:
  0.0 410.4 jit_solution(15838693382025844074)
XLA Ops:
  0.6 1.3 broadcast_in_dim.71
  1.9 1.0 reduce-precision_convert_fusion.4
  3.1 1.5 copy.122.la_ref
  8.8 1.6 maximum_maximum_fusion.1
  11.2 1.2 copy-done.2
  12.5 2.5 pad_maximum_fusion.fw_ref
  20.1 3.5 multiply_sine_fusion
  23.6 1.0 copy.125.begin_ref
  25.3 81.8 %shard_map.317 = (bf16[4,256,128]{2,1,0:T(8,128)(2,1)}, f32[4,256,128]{2,1,0:T(8,128)}, f32[4,256,1]{2,1,0:T(8,128)}, bf16[8,4,256,256]{3,2,1,0:T(8,128)(2,1)}, ...) custom-call(bf16[4,256,2048]{2,1,0:T(8,128)(2,1)} %hid_ref.1, ...), custom_call_target="tpu_custom_call" | custom-call | flops 3221225472 | bytes 33554432 | tf_op jit(solution)/shard_map/pallas_call | solution.py:393
  107.1 1.7 constant_dynamic-slice_fusion
  110.2 1.3 fusion.21
  112.3 83.6 %shard_map.318 = (f32[64,2048]{1,0:T(8,128)}, bf16[64,2048]{1,0:T(8,128)(2,1)}, bf16[4,256,128]{2,1,0:T(8,128)(2,1)}, f32[80,2048]{1,0:T(8,128)}, f32[4,56,352]{2,1,0:T(8,128)}, /*index=5*/f32[4,16,128]{2,1,0:T(8,128)}) custom-call(bf16[4,256,128]{2,1,0:T(8,128)(2,1)} %get-tuple-element.44.mixed_ref, bf16[64,2048]{1,0:T(8,128)(2,1)} %fusion.64.hid_ref, ...), custom_call_target="tpu_custom_call" | custom-call | flops 8858370048 | bytes 33554432 | tf_op jit(solution)/shard_map/pallas_call | solution.py:627
  195.8 42.6 %shard_map.319 = (bf16[4,256,384]{2,1,0:T(8,128)(2,1)}, bf16[4,256,2048]{2,1,0:T(8,128)(2,1)}) custom-call(bf16[4,256,128]{2,1,0:T(8,128)(2,1)} %get-tuple-element.42.q_ref, bf16[8,4,256,256]{3,2,1,0:T(8,128)(2,1)} %get-tuple-element.43.kv_ref, bf16[4,256,128]{2,1,0:T(8,128)(2,1)} %get-tuple-element.48.dmix_ref, f32[4,256,128]{2,1,0:T(8,128)} %get-tuple-element.49.soft_ref, ...), custom_call_target="tpu_custom_call" | custom-call | flops 2684354560 | bytes 33554432 | tf_op jit(solution)/shard_map/pallas_call | solution.py:800
  238.4 73.6 %shard_map.320 = bf16[4,256,2048]{2,1,0:T(8,128)(2,1)} custom-call(bf16[4,256,384]{2,1,0:T(8,128)(2,1)} %get-tuple-element.53.grads_ref, bf16[2048,384]{1,0:T(8,128)(2,1)} %get-tuple-element.54.weight_ref, bf16[64,2048]{1,0:T(8,128)(2,1)} %fusion.64.hid_ref, f32[1,2048]{1,0:T(1,128)} %bitcast.314, f32[64,2048]{1,0:T(8,128)} %get-tuple-element.55.dres_ref), custom_call_target="tpu_custom_call" | custom-call | flops 1610612736 | bytes 16777216 | tf_op jit(solution)/shard_map/pallas_call | solution.py:929
  312.1 6.7 %convert_element_type.208 = f32[4,256,2048]{2,1,0:T(8,128)} convert(bf16[4,256,2048]{2,1,0:T(8,128)(2,1)} %shard_map.320) | non-fusion elementwise | flops 2097152 | bytes 12582912 | tf_op jit(solution)/shard_map/convert_element_type | solution.py:1222
  318.7 2.5 reshape.231
  321.2 2.3 fusion.182
  323.6 1.7 copy.127
  327.5 1.3 multiply_reduce_fusion.2
  328.8 1.8 copy.129
  330.6 1.1 multiply_reduce_fusion.1
  331.7 1.1 copy.130
  333.9 3.2 fusion.79
  341.1 1.3 maximum_maximum_fusion.all_ref
  345.0 2.4 concatenate.71.ctx_ref
  347.4 43.9 %shard_map.321 = (f32[192,2048]{1,0:T(8,128)}, f32[56,352]{1,0:T(8,128)}, f32[72,128]{1,0:T(8,128)}) custom-call(f32[192,2048]{1,0:T(8,128)} %maximum_maximum_fusion.all_ref, f32[4,56,352]{2,1,0:T(8,128)} %get-tuple-element.61.block_ref, f32[4,16,128]{2,1,0:T(8,128)} %get-tuple-element.62.lower_ref, f32[56,128]{1,0:T(8,128)} %concatenate.71.ctx_ref), custom_call_target="tpu_custom_call" | custom-call | flops 1048576 | bytes 4194304 | tf_op jit(solution)/shard_map/pallas_call | solution.py:1036
  391.2 1.9 slice_multiply_fusion
  393.1 1.3 slice.261
  394.5 1.3 slice.262
  397.4 1.5 fusion.11
  404.2 1.2 fusion.7
  405.4 4.8 %copy.145 = bf16[4,256,2048]{2,1,0:T(8,128)(2,1)} copy(bf16[4,256,2048]{2,1,0:T(8,128)(2,1)} %get-tuple-element.151) | data formatting | bytes 8388608
  (181 shorter events, 29.5 us)
Async XLA Ops:
  3.0 1.6 copy-start.18
  3.0 2.2 copy-start.3
  8.8 2.2 copy-start.11
  11.0 1.4 copy-start.2
  11.0 1.5 copy-start.5
  12.5 2.5 copy-start.28
  12.5 2.6 copy-start.24
  12.5 2.6 copy-start.26
  15.2 2.0 copy-start.36
  16.1 2.1 copy-start.31
  16.1 2.1 copy-start.32
  16.2 3.6 copy-start.29
  17.2 7.4 %copy-start.30 = (s32[4,2048]{1,0:T(4,128)S(1)}, s32[4,2048]{1,0:T(4,128)}, u32[]{:S(2)}) copy-start(s32[4,2048]{1,0:T(4,128)} %param.24) | copy-start | bytes 98308
  107.1 2.5 copy-start.39
  325.8 4.8 %copy-start.15 = (f32[1024,1,128]{2,1,0:T(1,128)S(1)}, f32[1024,1,128]{2,1,0:T(1,128)}, u32[]{:S(2)}) copy-start(f32[1024,1,128]{2,1,0:T(1,128)} %get-tuple-element.87) | copy-start | bytes 1572868
  326.7 6.1 %copy-start.14 = (f32[1024,1,128]{2,1,0:T(1,128)S(1)}, f32[1024,1,128]{2,1,0:T(1,128)}, u32[]{:S(2)}) copy-start(f32[1024,1,128]{2,1,0:T(1,128)} %get-tuple-element.88) | copy-start | bytes 1572868
  327.5 5.5 %copy-start.38 = (f32[3,128]{1,0:T(4,128)S(1)}, f32[3,128]{1,0:T(4,128)}, u32[]{:S(2)}) copy-start(f32[3,128]{1,0:T(4,128)} %maga_ref.1) | copy-start | bytes 4612
  327.5 5.5 %copy-start.40 = (f32[3,128]{1,0:T(4,128)S(1)}, f32[3,128]{1,0:T(4,128)}, u32[]{:S(2)}) copy-start(f32[3,128]{1,0:T(4,128)} %get-tuple-element.58) | copy-start | bytes 4612
  327.5 5.5 %copy-start.19 = (f32[3,16,128]{2,1,0:T(8,128)S(1)}, f32[3,16,128]{2,1,0:T(8,128)}, u32[]{:S(2)}) copy-start(f32[3,16,128]{2,1,0:T(8,128)} %param.32) | copy-start | bytes 73732
  333.9 3.3 copy-start.4
  333.9 3.6 copy-start.1
  337.7 2.2 copy-start
  340.9 1.5 copy-start.13
  344.9 50.8 %copy-start.33 = (f32[2048]{0:T(1024)S(1)}, f32[2048]{0:T(1024)}, u32[]{:S(2)}) copy-start(f32[2048]{0:T(1024)} %param.36) | copy-start | bytes 24580
  344.9 50.8 %copy-start.35 = (f32[2,2048]{1,0:T(2,128)S(1)}, f32[2,2048]{1,0:T(2,128)}, u32[]{:S(2)}) copy-start(f32[2,2048]{1,0:T(2,128)} %get-tuple-element.47.sq_ref) | copy-start | bytes 49156
  344.9 51.7 %copy-start.6 = (bf16[128,2048]{1,0:T(8,128)(2,1)S(1)}, bf16[128,2048]{1,0:T(8,128)(2,1)}, u32[]{:S(2)}) copy-start(bf16[128,2048]{1,0:T(8,128)(2,1)} %param.28) | copy-start | bytes 1572868
  344.9 51.7 %copy-start.10 = (f32[16,2048]{1,0:T(8,128)S(1)}, f32[16,2048]{1,0:T(8,128)}, u32[]{:S(2)}) copy-start(f32[16,2048]{1,0:T(8,128)} %param.35) | copy-start | bytes 393220
  391.2 7.7 %copy-start.20 = (f32[192,2048]{1,0:T(8,128)S(1)}, f32[192,2048]{1,0:T(8,128)}, u32[]{:S(2)}) copy-start(f32[192,2048]{1,0:T(8,128)} %get-tuple-element.65) | copy-start | bytes 4718596
  396.6 4.4 %copy-start.17 = (f32[704,128]{1,0:T(8,128)S(1)}, f32[704,128]{1,0:T(8,128)}, u32[]{:S(2)}) copy-start(f32[704,128]{1,0:T(8,128)} %get-tuple-element.69) | copy-start | bytes 1081348
  400.3 1.2 copy-start.22
  401.1 2.2 copy-start.8
  401.1 2.4 copy-start.25
  (9 other events, 9.1 us)

commit v2 on v1

--- a/solution.py
+++ b/solution.py
@@ -35,11 +35,6 @@
 def exact_dot(bf, full, dims):
     high, low = halves(full)
     return dot32(bf, high, dims) + dot32(bf, low, dims)
-
-
-def exact_dot_left(full, bf, dims):
-    high, low = halves(full)
-    return dot32(high, bf, dims) + dot32(low, bf, dims)
 
 
 def rotate(tensor, cosine, sine_part):
@@ -826,69 +821,176 @@
     )(queries, kv, dmix, soft, log, begin, tag, cosine, sine, block)
 
 
-def input_grad_kernel(
-    grads_ref, weight_ref, hid_ref, gain_ref, dres_ref,
-    grad_out,
-    rel, send_l, send_r, recv_l, recv_r, acc_l, acc_r, send_2, recv_2, d_one, spread,
-    s_one, r_one, s_two, r_two, s_gat, r_gat, local,
+def tail_kernel(
+    grads_ref, weight_ref, hid_ref, gain_ref, dres_ref, pre_ref, thr_ref, n1_ref, inner_ref,
+    cola_ref, maga_ref, uppera_ref, early_ref, both_ref, block_ref, lower_ref,
+    grad_out, all_out, block_out, ctx_out,
+    rel, two, near, held, hop, came, acc, send_2, recv_2, d_one, spread, n1, down, all_s,
+    c_r, z_s, z_r, x_s, x_r, y_s, y_r, bx_r, lx_r, b_one, b_two, e_one, e_two, e_z, b_z,
+    s_one, r_one, s_two, r_two, s_gat, r_gat, ss, rs, local,
 ):
     z, core, y, x = place()
     rows, here, deep = grads_ref.shape
     piece, width = hid_ref.shape
     half = width // 2
+    mid = here // 2
+    n = all_s.shape[0]
+    nc, nz = n // 2, n // 2 // Z
+    wx, wy = width // X, width // X // Y
+    rank = 16
+    load = keep(n1_ref, n1, local.at[0])
     for i in range(X):
         for j in range(Y):
             rel[i, j] = grads_ref[
                 (x + i) % X, pl.ds(pl.multiple_of(((y + j) % Y) * piece, piece), piece)
             ]
-    greet([device(dx=d) for d in (1, 2, 3)] + [device(dy=d) for d in (1, 2, 3)])
-    one = []
-    for d in (2, 1, 3, 0):
-        lhs_l = rel[d].reshape(here, deep)
-        lhs_r = jnp.concatenate([rel[i, d] for i in range(X)], axis=0)
+    greet(
+        [device(dx=d) for d in (1, 2, 3)]
+        + [device(dy=d) for d in (1, 2, 3)]
+        + [device(dz=d) for d in (1, 2, 3)]
+        + [device(dc=1)]
+    )
+
+    def to(k, d):
+        return device(dy=d) if k else device(dx=d)
+
+    def ds(index, size):
+        return pl.ds(pl.multiple_of(index * size, size), size)
+
+    def done(copies):
+        for copy in copies:
+            copy.wait()
+
+    def term(k, d, begin, size):
+        if k:
+            lhs = jnp.concatenate([rel[i, d] for i in range(X)], axis=0)
+        else:
+            lhs = rel[d].reshape(here, deep)
+        return dot32(lhs, weight_ref[k * half + begin : k * half + begin + size], ((1,), (1,)))
+
+    one = {}
+    for k in range(2):
         for start, size in tiles(half, 512):
-            at = slice(start, start + size)
-            part = dot32(lhs_l, weight_ref[at], ((1,), (1,)))
-            if d:
-                send_l[d - 1, :, at] = part.astype(BF16)
-            else:
-                acc_l[:, at] = part
-        if d:
-            one.append(
-                send(send_l.at[d - 1], recv_l.at[d - 1], s_one.at[0, d - 1], r_one.at[0, d - 1],
-                     device(dx=d))
-            )
+            two[k, :, start : start + size] = term(k, 2, start, size).astype(BF16)
+        one[k, 0] = send(
+            two.at[k, pl.ds(0, mid)], hop.at[k, 0], s_one.at[k, 0], r_one.at[k, 0], to(k, 1)
+        )
+        one[k, 1] = send(
+            two.at[k, pl.ds(mid, mid)], hop.at[k, 1], s_one.at[k, 1], r_one.at[k, 1], to(k, 3)
+        )
+    for k in range(2):
+        for side, d in enumerate((1, 3)):
+            plain = mid if side == 0 else 0
+            other = mid - plain
+            for start, size in tiles(half, 512):
+                at = slice(start, start + size)
+                part = term(k, d, start, size)
+                near[k, side, plain : plain + mid, at] = part[plain : plain + mid].astype(BF16)
+                held[k, side, :, at] = part[other : other + mid]
+            one[k, 2 + side] = send(
+                near.at[k, side, pl.ds(plain, mid)], came.at[k, side, pl.ds(plain, mid)],
+                s_one.at[k, 2 + side], r_one.at[k, 2 + side], to(k, d),
+            )
+    for k in range(2):
         for start, size in tiles(half, 512):
-            at = slice(start, start + size)
-            part = dot32(lhs_r, weight_ref[half + start : half + start + size], ((1,), (1,)))
-            if d:
-                send_r[d - 1, :, at] = part.astype(BF16)
-            else:
-                acc_r[:, at] = part
-        if d:
-            one.append(
-                send(send_r.at[d - 1], recv_r.at[d - 1], s_one.at[1, d - 1], r_one.at[1, d - 1],
-                     device(dy=d))
-            )
-    for copy in one:
-        copy.wait()
-    two = []
-    for k, (acc, recv) in enumerate(((acc_l, recv_l), (acc_r, recv_r))):
+            acc[k, :, start : start + size] = term(k, 0, start, size)
+
+    for m in range(3):
+        at = slice(m * HD, (m + 1) * HD)
+        grad = grads_ref[:, :, at].reshape(rows * here, HD)
+        before = pre_ref[:, :, at].reshape(rows * here, HD)
+        column, magnitude = cola_ref[m : m + 1], maga_ref[m : m + 1]
+        ratio = magnitude / column
+        mag = jnp.sum(grad.astype(F32) * before, axis=0, keepdims=True) / magnitude
+        pull = magnitude * mag / (column * column)
+        thin = thr_ref[:, :, m * rank : (m + 1) * rank] + thr_ref[
+            :, :, (3 + m) * rank : (4 + m) * rank
+        ]
+        thin = thin.reshape(rows * here, rank).astype(BF16)
+        part = dot32(thin, grad, ((0,), (0,)))
+        e_one[(1 + m) * rank : (2 + m) * rank] = adapter_scale * (
+            part * ratio - inner_ref[m] * pull
+        )
+        e_one[4 * rank + m : 4 * rank + m + 1] = mag
+        upper = uppera_ref[m]
+        down[:, m * rank : (m + 1) * rank] = dot32(
+            grad, (upper * ratio).astype(BF16), ((1,), (1,))
+        ).astype(BF16)
+        pulled = (upper * (mag / column)).astype(BF16)
+        for start, size in tiles(width, 512):
+            all_s[(7 + m) * rank : (8 + m) * rank, start : start + size] = dot32(
+                pulled, weight_ref[start : start + size, at], ((1,), (1,))
+            )
+    e_one[4 * rank + 3 :] = jnp.zeros((e_one.shape[0] - 4 * rank - 3, HD), F32)
+    load.wait()
+    for start, size in tiles(width, 512):
+        at = slice(start, start + size)
+        value = dot32(
+            down[...], n1[:, :, at].reshape(rows * here, size), ((0,), (0,))
+        )
+        all_s[7 * rank : 10 * rank, at] = value - all_s[7 * rank : 10 * rank, at]
+    all_s[0 : 5 * rank] = early_ref[...]
+    all_s[5 * rank : 7 * rank] = both_ref[...] * (1.0 / (2 * Z))
+    all_s[10 * rank :] = jnp.zeros((n - 10 * rank, width), F32)
+
+    def go(k, d, src, dst, where):
+        return send(src, dst, ss.at[k, d], rs.at[k, d], where)
+
+    first = [go(0, 0, all_s.at[ds(1 - core, nc)], c_r, device(dc=1))]
+    slots = []
+    for d in NEAR_LAST:
+        slots.append(go(1, d, block_ref.at[X - d], bx_r.at[d - 1], device(dx=d)))
+        slots.append(go(2, d, lower_ref.at[X - d], lx_r.at[d - 1], device(dx=d)))
+    for k in range(2):
+        for side, d in enumerate((1, 3)):
+            one[k, side].wait_recv()
+            other = 0 if side == 0 else mid
+            near[k, side, other : other + mid] = (
+                held[k, side] + hop[k, side].astype(F32)
+            ).astype(BF16)
+            one[k, 4 + side] = send(
+                near.at[k, side, pl.ds(other, mid)], came.at[k, side, pl.ds(other, mid)],
+                s_one.at[k, 4 + side], r_one.at[k, 4 + side], to(k, d),
+            )
+    done(first)
+    z_s[...] = all_s[ds(core, nc)] + c_r[...]
+    zc = [go(3, d, z_s.at[ds((z + d) % Z, nz)], z_r.at[d - 1], device(dz=d)) for d in NEAR_LAST]
+    done(slots)
+    b_one[...] = block_ref[0] + (bx_r[0] + bx_r[1] + bx_r[2])
+    e_one[:rank] = lower_ref[0] + (lx_r[0] + lx_r[1] + lx_r[2])
+    cc = [go(4, 0, b_one, b_two, device(dc=1)), go(5, 0, e_one, e_two, device(dc=1))]
+    for index in range(2):
+        for k in range(2):
+            one[k, index].wait_send()
+    for k in range(2):
+        for index in (2, 3, 4, 5):
+            one[k, index].wait()
+    seconds = []
+    for k in range(2):
         for d in (2, 1, 3, 0):
             at = slice(d * piece, (d + 1) * piece)
-            part = acc[at] + (
-                recv[0, at].astype(F32) + recv[1, at].astype(F32) + recv[2, at].astype(F32)
-            )
+            part = acc[k, at] + (came[k, 0, at].astype(F32) + came[k, 1, at].astype(F32))
             if d:
                 send_2[k, d - 1] = part.astype(BF16)
-                two.append(
-                    send(send_2.at[k, d - 1], recv_2.at[k, d - 1], s_two.at[k, d - 1],
-                         r_two.at[k, d - 1], device(dx=d) if k else device(dy=d))
+                seconds.append(
+                    send(
+                        send_2.at[k, d - 1], recv_2.at[k, d - 1], s_two.at[k, d - 1],
+                        r_two.at[k, d - 1], to(1 - k, d),
+                    )
                 )
             else:
                 d_one[:, k * half : (k + 1) * half] = part
-    for copy in two:
-        copy.wait()
+    done(cc)
+    b_two[...] += b_one[...]
+    e_two[...] += e_one[...]
+    done(zc)
+    x_s[...] = z_s[ds(z, nz)] + (z_r[0] + z_r[1] + z_r[2])
+    cz = []
+    for d in NEAR_LAST:
+        cz.append(go(6, d, b_two, b_z.at[d - 1], device(dz=d)))
+        cz.append(go(7, d, e_two, e_z.at[d - 1], device(dz=d)))
+    xc = [go(8, d, x_s.at[:, ds((x + d) % X, wx)], x_r.at[d - 1], device(dx=d)) for d in NEAR_LAST]
+    done(seconds)
     for k in range(2):
         d_one[:, k * half : (k + 1) * half] += (
             recv_2[k, 0].astype(F32) + recv_2[k, 1].astype(F32) + recv_2[k, 2].astype(F32)
@@ -900,171 +1002,127 @@
         inverse * scaled
         - inputs * (inverse * inverse * inverse) * jnp.mean(inputs * scaled, axis=1, keepdims=True)
     )
-    tokens = pl.ds(pl.multiple_of(y * piece, piece), piece)
+    tokens = ds(y, piece)
     left, right = pl.ds(0, half), pl.ds(half, half)
     spread[x, tokens] = result.astype(BF16)
     gat = []
     for d in NEAR_LAST:
-        for k, (cut, to) in enumerate(((left, device(dx=d)), (right, device(dy=d)))):
+        for k, cut in enumerate((left, right)):
             at = spread.at[x, tokens, cut]
-            gat.append(send(at, at, s_gat.at[k, d - 1], r_gat.at[k, d - 1], to))
-    for copy in gat:
-        copy.wait()
-    gat = []
-    for d in NEAR_LAST:
-        at = spread.at[:, tokens, left]
-        gat.append(send(at, at, s_gat.at[2, d - 1], r_gat.at[2, d - 1], device(dy=d)))
-        at = spread.at[x, :, right]
-        gat.append(send(at, at, s_gat.at[3, d - 1], r_gat.at[3, d - 1], device(dx=d)))
-    for copy in gat:
-        copy.wait()
-    out = keep(spread, grad_out, local.at[0])
+            gat.append(send(at, at, s_gat.at[k, d - 1], r_gat.at[k, d - 1], to(k, d)))
+    done(xc)
+    y_s[...] = x_s[:, ds(x, wx)] + (x_r[0] + x_r[1] + x_r[2])
+    yc = [go(9, d, y_s.at[:, ds((y + d) % Y, wy)], y_r.at[d - 1], device(dy=d)) for d in NEAR_LAST]
+    done(gat)
+
+    def block_of(k, d):
+        if k:
+            return spread.at[(x + d) % X, :, right]
+        return spread.at[:, ds((y + d) % Y, piece), left]
+
+    def part_of(k, d, second):
+        if k:
+            return spread.at[(x + d) % X, pl.ds(second * mid, mid), right]
+        return spread.at[pl.ds(second * 2, 2), ds((y + d) % Y, piece), left]
+
+    last = {}
+    for k in range(2):
+        for side, d in enumerate((1, 3)):
+            last[k, side] = send(
+                block_of(k, 0), block_of(k, 0), s_gat.at[2 + k, side], r_gat.at[2 + k, side],
+                to(1 - k, d),
+            )
+    mine = ds(core * Z + z, nz)
+    done(yc)
+    all_out[mine, ds(x * Y + y, wy)] = y_s[:, ds(y, wy)] + (y_r[0] + y_r[1] + y_r[2])
+    spot = all_out.at[mine, ds(x * Y + y, wy)]
+    done([go(10, d, spot, spot, device(dy=d)) for d in NEAR_LAST])
+    spot = all_out.at[mine, ds(x, wx)]
+    sx = [go(11, d, spot, spot, device(dx=d)) for d in NEAR_LAST]
+    for k in range(2):
+        for side, d in enumerate((1, 3)):
+            last[k, side].wait_recv()
+            at = part_of(k, -d % 4, side)
+            last[k, 2 + side] = send(
+                at, at, s_gat.at[4 + k, side], r_gat.at[4 + k, side], to(1 - k, d)
+            )
+    done(sx)
+    spot = all_out.at[mine]
+    done([go(12, d, spot, spot, device(dz=d)) for d in NEAR_LAST])
+    spot = all_out.at[ds(core, nc)]
+    sc = [go(13, 0, spot, spot, device(dc=1))]
+    done(cz)
+    block_out[...] = b_two[...] + (b_z[0] + b_z[1] + b_z[2])
+    ctx_out[...] = e_two[...] + (e_z[0] + e_z[1] + e_z[2])
+    for k in range(2):
+        for side in range(2):
+            last[k, side].wait_send()
+            last[k, 2 + side].wait()
+    out = keep(spread, grad_out, local.at[1])
+    done(sc)
     out.wait()
 
 
-def input_grad(grads, weight, hid_own, gain, d_resid):
+def tail(
+    grads, weight, hid_own, gain, d_resid, pre, thr, n1, inner, cola, maga, uppera, early, both,
+    block, lower,
+):
     rows, here, deep = grads.shape
     piece, width = hid_own.shape
     half = width // 2
+    mid = here // 2
+    _, bn, bw = block.shape
+    n = 192
+    en = 72
+    nc, nz = n // 2, n // 2 // Z
+    wx, wy = width // X, width // X // Y
+    s = jax.ShapeDtypeStruct
+    v = pltpu.VMEM
     return call(
-        input_grad_kernel,
-        jax.ShapeDtypeStruct((rows, here, width), BF16),
-        [VM] * 5,
-        ANY,
+        tail_kernel,
+        (s((rows, here, width), BF16), s((n, width), F32), s((bn, bw), F32), s((en, HD), F32)),
+        [VM] * 7 + [ANY] + [VM] * 8,
+        (ANY, VM, VM, VM),
         [
-            pltpu.VMEM((X, Y, piece, deep), BF16),
-            pltpu.VMEM((3, here, half), BF16),
-            pltpu.VMEM((3, here, half), BF16),
-            pltpu.VMEM((3, here, half), BF16),
-            pltpu.VMEM((3, here, half), BF16),
-            pltpu.VMEM((here, half), F32),
-            pltpu.VMEM((here, half), F32),
-            pltpu.VMEM((2, 3, piece, half), BF16),
-            pltpu.VMEM((2, 3, piece, half), BF16),
-            pltpu.VMEM((piece, width), F32),
-            pltpu.VMEM((rows, here, width), BF16),
-            dma(2, 3), dma(2, 3), dma(2, 3), dma(2, 3), dma(4, 3), dma(4, 3), dma(1),
+            v((X, Y, piece, deep), BF16),
+            v((2, here, half), BF16),
+            v((2, 2, here, half), BF16),
+            v((2, 2, mid, half), F32),
+            v((2, 2, mid, half), BF16),
+            v((2, 2, here, half), BF16),
+            v((2, here, half), F32),
+            v((2, 3, piece, half), BF16),
+            v((2, 3, piece, half), BF16),
+            v((piece, width), F32),
+            v((rows, here, width), BF16),
+            v((rows, here, width), BF16),
+            v((rows * here, 48), BF16),
+            v((n, width), F32),
+            v((nc, width), F32),
+            v((nc, width), F32),
+            v((3, nz, width), F32),
+            v((nz, width), F32),
+            v((3, nz, wx), F32),
+            v((nz, wx), F32),
+            v((3, nz, wy), F32),
+            v((3, bn, bw), F32),
+            v((3, 16, HD), F32),
+            v((bn, bw), F32),
+            v((bn, bw), F32),
+            v((en, HD), F32),
+            v((en, HD), F32),
+            v((3, en, HD), F32),
+            v((3, bn, bw), F32),
+            dma(2, 6), dma(2, 6), dma(2, 3), dma(2, 3), dma(6, 3), dma(6, 3),
+            dma(14, 4), dma(14, 4), dma(2),
         ],
         3,
         2 * rows * here * deep * width,
         16 * 2**20,
-    )(grads, weight, hid_own, gain, d_resid)
-
-
-def sums_kernel(
-    all_ref, block_ref, lower_ref, ctx_ref,
-    all_out, block_out, ctx_out,
-    c_r, z_s, z_r, x_s, x_r, y_s, y_r, gath, bx_r, lx_r, b_one, b_two, e_one, e_two, e_z, b_z,
-    ss, rs,
-):
-    z, core, y, x = place()
-    n, width = all_ref.shape
-    nc, nz = n // 2, n // 2 // Z
-    wx, wy = width // X, width // X // Y
-    rank = lower_ref.shape[1]
-    greet(
-        [device(dx=d) for d in (1, 2, 3)]
-        + [device(dy=d) for d in (1, 2, 3)]
-        + [device(dz=d) for d in (1, 2, 3)]
-        + [device(dc=1)]
-    )
-
-    def go(k, d, src, dst, to):
-        return send(src, dst, ss.at[k, d], rs.at[k, d], to)
-
-    def ds(index, size):
-        return pl.ds(pl.multiple_of(index * size, size), size)
-
-    def done(copies):
-        for copy in copies:
-            copy.wait()
-
-    first = [go(0, 0, all_ref.at[ds(1 - core, nc)], c_r, device(dc=1))]
-    slots = []
-    for d in NEAR_LAST:
-        slots.append(go(1, d, block_ref.at[X - d], bx_r.at[d - 1], device(dx=d)))
-        slots.append(go(2, d, lower_ref.at[X - d], lx_r.at[d - 1], device(dx=d)))
-    done(first)
-    z_s[...] = all_ref[ds(core, nc)] + c_r[...]
-    zc = [go(3, d, z_s.at[ds((z + d) % Z, nz)], z_r.at[d - 1], device(dz=d)) for d in NEAR_LAST]
-    done(slots)
-    b_one[...] = block_ref[0] + (bx_r[0] + bx_r[1] + bx_r[2])
-    e_one[:rank] = lower_ref[0] + (lx_r[0] + lx_r[1] + lx_r[2])
-    e_one[rank:] = ctx_ref[...]
-    cc = [
-        go(4, 0, b_one, b_two, device(dc=1)),
-        go(5, 0, e_one, e_two, device(dc=1)),
-    ]
-    done(cc)
-    b_two[...] += b_one[...]
-    e_two[...] += e_one[...]
-    cz = []
-    for d in NEAR_LAST:
-        cz.append(go(6, d, b_two, b_z.at[d - 1], device(dz=d)))
-        cz.append(go(7, d, e_two, e_z.at[d - 1], device(dz=d)))
-    done(zc)
-    x_s[...] = z_s[ds(z, nz)] + (z_r[0] + z_r[1] + z_r[2])
-    xc = [go(8, d, x_s.at[:, ds((x + d) % X, wx)], x_r.at[d - 1], device(dx=d)) for d in NEAR_LAST]
-    done(xc)
-    y_s[...] = x_s[:, ds(x, wx)] + (x_r[0] + x_r[1] + x_r[2])
-    yc = [go(9, d, y_s.at[:, ds((y + d) % Y, wy)], y_r.at[d - 1], device(dy=d)) for d in NEAR_LAST]
-    done(yc)
-    mine = ds(core * Z + z, nz)
-    at_y = x * Y + y
-    gath[mine, ds(at_y, wy)] = y_s[:, ds(y, wy)] + (y_r[0] + y_r[1] + y_r[2])
-    spot = gath.at[mine, ds(at_y, wy)]
-    done([go(10, d, spot, spot, device(dy=d)) for d in NEAR_LAST])
-    spot = gath.at[mine, ds(x, wx)]
-    done([go(11, d, spot, spot, device(dx=d)) for d in NEAR_LAST])
-    spot = gath.at[mine]
-    done([go(12, d, spot, spot, device(dz=d)) for d in NEAR_LAST])
-    spot = gath.at[ds(core, nc)]
-    done([go(13, 0, spot, spot, device(dc=1))])
-    all_out[...] = gath[...]
-    done(cz)
-    block_out[...] = b_two[...] + (b_z[0] + b_z[1] + b_z[2])
-    ctx_out[...] = e_two[...] + (e_z[0] + e_z[1] + e_z[2])
-
-
-def sums(everywhere, block, lower, local):
-    n, width = everywhere.shape
-    _, bn, bw = block.shape
-    rank = lower.shape[1]
-    en = local.shape[0] + rank
-    nc, nz = n // 2, n // 2 // Z
-    wx, wy = width // X, width // X // Y
-    return call(
-        sums_kernel,
-        (
-            jax.ShapeDtypeStruct((n, width), F32),
-            jax.ShapeDtypeStruct((bn, bw), F32),
-            jax.ShapeDtypeStruct((en, HD), F32),
-        ),
-        [VM] * 4,
-        (VM,) * 3,
-        [
-            pltpu.VMEM((nc, width), F32),
-            pltpu.VMEM((nc, width), F32),
-            pltpu.VMEM((3, nz, width), F32),
-            pltpu.VMEM((nz, width), F32),
-            pltpu.VMEM((3, nz, wx), F32),
-            pltpu.VMEM((nz, wx), F32),
-            pltpu.VMEM((3, nz, wy), F32),
-            pltpu.VMEM((n, width), F32),
-            pltpu.VMEM((3, bn, bw), F32),
-            pltpu.VMEM((3, rank, HD), F32),
-            pltpu.VMEM((bn, bw), F32),
-            pltpu.VMEM((bn, bw), F32),
-            pltpu.VMEM((en, HD), F32),
-            pltpu.VMEM((en, HD), F32),
-            pltpu.VMEM((3, en, HD), F32),
-            pltpu.VMEM((3, bn, bw), F32),
-            dma(14, 4), dma(14, 4),
-        ],
-        4,
-        2**20,
-        2**22,
-    )(everywhere, block, lower, local)
+    )(
+        grads, weight, hid_own, gain, d_resid, pre, thr, n1, inner, cola, maga, uppera, early, both,
+        block, lower,
+    )
 
 
 def on_device(
@@ -1094,14 +1152,12 @@
     rows, here, width = hidden.shape
     length = segments.shape[1]
     ff = reduce_frozen.shape[0]
-    flat = rows * here
     piece = here // Y
     rank = output_lower.shape[1]
     ctx = lax.axis_index("ctx")
     tp = lax.axis_index("tp")
     y, x = tp // X, tp % X
     offset = ctx * here
-    share = 1.0 / (2 * Z)
 
     def left_factor(a):
         high, low = halves(a)
@@ -1218,50 +1274,25 @@
         sine_part,
         block_own,
     )
-    hidden_grad = input_grad(grads_low, weight_attend, hid_own, gain_one[None], d_resid)
-    hidden_grad = hidden_grad.astype(F32)
-    pre = pre.reshape(flat, 3 * HD)
-    through_three = through_three.reshape(flat, HD)
-    normed_one = normed_one.reshape(flat, width)
-
-    late = []
-    local = []
-    mags = []
-    through_three = through_three[:, : 3 * rank] + through_three[:, 3 * rank : 6 * rank]
-    flat_grads = grads_low.reshape(flat, 3, HD)
-    flat_pre = pre.reshape(flat, 3, HD)
-    downs = []
-    for m in range(3):
-        grad = flat_grads[:, m]
-        ratio = attend_magnitude[m] / column_attend[m]
-        mag = jnp.sum(grad.astype(F32) * flat_pre[:, m], axis=0)
-        mags.append(mag / attend_magnitude[m])
-        pull = attend_magnitude[m] * (mags[m] * column_attend[m]) / column_attend[m] ** 3
-        upper_part = exact_dot_left(
-            through_three[:, m * rank : (m + 1) * rank], grad, ((0,), (0,))
-        )
-        local.append(adapter_scale * (upper_part * ratio - inner_attend[m] * pull))
-        downs.append(exact_dot(grad, attend_upper[m] * ratio, ((1,), (1,))))
-        pulled = attend_upper[m] * pull
-        outer = exact_dot_left(pulled, attend_frozen[m], ((1,), (1,)))
-        outer = outer + adapter_scale * jnp.dot(
-            jnp.dot(pulled, attend_upper[m].T, precision=lax.Precision.HIGHEST),
-            attend_lower[m].T,
-            precision=lax.Precision.HIGHEST,
-        )
-        late.append(outer)
-    late = exact_dot_left(jnp.concatenate(downs, axis=1), normed_one, ((0,), (0,))) - (
-        jnp.concatenate(late, axis=0)
-    )
-    local = jnp.concatenate(local + [jnp.stack(mags), jnp.zeros((5, HD), F32)], axis=0)
-    everywhere, block_x, small_ctx = sums(
-        jnp.concatenate(
-            [early, inner_both * share, late, jnp.zeros((32, width), F32)], axis=0
-        ),
+    hidden_grad, everywhere, block_x, small_ctx = tail(
+        grads_low,
+        weight_attend,
+        hid_own,
+        gain_one[None],
+        d_resid,
+        pre,
+        through_three,
+        normed_one,
+        inner_attend,
+        column_attend,
+        attend_magnitude,
+        attend_upper,
+        early,
+        inner_both,
         block_x,
         lower_out,
-        local,
-    )
+    )
+    hidden_grad = hidden_grad.astype(F32)
     lower_out, local = small_ctx[:rank], small_ctx[rank:]
     late = adapter_scale * everywhere[7 * rank : 10 * rank]
     early = everywhere[: 7 * rank]

time: 416 us -> 343 us (0.82)
  Pallas kernels: 325 us -> 285 us
  local copies, waits for them, and re-layouts: 35.2 us -> 18.9 us
  matrix products: 13.9 us -> 3.68 us
  other arithmetic: 34.4 us -> 28.5 us
    pallas_call x2 -> x1, Pallas kernels: 117 us -> 77.4 us  [tail(): call(tail_kernel, (s((rows, here, width), BF16), s((n, width), F32), s((b...]
    dot_general x24 -> x4, matrix products: 10.5 us -> 2.16 us  [dot32(): return lax.dot_general(a, b, (dims, ((), ())), preferred_element_type=F32)]
    slice x5 -> x0, local copies, waits for them, and re-layouts: 6.92 us -> none  [the longest x4 4.58 us: on_device(): grad = flat_grads[:, m]]
    unnamed x86 -> x52, local copies, waits for them, and re-layouts: 8.85 us -> 8.16 us
where the time goes in v2:
time: 343 us; the launch traced here: 338 us
  Pallas kernels  285 us (83%)
  other arithmetic  28.5 us (8%)
  local copies, waits for them, and re-layouts  18.9 us (6%)
  matrix products  3.68 us (1%)
    pallas_call x1, Pallas kernels, feed(): call(feed_kernel, (s((piece, width), F32), s((piece, width), BF16), s((X,...  83.5 us
    pallas_call x1, Pallas kernels, front(): call(front_kernel, (s((X, here, HD), BF16), s((rows, here, HD), F32), s((...  81.8 us
    pallas_call x1, Pallas kernels, tail(): call(tail_kernel, (s((rows, here, width), BF16), s((n, width), F32), s((b...  77.4 us
    pallas_call x1, Pallas kernels, attend_back(): call(attend_back_kernel, (jax.ShapeDtypeStruct((rows, here, 3 * HD), BF16...  42.7 us
    unnamed x52, local copies, waits for them, and re-layouts  8.16 us

profile of v2, /device:TPU:0, one launch (start us, length us, event | category | flops | bytes accessed | tf_op | source)
XLA Modules:
  0.0 337.8 jit_solution(10629554417299149310)
XLA Ops:
  0.6 1.3 broadcast_in_dim.51
  1.9 1.0 reduce-precision_convert_fusion.1
  3.1 1.5 copy.95.la_ref
  5.9 0.9 fusion.42
  7.9 0.9 copy-done.7
  8.8 1.6 maximum_maximum_fusion
  11.2 1.2 copy-done
  12.5 2.5 pad_maximum_fusion.fw_ref
  15.2 0.9 copy.96.aw_ref
  16.2 1.0 pad_maximum_fusion.1.bw_ref
  17.2 1.0 reshape.107.mage_ref
  18.2 0.6 pad_maximum_fusion.9.mago_ref
  19.0 0.7 select_maximum_fusion.small_ref
  20.1 3.6 %multiply_sine_fusion = (f32[4,256,128]{2,1,0:T(8,128)}, f32[4,256,128]{2,1,0:T(8,128)}) fusion(f32[128]{0:T(128)S(1)} %pad_maximum_fusion.10, f32[4,256]{1,0:T(4,128)S(1)} %get-tuple-element.115), kind=kLoop, calls=%fused_computation.23 | loop fusion | flops 131072 | bytes 1053184 | tf_op jit(solution)/shard_map/sin | solution.py:1211
  23.7 1.0 copy.98.begin_ref
  24.7 0.6 broadcast_in_dim.48.tag_ref
  25.4 81.8 %shard_map.317 = (bf16[4,256,128]{2,1,0:T(8,128)(2,1)}, f32[4,256,128]{2,1,0:T(8,128)}, f32[4,256,1]{2,1,0:T(8,128)}, bf16[8,4,256,256]{3,2,1,0:T(8,128)(2,1)}, ...) custom-call(bf16[4,256,2048]{2,1,0:T(8,128)(2,1)} %hid_ref.1, ...), custom_call_target="tpu_custom_call" | custom-call | flops 3221225472 | bytes 33554432 | tf_op jit(solution)/shard_map/pallas_call | solution.py:388
  107.2 1.7 constant_dynamic-slice_fusion
  108.9 0.8 fusion.12.hid_ref
  110.3 1.3 fusion.8
  111.7 0.7 pad_maximum_fusion.4.upper_ref
  112.4 83.5 %shard_map.318 = (f32[64,2048]{1,0:T(8,128)}, bf16[64,2048]{1,0:T(8,128)(2,1)}, bf16[4,256,128]{2,1,0:T(8,128)(2,1)}, f32[80,2048]{1,0:T(8,128)}, f32[4,56,352]{2,1,0:T(8,128)}, /*index=5*/f32[4,16,128]{2,1,0:T(8,128)}) custom-call(bf16[4,256,128]{2,1,0:T(8,128)(2,1)} %get-tuple-element.45.mixed_ref, bf16[64,2048]{1,0:T(8,128)(2,1)} %fusion.12.hid_ref, ...), custom_call_target="tpu_custom_call" | custom-call | flops 8858370048 | bytes 33554432 | tf_op jit(solution)/shard_map/pallas_call | solution.py:622
  195.9 42.7 %shard_map.319 = (bf16[4,256,384]{2,1,0:T(8,128)(2,1)}, bf16[4,256,2048]{2,1,0:T(8,128)(2,1)}) custom-call(bf16[4,256,128]{2,1,0:T(8,128)(2,1)} %get-tuple-element.43.q_ref, bf16[8,4,256,256]{3,2,1,0:T(8,128)(2,1)} %get-tuple-element.44.kv_ref, bf16[4,256,128]{2,1,0:T(8,128)(2,1)} %get-tuple-element.49.dmix_ref, f32[4,256,128]{2,1,0:T(8,128)} %get-tuple-element.50.soft_ref, ...), custom_call_target="tpu_custom_call" | custom-call | flops 2684354560 | bytes 33554432 | tf_op jit(solution)/shard_map/pallas_call | solution.py:795
  238.6 77.4 %shard_map.320 = (bf16[4,256,2048]{2,1,0:T(8,128)(2,1)}, f32[192,2048]{1,0:T(8,128)}, f32[56,352]{1,0:T(8,128)}, f32[72,128]{1,0:T(8,128)}) custom-call(bf16[4,256,384]{2,1,0:T(8,128)(2,1)} %get-tuple-element.54.grads_ref, bf16[2048,384]{1,0:T(8,128)(2,1)} %get-tuple-element.55.weight_ref, bf16[64,2048]{1,0:T(8,128)(2,1)} %fusion.12.hid_ref, ...), custom_call_target="tpu_custom_call" | custom-call | flops 1610612736 | bytes 16777216 | tf_op jit(solution)/shard_map/pallas_call | solution.py:1081
  316.0 6.8 %convert_element_type.103 = f32[4,256,2048]{2,1,0:T(8,128)} convert(bf16[4,256,2048]{2,1,0:T(8,128)(2,1)} %get-tuple-element.66) | non-fusion elementwise | flops 2097152 | bytes 12582912 | tf_op jit(solution)/shard_map/convert_element_type | solution.py:1295
  322.8 0.8 slice_multiply_fusion
  325.6 0.8 fusion.7
  326.4 0.7 subtract_multiply_fusion
  327.8 0.7 slice_multiply_fusion.1
  330.1 0.6 pad_maximum_fusion.7
  331.7 1.2 fusion.3
  332.8 4.8 %copy.105 = bf16[4,256,2048]{2,1,0:T(8,128)(2,1)} copy(bf16[4,256,2048]{2,1,0:T(8,128)(2,1)} %get-tuple-element.134) | data formatting | bytes 8388608
  (101 shorter events, 9.8 us)
Async XLA Ops:
  3.0 1.6 copy-start.12
  3.0 2.2 copy-start.4
  5.9 1.1 copy-start.6
  7.7 1.0 copy-start.7
  8.8 2.2 copy-start.5
  11.0 1.4 copy-start
  11.0 1.5 copy-start.1
  12.5 2.5 copy-start.15
  12.5 2.5 copy-start.11
  12.5 2.6 copy-start.13
  15.0 1.1 copy-start.2
  15.0 1.1 copy-start.3
  15.2 2.0 copy-start.22
  16.1 2.1 copy-start.19
  16.1 2.1 copy-start.20
  16.2 3.6 %copy-start.16 = (s32[4,2048]{1,0:T(4,128)S(1)}, s32[4,2048]{1,0:T(4,128)}, u32[]{:S(2)}) copy-start(s32[4,2048]{1,0:T(4,128)} %param.23) | copy-start | bytes 98308
  17.2 7.5 %copy-start.18 = (s32[4,2048]{1,0:T(4,128)S(1)}, s32[4,2048]{1,0:T(4,128)}, u32[]{:S(2)}) copy-start(s32[4,2048]{1,0:T(4,128)} %param.24) | copy-start | bytes 98308
  107.2 2.5 copy-start.23
  316.0 6.8 %copy-start.9 = (f32[192,2048]{1,0:T(8,128)S(1)}, f32[192,2048]{1,0:T(8,128)}, u32[]{:S(2)}) copy-start(f32[192,2048]{1,0:T(8,128)} %get-tuple-element.67) | copy-start | bytes 4718596
  316.0 7.6 %copy-start.17 = (f32[72,128]{1,0:T(8,128)S(1)}, f32[72,128]{1,0:T(8,128)}, u32[]{:S(2)}) copy-start(f32[72,128]{1,0:T(8,128)} %get-tuple-element.68) | copy-start | bytes 110596
  316.0 8.8 %copy-start.21 = (f32[2,2048]{1,0:T(2,128)S(1)}, f32[2,2048]{1,0:T(2,128)}, u32[]{:S(2)}) copy-start(f32[2,2048]{1,0:T(2,128)} %get-tuple-element.48.sq_ref) | copy-start | bytes 49156
  324.8 3.7 %copy-start.8 = (f32[704,128]{1,0:T(8,128)S(1)}, f32[704,128]{1,0:T(8,128)}, u32[]{:S(2)}) copy-start(f32[704,128]{1,0:T(8,128)} %get-tuple-element.71) | copy-start | bytes 1081348
  327.8 1.2 copy-start.10
  328.5 0.9 copy-start.14

commit v3 on v2

--- a/solution.py
+++ b/solution.py
@@ -16,11 +16,6 @@
 rotary_base = 10000.0
 F32 = jnp.float32
 BF16 = jnp.bfloat16
-
-
-def roll_blocks(a, axis, start):
-    n = a.shape[axis]
-    return lax.dynamic_slice_in_dim(jnp.concatenate([a, a], axis=axis), start, n, axis)
 
 
 def halves(a):
@@ -157,23 +152,26 @@
 
 
 def front_kernel(
-    hid_ref, gain_ref, fa_ref, la_ref, ua_ref, maga_ref, thin_ref, fw_ref, aw_ref, bw_ref,
+    hid_ref, gain_ref, fa_ref, la_ref, ua_ref, maga_ref, thin_ref, fo_ref, fe_ref, fr_ref, aw_ref, bw_ref,
     mage_ref, mago_ref, el_ref, small_ref, cos_ref, sin_ref, begin_ref, tag_ref,
     mixed_out, soft_out, log_out, kv_out, weights_out, wq_out, q_out, pre_out, thr_out,
-    cola_out, cole_out, sq_out, ina_out, ine_out, ino_out, n1_out, small_out,
-    kv_all, score, soft, logs, mixed, mixed_x, joined, w_own, wq_all, normed, kv_own, small,
+    cola_out, cole_out, sq_out, ina_out, ine_out, ino_out, n1_out, small,
+    kv_all, score, soft, logs, mixed, mixed_x, joined, w_own, wq_all, normed, kv_own,
     sq_x, sq_y, sq_one, ja,
     kv_send, kv_recv, sib_send, sib_recv, a_send, a_recv, b_send, b_recv, ws_send, ws_recv,
-    m_send, m_recv, sq_send, sq_recv, sm_send, sm_recv, local, n_local,
+    wz_send, wz_recv, wo_send, wo_recv, m_send, m_recv, sq_send, sq_recv, local, n_local,
 ):
     z, core, y, x = place()
     me = z * 2 + core
     rows, here, width = hid_ref.shape
     length = Z * 2 * here
-    count = fw_ref.shape[0]
-    ff = (count - HD) // 3
+    ff = fr_ref.shape[0]
     piece = here // Y
-    cols = pl.ds(pl.multiple_of(core * (width // 2), width // 2), width // 2)
+    step = width // 16
+    odd = z % 2
+    xcols = pl.ds(pl.multiple_of((core * 8 + odd * 3) * step, step), 5 * step)
+    zmine = pl.ds(pl.multiple_of((core * 8 + odd * 5) * step, step), 3 * step)
+    zother = pl.ds(pl.multiple_of((core * 8 + (1 - odd) * 5) * step, step), 3 * step)
     greet(
         [device(dx=d) for d in (1, 2, 3)]
         + [device(dy=d) for d in (1, 2, 3)]
@@ -183,7 +181,11 @@
 
     def join(matrix, start, size, at):
         low = dot32(aw_ref[start : start + size], bw_ref[matrix, :, at], ((1,), (0,)))
-        return fw_ref[start : start + size, at].astype(F32) + adapter_scale * low
+        if matrix in (1, 2):
+            frozen = fe_ref[matrix - 1, :, at]
+        else:
+            frozen = fr_ref[:, at] if matrix else fo_ref[:, at]
+        return frozen.astype(F32) + adapter_scale * low
 
     for s, size in tiles(width, 512):
         at = slice(s, s + size)
@@ -196,14 +198,65 @@
         for d in NEAR_LAST
     ]
 
-    def there(slot, start, size):
+    where = ((HD, ff), (HD + ff, ff), (0, HD))
+    moves = [{}, {}, {}]
+
+    def there(slot, start, size, cols):
         return weights_out.at[slot, pl.ds(start, size), cols]
 
-    begin, relay, relay_far, finish = relay_plan(
-        there, a_send, a_recv, b_send, b_recv, ws_send, ws_recv, cols
-    )
-    where = ((HD, ff), (HD + ff, ff), (0, HD))
-    sent, more, last = {}, {}, {}
+    def begin(p):
+        start, size = where[p]
+        for k, (slot, d) in enumerate(((1, 1), (3, 3))):
+            moves[p]["a", k] = send(
+                w_own.at[pl.ds(start, size), xcols], there(slot, start, size, xcols),
+                a_send.at[p, k], a_recv.at[p, k], device(dx=d),
+            )
+
+    def share(p, slot):
+        start, size = where[p]
+        half = size // 2
+        at = there(slot, start, size, xcols)
+        moves[p]["s", slot] = send(
+            at, at, ws_send.at[p, slot - 1], ws_recv.at[p, slot - 1], device(dc=1)
+        )
+        for k, (first, d) in enumerate(((start, 1), (start + half, 3))):
+            at = there(slot, first, half, zmine)
+            moves[p]["z", slot, k] = send(
+                at, at, wz_send.at[p, slot - 1, k], wz_recv.at[p, slot - 1, k], device(dz=d)
+            )
+
+    def relay(p):
+        start, size = where[p]
+        half = size // 2
+        for k, (slot, first) in enumerate(((1, start), (3, start + half))):
+            moves[p]["a", k].wait_recv()
+            moves[p]["b", k] = send(
+                there(slot, first, half, xcols), there(2, first, half, xcols),
+                b_send.at[p, k], b_recv.at[p, k], device(dx=slot),
+            )
+            share(p, slot)
+
+    def relay_far(p):
+        moves[p]["b", 0].wait_recv()
+        moves[p]["b", 1].wait_recv()
+        share(p, 2)
+
+    def relay_z(p, slot):
+        start, size = where[p]
+        moves[p]["z", slot, 0].wait_recv()
+        moves[p]["z", slot, 1].wait_recv()
+        at = there(slot, start, size, zother)
+        moves[p]["o", slot] = send(
+            at, at, wo_send.at[p, slot - 1], wo_recv.at[p, slot - 1], device(dc=1)
+        )
+
+    def finish(p):
+        for slot in (1, 2, 3):
+            moves[p]["s", slot].wait_recv()
+            moves[p]["o", slot].wait_recv()
+        for copy in moves[p].values():
+            copy.wait_send()
+
     for m in range(2):
         start = HD + m * ff
         total = jnp.zeros((ff, 1), F32)
@@ -219,7 +272,7 @@
         for s, size in tiles(width, 512):
             at = slice(s, s + size)
             w_own[start : start + ff, at] = (joined[:, at] * ratio).astype(BF16)
-        sent[m] = begin(m, w_own.at[pl.ds(start, ff), cols], start, ff)
+        begin(m)
         inner = dot32(w_own[start : start + ff], el_ref[...], ((1,), (0,)))
         ine_out[m * ff : (m + 1) * ff] = inner / ratio
         source = small_ref[0:ff, m * 16 : (m + 1) * 16]
@@ -228,11 +281,7 @@
     small[0:ff, 32:48] = small_ref[0:ff, 32:48].astype(BF16)
     small[0:ff, 80:] = jnp.zeros((ff, HD - 80), BF16)
     small[ff:] = small_ref[ff:].astype(BF16)
-    sm_copies = [
-        send(small, small_out.at[d], sm_send.at[d - 1], sm_recv.at[d - 1], device(dx=d))
-        for d in NEAR_LAST
-    ]
-    own = [keep(small, small_out.at[0], local.at[0])]
+    own = []
     for copy in sq_copies:
         copy.wait()
     sq_one[...] += sq_x[0] + sq_x[1] + sq_x[2]
@@ -256,7 +305,7 @@
         inner = dot32(la_ref[m], ja[...].astype(BF16), ((0,), (0,)))
         ina_out[m] = inner[0:16] + inner[32:48]
     own.append(keep(wq_all, wq_out, local.at[1]))
-    kv_copies, sib_copies, n_copies = [], [], []
+    kv_copies, sib_copies, n_copies = {}, [], []
     gain = gain_ref[...]
     for r in range(rows):
         inputs = hid_ref[r].astype(F32)
@@ -273,12 +322,9 @@
         q_out[r] = rotate(pre[:, :HD], cosine, sine).astype(BF16)
         kv_own[r, :, :HD] = rotate(pre[:, HD : 2 * HD], cosine, sine).astype(BF16)
         kv_own[r, :, HD:] = pre[:, 2 * HD :].astype(BF16)
-        for d in NEAR_LAST:
-            kv_copies.append(
-                send(
-                    kv_own.at[r], kv_all.at[me, r], kv_send.at[r, d - 1], kv_recv.at[r, d - 1],
-                    device(dz=d),
-                )
+        for k, d in enumerate((1, 3)):
+            kv_copies[r, k] = send(
+                kv_own.at[r], kv_all.at[me, r], kv_send.at[r, k], kv_recv.at[r, k], device(dz=d)
             )
         sib_copies.append(
             send(kv_own.at[r], kv_all.at[me, r], sib_send.at[r, 0], sib_recv.at[r, 0], device(dc=1))
@@ -297,21 +343,31 @@
         w_own[HD + 2 * ff :, at] = (two * ratios[1:2, at]).astype(BF16)
         ino_out[0:16, at] = dot32(small[ff:], one.astype(BF16), ((0,), (0,)))[0:16]
         ino_out[16:32, at] = dot32(small[0:ff], two.astype(BF16), ((0,), (0,)))[32:48]
-    sent[2] = begin(2, w_own.at[pl.ds(0, HD), cols], 0, HD)
+    begin(2)
     own.append(keep(w_own, weights_out.at[0], local.at[3]))
-    more[0] = relay(0, sent[0], *where[0])
 
     def pass_kv(r):
-        for k, d in enumerate(NEAR_LAST):
-            kv_copies[3 * r + k].wait_recv()
-            slot = ((z + Z - d) % Z) * 2 + core
-            at = kv_all.at[slot, r]
-            sib_copies.append(send(at, at, sib_send.at[r, d], sib_recv.at[r, d], device(dc=1)))
+        for k, d in enumerate((1, 3)):
+            kv_copies[r, k].wait_recv()
+            at = kv_all.at[((z + Z - d) % Z) * 2 + core, r]
+            if (k == 0) == (r < rows // 2):
+                kv_copies[r, 2] = send(at, at, kv_send.at[r, 2], kv_recv.at[r, 2], device(dz=d))
+            sib_copies.append(
+                send(at, at, sib_send.at[r, 1 + k], sib_recv.at[r, 1 + k], device(dc=1))
+            )
+
+    def pass_far(r):
+        kv_copies[r, 2].wait_recv()
+        at = kv_all.at[((z + 2) % Z) * 2 + core, r]
+        sib_copies.append(send(at, at, sib_send.at[r, 3], sib_recv.at[r, 3], device(dc=1)))
 
     for r in range(rows):
         pass_kv(r)
-    more[1] = relay(1, sent[1], *where[1])
-    own[2].wait()
+    relay(0)
+    for r in range(rows):
+        pass_far(r)
+    relay(1)
+    own[1].wait()
     for copy in sib_copies:
         copy.wait_recv()
     own.append(keep(kv_all, kv_out, local.at[4]))
@@ -354,35 +410,43 @@
         else:
             mixed_x[0] = mixed[0]
         if i == 2:
-            more[2] = relay(2, sent[2], *where[2])
+            relay(2)
+        if i == 1:
+            relay_far(0)
+            relay_z(0, 1)
+            relay_z(0, 3)
         if i == 3:
-            last[0] = relay_far(0, more[0], *where[0])
+            relay_far(1)
+            relay_z(1, 1)
+            relay_z(1, 3)
     own.append(keep(soft, soft_out, local.at[5]))
     own.append(keep(logs, log_out, local.at[6]))
-    last[1] = relay_far(1, more[1], *where[1])
-    last[2] = relay_far(2, more[2], *where[2])
+    relay_far(2)
+    relay_z(2, 1)
+    relay_z(2, 3)
+    for p in range(PIECES):
+        relay_z(p, 2)
     for copy in m_copies:
         copy.wait()
     own.append(keep(mixed_x, mixed_out, local.at[7]))
-    for copy in kv_copies + sib_copies:
+    for copy in list(kv_copies.values()) + sib_copies:
         copy.wait_send()
-    for copy in sm_copies:
-        copy.wait()
     for p in range(PIECES):
-        finish(sent[p], more[p], last[p])
+        finish(p)
     for copy in n_copies[rows - 2 :]:
         copy.wait()
-    own.pop(2)
+    own.pop(1)
     for copy in own:
         copy.wait()
 
 
 def front(
-    hidden, gain, fa, la, ua, maga, thin, fw, aw, bw, mage, mago, el, small, cos, sin, begin, tag
+    hidden, gain, fa, la, ua, maga, thin, fo, fe, fr, aw, bw, mage, mago, el, small, cos, sin,
+    begin, tag,
 ):
     rows, here, width = hidden.shape
-    count = fw.shape[0]
-    ff = (count - HD) // 3
+    ff = fr.shape[0]
+    count = HD + 3 * ff
     length = 2 * Z * here
     s = jax.ShapeDtypeStruct
     return call(
@@ -404,10 +468,10 @@
             s((2 * ff, HD), F32),
             s((32, width), F32),
             s((rows, here, width), BF16),
-            s((X, ff + HD, HD), BF16),
+            s((ff + HD, HD), BF16),
         ),
-        [VM] * 18,
-        (ANY,) * 6 + (VM,) * 9 + (ANY, ANY),
+        [VM] * 20,
+        (ANY,) * 6 + (VM,) * 9 + (ANY, VM),
         [
             pltpu.VMEM((2 * Z, rows, here, 2 * HD), BF16),
             pltpu.VMEM((here, length), F32),
@@ -420,28 +484,32 @@
             pltpu.VMEM((width, 3 * HD), BF16),
             pltpu.VMEM((2, here, width), BF16),
             pltpu.VMEM((rows, here, 2 * HD), BF16),
-            pltpu.VMEM((ff + HD, HD), BF16),
             pltpu.VMEM((3, 2, width), F32),
             pltpu.VMEM((3, 2, width), F32),
             pltpu.VMEM((2, width), F32),
             pltpu.VMEM((width, HD), F32),
             dma(rows, 3), dma(rows, 3), dma(rows, 4), dma(rows, 4),
             dma(PIECES, 2), dma(PIECES, 2), dma(PIECES, 2), dma(PIECES, 2),
+            dma(PIECES, 3), dma(PIECES, 3), dma(PIECES, 3, 2), dma(PIECES, 3, 2),
             dma(PIECES, 3), dma(PIECES, 3),
-            dma(3), dma(3), dma(2, 3), dma(2, 3), dma(3), dma(3), dma(8), dma(rows),
+            dma(3), dma(3), dma(2, 3), dma(2, 3), dma(8), dma(rows),
         ],
         0,
         2 * 2 * rows * here * length * HD + 2 * rows * here * width * 4 * HD,
         32 * 2**20,
-    )(hidden, gain, fa, la, ua, maga, thin, fw, aw, bw, mage, mago, el, small, cos, sin, begin, tag)
+    )(
+        hidden, gain, fa, la, ua, maga, thin, fo, fe, fr, aw, bw, mage, mago, el, small, cos, sin,
+        begin, tag,
+    )
 
 
 def feed_kernel(
-    mixed_ref, hid_ref, gain_ref, cot_ref, weights_ref, small_ref, el_ref, upper_ref, mago_ref,
+    mixed_ref, hidden_ref, gain_ref, cotangent_ref, weights_ref, small_ref, el_ref, upper_ref, mago_ref,
     sq_ref,
-    resid_grad_out, block_out, dmix_out, early_out, columns_out, lower_out,
-    out_w, gate_w, up_w, down_w, normed, low, act, dgate, dup, sends, recvs, acc, resid_s, mags,
-    load, s_send, s_recv, a_send, a_recv, b_send, b_recv, ws_send, ws_recv,
+    resid_grad_out, resid_s, ff_own, ff_send, dmix_out, early_out, columns_out, lower_out,
+    out_w, gate_w, up_w, down_w, normed, low, act, dgate, dup, sends, recvs, acc, mags,
+    hid_ref, cot_ref,
+    small_x, load, s_send, s_recv, local, sm_send, sm_recv, a_send, a_recv, b_send, b_recv, ws_send, ws_recv,
 ):
     z, core, y, x = place()
     width = hid_ref.shape[1]
@@ -450,7 +518,15 @@
     ff = gate_w.shape[0] // X
     cols = pl.ds(pl.multiple_of(core * (width // 2), width // 2), width // 2)
     down_rows = pl.ds(HD + 2 * ff, ff)
-    loads = [[], [], [], []]
+    tokens = pl.ds(pl.multiple_of(y * piece, piece), piece)
+    loads = [[], [], [], [], [keep(hidden_ref.at[x, tokens], hid_ref, local.at[0])]]
+    for j in range(Y):
+        block = pl.ds(pl.multiple_of(((y + j) % Y) * piece, piece), piece)
+        loads[4].append(
+            keep(
+                cotangent_ref.at[x, block], cot_ref.at[pl.ds(j * piece, piece)], local.at[1 + j]
+            )
+        )
     for w, (dst, start, size) in enumerate(((out_w, 0, HD), (gate_w, HD, ff), (up_w, HD + ff, ff))):
         for i in range(X):
             loads[w].append(
@@ -461,7 +537,7 @@
             )
     loads[3].append(keep(weights_ref.at[0, down_rows], down_w.at[pl.ds(0, ff)], load.at[3, 0]))
     greet(
-        [device(dy=d) for d in (1, 2, 3)] + [device(dx=1), device(dx=3), device(dc=1)]
+        [device(dy=d) for d in (1, 2, 3)] + [device(dx=1), device(dx=2), device(dx=3), device(dc=1)]
     )
 
     def there(slot, start, size):
@@ -471,6 +547,10 @@
         there, a_send, a_recv, b_send, b_recv, ws_send, ws_recv, cols
     )
     sent = begin(0, weights_ref.at[0, down_rows, cols], 0, ff)
+    sm_copies = [
+        send(small_ref, small_x.at[d], sm_send.at[d - 1], sm_recv.at[d - 1], device(dx=d))
+        for d in NEAR_LAST
+    ]
 
     def loaded(w):
         for copy in loads[w]:
@@ -486,9 +566,10 @@
         ]
 
     def put(k, part, start, size):
-        acc[k, :, start : start + size] = part[:piece]
+        at = slice(start, start + size)
+        acc[k, :, at] = part[:piece]
         for d in range(1, Y):
-            sends[k, d - 1, :, start : start + size] = part[d * piece : (d + 1) * piece].astype(BF16)
+            sends[k, d - 1, :, at] = part[d * piece : (d + 1) * piece].astype(BF16)
 
     def summed(k, copies):
         for copy in copies:
@@ -514,10 +595,8 @@
     ratios = mago_ref[...] / jnp.sqrt(sq_ref[...])
     upper_o = (upper_ref[0:16] * ratios[0:1]).astype(BF16)
     upper_d = (upper_ref[16:32] * ratios[1:2]).astype(BF16)
+    loaded(4)
     through_down = dot32(cot_ref[...], upper_d, ((1,), (1,))).astype(BF16)
-    small = jnp.concatenate([small_ref[i, 0:ff] for i in range(X)], axis=0)
-    small_o = jnp.concatenate([small_ref[i, ff:] for i in range(X)], axis=0)
-    from_mixed = dot32(mixed_cat, small_o, ((1,), (0,)))[:, 0:16].astype(BF16)
     attended = summed(0, copies)
     acc[0] = attended
     gain = gain_ref[...]
@@ -556,8 +635,15 @@
     two_copies = start_scatter(1)
     for start, size in tiles(width, 512):
         at = slice(start, start + size)
-        put(2, dot32(act[...], down_w[:, at], ((1,), (0,))), start, size)
-    ff_copies = start_scatter(2)
+        part = dot32(act[...], down_w[:, at], ((1,), (0,)))
+        ff_own[:, at] = part[:piece]
+        for d in range(1, Y):
+            ff_send[d - 1, :, at] = part[d * piece : (d + 1) * piece].astype(BF16)
+    for copy in sm_copies:
+        copy.wait()
+    small = jnp.concatenate([small_ref[0:ff]] + [small_x[i, 0:ff] for i in range(1, X)], axis=0)
+    small_o = jnp.concatenate([small_ref[ff:]] + [small_x[i, ff:] for i in range(1, X)], axis=0)
+    from_mixed = dot32(mixed_cat, small_o, ((1,), (0,)))[:, 0:16].astype(BF16)
     through = dot32(normed[...], el_ref[...], ((1,), (0,)))
     through = (through[:, 0:32] + through[:, 32:64]).astype(BF16)
     gate_down = dot32(dgate[...], small, ((1,), (0,)))[:, 0:16].astype(BF16)
@@ -596,12 +682,7 @@
     low[0:piece] = own_low
     copies = start_gather(low, 4)
     mag_out = jnp.sum(own_low.astype(F32) * acc[0], axis=0, keepdims=True)
-    feedforward = summed(2, ff_copies)
-    block_out[...] = (resid_s[...] + feedforward).astype(BF16)
-    mag_down = jnp.sum(cot_own * feedforward, axis=0, keepdims=True)
-    early_out[64:80] = jnp.concatenate(
-        [mag_out, mag_down, jnp.zeros((14, width), F32)], axis=0
-    )
+    early_out[64:80] = jnp.concatenate([mag_out, jnp.zeros((15, width), F32)], axis=0)
     for copy in copies:
         copy.wait()
     d_mixed = dot32(low[...], out_w[...], ((1,), (1,))).astype(BF16)
@@ -614,57 +695,62 @@
     early_out[32:48] = dot32(from_mixed, low[...], ((0,), (0,)))
 
 
-def feed(mixed_x, hid_own, gain, cot_row, weights, small_x, el, upper, mago, squares):
-    here, width = cot_row.shape
+def feed(mixed_x, hidden, gain, cotangent, weights, small, el, upper, mago, squares):
+    _, here, width = hidden.shape
     piece = here // Y
-    hidden = (weights.shape[1] - HD) // 3 * X
+    many = (weights.shape[1] - HD) // 3 * X
     s = jax.ShapeDtypeStruct
     return call(
         feed_kernel,
         (
             s((piece, width), F32),
-            s((piece, width), BF16),
+            s((piece, width), F32),
+            s((piece, width), F32),
+            s((Y - 1, piece, width), BF16),
             s((X, here, HD), BF16),
             s((80, width), F32),
-            s((X, 56, hidden // X), F32),
+            s((X, 56, many // X), F32),
             s((X, 16, HD), F32),
         ),
-        [VM, VM, VM, VM, ANY, VM, VM, VM, VM, VM],
-        (VM,) * 6,
+        [VM, ANY, VM, ANY, ANY, VM, VM, VM, VM, VM],
+        (VM,) * 8,
         [
             pltpu.VMEM((X * HD, width), BF16),
-            pltpu.VMEM((hidden, width), BF16),
-            pltpu.VMEM((hidden, width), BF16),
-            pltpu.VMEM((hidden, width), BF16),
+            pltpu.VMEM((many, width), BF16),
+            pltpu.VMEM((many, width), BF16),
+            pltpu.VMEM((many, width), BF16),
             pltpu.VMEM((here, width), BF16),
             pltpu.VMEM((here, width), BF16),
-            pltpu.VMEM((here, hidden), BF16),
-            pltpu.VMEM((here, hidden), BF16),
-            pltpu.VMEM((here, hidden), BF16),
-            pltpu.VMEM((3, Y - 1, piece, width), BF16),
-            pltpu.VMEM((3, Y - 1, piece, width), BF16),
-            pltpu.VMEM((3, piece, width), F32),
-            pltpu.VMEM((piece, width), F32),
-            pltpu.VMEM((2, hidden), F32),
-            dma(4, X), dma(5, 3), dma(5, 3), dma(1, 2), dma(1, 2), dma(1, 2), dma(1, 2),
+            pltpu.VMEM((here, many), BF16),
+            pltpu.VMEM((here, many), BF16),
+            pltpu.VMEM((here, many), BF16),
+            pltpu.VMEM((2, Y - 1, piece, width), BF16),
+            pltpu.VMEM((2, Y - 1, piece, width), BF16),
+            pltpu.VMEM((2, piece, width), F32),
+            pltpu.VMEM((2, many), F32),
+            pltpu.VMEM((piece, width), BF16),
+            pltpu.VMEM((here, width), BF16),
+            pltpu.VMEM((X,) + small.shape, BF16),
+            dma(4, X), dma(5, 3), dma(5, 3), dma(1 + Y), dma(3), dma(3), dma(1, 2), dma(1, 2), dma(1, 2), dma(1, 2),
             dma(1, 3), dma(1, 3),
         ],
         1,
-        2 * here * hidden * width * 6,
+        2 * here * many * width * 6,
         32 * 2**20,
-    )(mixed_x, hid_own, gain, cot_row, weights, small_x, el, upper, mago, squares)
+    )(mixed_x, hidden, gain, cotangent, weights, small, el, upper, mago, squares)
 
 
 def attend_back_kernel(
-    q_ref, kv_ref, dmix_ref, soft_ref, log_ref, begin_ref, tag_ref, cos_ref, sin_ref, block_ref,
-    grads_out, block_out,
-    kv_all, dmix_all, dmix_abs, part, own, sib_s, sib_r, z_own, z_s, z_r, dq_s,
-    d_send, d_recv, b_send, b_recv, sib_send, sib_recv, z_send, z_recv, local,
+    q_ref, kv_ref, dmix_ref, soft_ref, log_ref, begin_ref, tag_ref, cos_ref, sin_ref, resid_ref,
+    ff_own, ff_send, cot_ref,
+    grads_out, block_out, mag_out,
+    kv_all, dmix_all, dmix_abs, part, own, sib_s, sib_r, z_own, z_s, z_r, dq_s, ff_r, block_ref,
+    cot_own, f_send, f_recv, d_send, d_recv, b_send, b_recv, sib_send, sib_recv, z_send, z_recv, local,
 ):
     z, core, y, x = place()
     me = z * 2 + core
     rows, here = q_ref.shape[0], q_ref.shape[1]
-    piece, width = block_ref.shape
+    piece, width = resid_ref.shape
     half = width // 2
     load = keep(kv_ref, kv_all, local.at[0])
     greet(
@@ -682,27 +768,18 @@
     own_mix = keep(dmix_ref.at[0], dmix_all.at[x], local.at[1])
     tokens = pl.ds(pl.multiple_of(y * piece, piece), piece)
     left, right = pl.ds(0, half), pl.ds(half, half)
-    own_block = keep(block_ref, block_out.at[x, tokens], local.at[2])
-    block_one = []
-    for d in NEAR_LAST:
-        block_one.append(
-            send(
-                block_ref.at[:, left], block_out.at[x, tokens, left],
-                b_send.at[0, d - 1], b_recv.at[0, d - 1], device(dx=d),
-            )
-        )
-        block_one.append(
-            send(
-                block_ref.at[:, right], block_out.at[x, tokens, right],
-                b_send.at[1, d - 1], b_recv.at[1, d - 1], device(dy=d),
-            )
-        )
+    load_cot = keep(cot_ref.at[x, tokens], cot_own, local.at[2])
+    f_copies = [
+        send(ff_send.at[d - 1], ff_r.at[d - 1], f_send.at[d - 1], f_recv.at[d - 1], device(dy=d))
+        for d in NEAR_LAST
+    ]
+    block_one, block_two = [], {}
     load.wait()
     own_mix.wait()
     for copy in d_copies:
         copy.wait()
     spot_q = lax.broadcasted_iota(jnp.int32, (here, 1), 0) + me * here
-    sib_copies, z_copies, block_two = [], [], []
+    sib_copies, z_copies = [], []
 
     def pass_on(r):
         sib_copies[r].wait()
@@ -759,23 +836,53 @@
         grads_out[r, :, :HD] = back(dq_s[r], r).astype(BF16)
         if r:
             pass_on(r - 1)
+        if r == 0:
+            load_cot.wait()
+            for copy in f_copies:
+                copy.wait()
+            feedforward = ff_own[...] + (
+                ff_r[0].astype(F32) + ff_r[1].astype(F32) + ff_r[2].astype(F32)
+            )
+            mag_out[...] = jnp.zeros(mag_out.shape, F32) + jnp.sum(
+                cot_own[...].astype(F32) * feedforward, axis=0, keepdims=True
+            )
+            block_ref[...] = (resid_ref[...] + feedforward).astype(BF16)
+            own_block = keep(block_ref, block_out.at[x, tokens], local.at[3])
+            for d in NEAR_LAST:
+                for k, cut in enumerate((left, right)):
+                    block_one.append(
+                        send(
+                            block_ref.at[:, cut], block_out.at[x, tokens, cut],
+                            b_send.at[k, d - 1], b_recv.at[k, d - 1],
+                            device(dy=d) if k else device(dx=d),
+                        )
+                    )
         if r == 1:
             own_block.wait()
             for copy in block_one:
                 copy.wait()
-            for d in NEAR_LAST:
-                spread = block_out.at[:, tokens, left]
-                block_two.append(
-                    send(
-                        spread, spread, b_send.at[2, d - 1], b_recv.at[2, d - 1], device(dy=d)
+            for k in range(2):
+                for side, d in enumerate((1, 3)):
+                    at = block_out.at[x, :, right] if k else block_out.at[:, tokens, left]
+                    block_two[k, side] = send(
+                        at, at, b_send.at[2 + k, side], b_recv.at[2 + k, side],
+                        device(dx=d) if k else device(dy=d),
                     )
-                )
-                spread = block_out.at[x, :, right]
-                block_two.append(
-                    send(
-                        spread, spread, b_send.at[3, d - 1], b_recv.at[3, d - 1], device(dx=d)
+        if r == 3:
+            for k in range(2):
+                for side, d in enumerate((1, 3)):
+                    block_two[k, side].wait_recv()
+                    if k:
+                        at = block_out.at[
+                            (x + X - d) % X, pl.ds(side * (here // 2), here // 2), right
+                        ]
+                    else:
+                        block = pl.ds(pl.multiple_of(((y + Y - d) % Y) * piece, piece), piece)
+                        at = block_out.at[pl.ds(side * (rows // 2), rows // 2), block, left]
+                    block_two[k, 2 + side] = send(
+                        at, at, b_send.at[4 + k, side], b_recv.at[4 + k, side],
+                        device(dx=d) if k else device(dy=d),
                     )
-                )
     pass_on(rows - 1)
     for r in range(rows):
         for copy in z_copies[3 * r : 3 * r + 3]:
@@ -785,21 +892,26 @@
         )
         grads_out[r, :, HD : 2 * HD] = back(total[:, :HD], r).astype(BF16)
         grads_out[r, :, 2 * HD :] = total[:, HD:].astype(BF16)
-    for copy in block_two:
-        copy.wait()
-
-
-def attend_back(queries, kv, dmix, soft, log, begin, tag, cosine, sine, block):
+    for k in range(2):
+        for side in range(2):
+            block_two[k, side].wait_send()
+            block_two[k, 2 + side].wait()
+
+
+def attend_back(
+    queries, kv, dmix, soft, log, begin, tag, cosine, sine, resid, ff_own, ff_send, cotangent
+):
     rows, here, _ = queries.shape
-    piece, width = block.shape
+    piece, width = resid.shape
     return call(
         attend_back_kernel,
         (
             jax.ShapeDtypeStruct((rows, here, 3 * HD), BF16),
             jax.ShapeDtypeStruct((rows, here, width), BF16),
+            jax.ShapeDtypeStruct((8, width), F32),
         ),
-        [VM, ANY, VM, VM, VM, VM, VM, VM, VM, VM],
-        (VM, ANY),
+        [VM, ANY] + [VM] * 9 + [ANY, ANY],
+        (VM, ANY, VM),
         [
             pltpu.VMEM((2 * Z, rows, here, 2 * HD), BF16),
             pltpu.VMEM((rows, here, HD), BF16),
@@ -812,32 +924,41 @@
             pltpu.VMEM((rows, Z - 1, here, 2 * HD), BF16),
             pltpu.VMEM((rows, Z - 1, here, 2 * HD), BF16),
             pltpu.VMEM((rows, here, HD), F32),
-            dma(3), dma(3), dma(4, 3), dma(4, 3), dma(rows), dma(rows), dma(rows, 3), dma(rows, 3),
-            dma(3),
+            pltpu.VMEM((Y - 1, piece, width), BF16),
+            pltpu.VMEM((piece, width), BF16),
+            pltpu.VMEM((piece, width), BF16),
+            dma(3), dma(3), dma(3), dma(3), dma(6, 3), dma(6, 3), dma(rows), dma(rows),
+            dma(rows, 3), dma(rows, 3), dma(4),
         ],
         2,
         2 * 5 * rows * here * 2 * Z * here * HD,
         32 * 2**20,
-    )(queries, kv, dmix, soft, log, begin, tag, cosine, sine, block)
+    )(
+        queries, kv, dmix, soft, log, begin, tag, cosine, sine, resid, ff_own, ff_send, cotangent
+    )
 
 
 def tail_kernel(
-    grads_ref, weight_ref, hid_ref, gain_ref, dres_ref, pre_ref, thr_ref, n1_ref, inner_ref,
+    grads_ref, weight_ref, hidden_ref, gain_ref, dres_ref, pre_ref, thr_ref, n1_ref, inner_ref,
     cola_ref, maga_ref, uppera_ref, early_ref, both_ref, block_ref, lower_ref,
-    grad_out, all_out, block_out, ctx_out,
+    magd_ref, grad_out, all_out, block_out, ctx_out,
     rel, two, near, held, hop, came, acc, send_2, recv_2, d_one, spread, n1, down, all_s,
-    c_r, z_s, z_r, x_s, x_r, y_s, y_r, bx_r, lx_r, b_one, b_two, e_one, e_two, e_z, b_z,
+    hid_ref, gath, c_r, z_s, z_b, z_r, x_s, x_r, y_v, bx_r, lx_r, b_one, b_two, e_one, e_two, e_z, b_z,
     s_one, r_one, s_two, r_two, s_gat, r_gat, ss, rs, local,
 ):
     z, core, y, x = place()
     rows, here, deep = grads_ref.shape
-    piece, width = hid_ref.shape
+    piece, width = dres_ref.shape
     half = width // 2
-    mid = here // 2
+    sub = piece // 2
+    mid = here // 4
     n = all_s.shape[0]
-    nc, nz = n // 2, n // 2 // Z
-    wx, wy = width // X, width // X // Y
+    nc = n // 2
+    wz, wx = width // Z, width // Z // X
     rank = 16
+    load_hid = keep(
+        hidden_ref.at[x, pl.ds(pl.multiple_of(y * piece, piece), piece)], hid_ref, local.at[2]
+    )
     load = keep(n1_ref, n1, local.at[0])
     for i in range(X):
         for j in range(Y):
@@ -868,32 +989,59 @@
             lhs = rel[d].reshape(here, deep)
         return dot32(lhs, weight_ref[k * half + begin : k * half + begin + size], ((1,), (1,)))
 
+    def cut(part, u, first, count):
+        return jnp.concatenate(
+            [
+                part[b * piece + u * sub : b * piece + (u + 1) * sub]
+                for b in range(first, first + count)
+            ],
+            axis=0,
+        )
+
     one = {}
+
+    def start_far(u):
+        for k in range(2):
+            for side, d in enumerate((1, 3)):
+                one[k, u, side] = send(
+                    two.at[k, u, pl.ds(side * mid, mid)], hop.at[k, u, side],
+                    s_one.at[k, u, side], r_one.at[k, u, side], to(k, d),
+                )
+
+    def start_near(u):
+        for k in range(2):
+            for side, d in enumerate((1, 3)):
+                plain = pl.ds((1 - side) * mid, mid)
+                one[k, u, 2 + side] = send(
+                    near.at[k, u, side, plain], came.at[k, u, side, plain],
+                    s_one.at[k, u, 2 + side], r_one.at[k, u, 2 + side], to(k, d),
+                )
+
     for k in range(2):
         for start, size in tiles(half, 512):
-            two[k, :, start : start + size] = term(k, 2, start, size).astype(BF16)
-        one[k, 0] = send(
-            two.at[k, pl.ds(0, mid)], hop.at[k, 0], s_one.at[k, 0], r_one.at[k, 0], to(k, 1)
-        )
-        one[k, 1] = send(
-            two.at[k, pl.ds(mid, mid)], hop.at[k, 1], s_one.at[k, 1], r_one.at[k, 1], to(k, 3)
-        )
+            part = term(k, 2, start, size)
+            for u in range(2):
+                two[k, u, :, start : start + size] = cut(part, u, 0, 4).astype(BF16)
+    start_far(0)
     for k in range(2):
         for side, d in enumerate((1, 3)):
-            plain = mid if side == 0 else 0
-            other = mid - plain
             for start, size in tiles(half, 512):
                 at = slice(start, start + size)
                 part = term(k, d, start, size)
-                near[k, side, plain : plain + mid, at] = part[plain : plain + mid].astype(BF16)
-                held[k, side, :, at] = part[other : other + mid]
-            one[k, 2 + side] = send(
-                near.at[k, side, pl.ds(plain, mid)], came.at[k, side, pl.ds(plain, mid)],
-                s_one.at[k, 2 + side], r_one.at[k, 2 + side], to(k, d),
-            )
+                rest = (1 - side) * mid
+                for u in range(2):
+                    near[k, u, side, rest : rest + mid, at] = cut(
+                        part, u, 2 * (1 - side), 2
+                    ).astype(BF16)
+                    held[k, u, side, :, at] = cut(part, u, 2 * side, 2)
+    start_near(0)
+    start_far(1)
+    start_near(1)
     for k in range(2):
         for start, size in tiles(half, 512):
-            acc[k, :, start : start + size] = term(k, 0, start, size)
+            part = term(k, 0, start, size)
+            for u in range(2):
+                acc[k, u, :, start : start + size] = cut(part, u, 0, 4)
 
     for m in range(3):
         at = slice(m * HD, (m + 1) * HD)
@@ -930,6 +1078,7 @@
         )
         all_s[7 * rank : 10 * rank, at] = value - all_s[7 * rank : 10 * rank, at]
     all_s[0 : 5 * rank] = early_ref[...]
+    all_s[4 * rank + 1 : 4 * rank + 2] = magd_ref[0:1]
     all_s[5 * rank : 7 * rank] = both_ref[...] * (1.0 / (2 * Z))
     all_s[10 * rank :] = jnp.zeros((n - 10 * rank, width), F32)
 
@@ -941,188 +1090,247 @@
     for d in NEAR_LAST:
         slots.append(go(1, d, block_ref.at[X - d], bx_r.at[d - 1], device(dx=d)))
         slots.append(go(2, d, lower_ref.at[X - d], lx_r.at[d - 1], device(dx=d)))
-    for k in range(2):
-        for side, d in enumerate((1, 3)):
-            one[k, side].wait_recv()
-            other = 0 if side == 0 else mid
-            near[k, side, other : other + mid] = (
-                held[k, side] + hop[k, side].astype(F32)
-            ).astype(BF16)
-            one[k, 4 + side] = send(
-                near.at[k, side, pl.ds(other, mid)], came.at[k, side, pl.ds(other, mid)],
-                s_one.at[k, 4 + side], r_one.at[k, 4 + side], to(k, d),
-            )
+    for u in range(2):
+        for k in range(2):
+            for side, d in enumerate((1, 3)):
+                one[k, u, side].wait_recv()
+                other = pl.ds(side * mid, mid)
+                near[k, u, side, side * mid : (side + 1) * mid] = (
+                    held[k, u, side] + hop[k, u, side].astype(F32)
+                ).astype(BF16)
+                one[k, u, 4 + side] = send(
+                    near.at[k, u, side, other], came.at[k, u, side, other],
+                    s_one.at[k, u, 4 + side], r_one.at[k, u, 4 + side], to(k, d),
+                )
     done(first)
     z_s[...] = all_s[ds(core, nc)] + c_r[...]
-    zc = [go(3, d, z_s.at[ds((z + d) % Z, nz)], z_r.at[d - 1], device(dz=d)) for d in NEAR_LAST]
+    z_b[...] = z_s[...].astype(BF16)
+    zc = [
+        go(3, d, z_b.at[:, ds((z + d) % Z, wz)], z_r.at[d - 1], device(dz=d)) for d in NEAR_LAST
+    ]
     done(slots)
     b_one[...] = block_ref[0] + (bx_r[0] + bx_r[1] + bx_r[2])
     e_one[:rank] = lower_ref[0] + (lx_r[0] + lx_r[1] + lx_r[2])
     cc = [go(4, 0, b_one, b_two, device(dc=1)), go(5, 0, e_one, e_two, device(dc=1))]
-    for index in range(2):
+    seconds = [[], []]
+    for u in range(2):
         for k in range(2):
-            one[k, index].wait_send()
-    for k in range(2):
-        for index in (2, 3, 4, 5):
-            one[k, index].wait()
-    seconds = []
-    for k in range(2):
-        for d in (2, 1, 3, 0):
-            at = slice(d * piece, (d + 1) * piece)
-            part = acc[k, at] + (came[k, 0, at].astype(F32) + came[k, 1, at].astype(F32))
-            if d:
-                send_2[k, d - 1] = part.astype(BF16)
-                seconds.append(
-                    send(
-                        send_2.at[k, d - 1], recv_2.at[k, d - 1], s_two.at[k, d - 1],
-                        r_two.at[k, d - 1], to(1 - k, d),
+            for index in range(2):
+                one[k, u, index].wait_send()
+            for index in (2, 3, 4, 5):
+                one[k, u, index].wait()
+        for k in range(2):
+            for d in (2, 1, 3, 0):
+                at = slice(d * sub, (d + 1) * sub)
+                part = acc[k, u, at] + (
+                    came[k, u, 0, at].astype(F32) + came[k, u, 1, at].astype(F32)
+                )
+                if d:
+                    send_2[u, k, d - 1] = part.astype(BF16)
+                    seconds[u].append(
+                        send(
+                            send_2.at[u, k, d - 1], recv_2.at[u, k, d - 1], s_two.at[u, k, d - 1],
+                            r_two.at[u, k, d - 1], to(1 - k, d),
+                        )
                     )
-                )
-            else:
-                d_one[:, k * half : (k + 1) * half] = part
+                else:
+                    d_one[u, :, k * half : (k + 1) * half] = part
     done(cc)
     b_two[...] += b_one[...]
     e_two[...] += e_one[...]
     done(zc)
-    x_s[...] = z_s[ds(z, nz)] + (z_r[0] + z_r[1] + z_r[2])
+    x_s[...] = z_s[:, ds(z, wz)] + (
+        z_r[0].astype(F32) + z_r[1].astype(F32) + z_r[2].astype(F32)
+    )
     cz = []
+    b_z[z] = b_two[...]
+    e_z[z] = e_two[...]
     for d in NEAR_LAST:
-        cz.append(go(6, d, b_two, b_z.at[d - 1], device(dz=d)))
-        cz.append(go(7, d, e_two, e_z.at[d - 1], device(dz=d)))
+        cz.append(go(6, d, b_two, b_z.at[z], device(dz=d)))
+        cz.append(go(7, d, e_two, e_z.at[z], device(dz=d)))
     xc = [go(8, d, x_s.at[:, ds((x + d) % X, wx)], x_r.at[d - 1], device(dx=d)) for d in NEAR_LAST]
-    done(seconds)
-    for k in range(2):
-        d_one[:, k * half : (k + 1) * half] += (
-            recv_2[k, 0].astype(F32) + recv_2[k, 1].astype(F32) + recv_2[k, 2].astype(F32)
+    left, right = pl.ds(0, half), pl.ds(half, half)
+    load_hid.wait()
+    gat = [[], []]
+    for u in range(2):
+        done(seconds[u])
+        for k in range(2):
+            d_one[u, :, k * half : (k + 1) * half] += (
+                recv_2[u, k, 0].astype(F32)
+                + recv_2[u, k, 1].astype(F32)
+                + recv_2[u, k, 2].astype(F32)
+            )
+        own = slice(u * sub, (u + 1) * sub)
+        inputs = hid_ref[own].astype(F32)
+        inverse = lax.rsqrt(jnp.mean(inputs * inputs, axis=1, keepdims=True) + epsilon)
+        scaled = d_one[u] * gain_ref[...]
+        result = dres_ref[own] + (
+            inverse * scaled
+            - inputs
+            * (inverse * inverse * inverse)
+            * jnp.mean(inputs * scaled, axis=1, keepdims=True)
         )
-    inputs = hid_ref[...].astype(F32)
-    inverse = lax.rsqrt(jnp.mean(inputs * inputs, axis=1, keepdims=True) + epsilon)
-    scaled = d_one[...] * gain_ref[...]
-    result = dres_ref[...] + (
-        inverse * scaled
-        - inputs * (inverse * inverse * inverse) * jnp.mean(inputs * scaled, axis=1, keepdims=True)
-    )
-    tokens = ds(y, piece)
-    left, right = pl.ds(0, half), pl.ds(half, half)
-    spread[x, tokens] = result.astype(BF16)
-    gat = []
-    for d in NEAR_LAST:
-        for k, cut in enumerate((left, right)):
-            at = spread.at[x, tokens, cut]
-            gat.append(send(at, at, s_gat.at[k, d - 1], r_gat.at[k, d - 1], to(k, d)))
-    done(xc)
-    y_s[...] = x_s[:, ds(x, wx)] + (x_r[0] + x_r[1] + x_r[2])
-    yc = [go(9, d, y_s.at[:, ds((y + d) % Y, wy)], y_r.at[d - 1], device(dy=d)) for d in NEAR_LAST]
-    done(gat)
-
-    def block_of(k, d):
+        spread[x, y, own] = result.astype(BF16)
+        for d in NEAR_LAST:
+            for k, side in enumerate((left, right)):
+                at = spread.at[x, y, pl.ds(u * sub, sub), side]
+                gat[u].append(
+                    send(at, at, s_gat.at[u, k, d - 1], r_gat.at[u, k, d - 1], to(k, d))
+                )
+        if u == 0:
+            done(xc)
+            y_v[y] = x_s[:, ds(x, wx)] + (x_r[0] + x_r[1] + x_r[2])
+            yc = [go(9, d, y_v.at[y], y_v.at[y], device(dy=d)) for d in NEAR_LAST]
+    done(yc)
+    mine = ds(core, nc)
+    at_x = ds(z * X + x, wx)
+    gath[mine, at_x] = (((y_v[0] + y_v[1]) + y_v[2]) + y_v[3]).astype(BF16)
+    sx = [go(10, d, gath.at[mine, at_x], gath.at[mine, at_x], device(dx=d)) for d in NEAR_LAST]
+
+    def part_of(k, u, d, first, count):
+        tokens = pl.ds(u * sub, sub)
         if k:
-            return spread.at[(x + d) % X, :, right]
-        return spread.at[:, ds((y + d) % Y, piece), left]
-
-    def part_of(k, d, second):
-        if k:
-            return spread.at[(x + d) % X, pl.ds(second * mid, mid), right]
-        return spread.at[pl.ds(second * 2, 2), ds((y + d) % Y, piece), left]
+            return spread.at[(x + d) % X, pl.ds(first, count), tokens, right]
+        return spread.at[pl.ds(first, count), (y + d) % Y, tokens, left]
 
     last = {}
-    for k in range(2):
-        for side, d in enumerate((1, 3)):
-            last[k, side] = send(
-                block_of(k, 0), block_of(k, 0), s_gat.at[2 + k, side], r_gat.at[2 + k, side],
-                to(1 - k, d),
-            )
-    mine = ds(core * Z + z, nz)
-    done(yc)
-    all_out[mine, ds(x * Y + y, wy)] = y_s[:, ds(y, wy)] + (y_r[0] + y_r[1] + y_r[2])
-    spot = all_out.at[mine, ds(x * Y + y, wy)]
-    done([go(10, d, spot, spot, device(dy=d)) for d in NEAR_LAST])
-    spot = all_out.at[mine, ds(x, wx)]
-    sx = [go(11, d, spot, spot, device(dx=d)) for d in NEAR_LAST]
-    for k in range(2):
-        for side, d in enumerate((1, 3)):
-            last[k, side].wait_recv()
-            at = part_of(k, -d % 4, side)
-            last[k, 2 + side] = send(
-                at, at, s_gat.at[4 + k, side], r_gat.at[4 + k, side], to(1 - k, d)
-            )
+    for u in range(2):
+        done(gat[u])
+        for k in range(2):
+            for side, d in enumerate((1, 3)):
+                at = part_of(k, u, 0, 0, 4)
+                last[k, u, side] = send(
+                    at, at, s_gat.at[u, 2 + k, side], r_gat.at[u, 2 + k, side], to(1 - k, d)
+                )
     done(sx)
-    spot = all_out.at[mine]
-    done([go(12, d, spot, spot, device(dz=d)) for d in NEAR_LAST])
-    spot = all_out.at[ds(core, nc)]
-    sc = [go(13, 0, spot, spot, device(dc=1))]
+    spot = gath.at[mine, ds(z, wz)]
+    sz = [go(11, d, spot, spot, device(dz=d)) for d in NEAR_LAST]
     done(cz)
-    block_out[...] = b_two[...] + (b_z[0] + b_z[1] + b_z[2])
-    ctx_out[...] = e_two[...] + (e_z[0] + e_z[1] + e_z[2])
-    for k in range(2):
-        for side in range(2):
-            last[k, side].wait_send()
-            last[k, 2 + side].wait()
+    block_out[...] = ((b_z[0] + b_z[1]) + b_z[2]) + b_z[3]
+    ctx_out[...] = ((e_z[0] + e_z[1]) + e_z[2]) + e_z[3]
+    done(sz)
+    spot = gath.at[mine]
+    sc = go(12, 0, spot, spot, device(dc=1))
+    for u in range(2):
+        for k in range(2):
+            for side, d in enumerate((1, 3)):
+                last[k, u, side].wait_recv()
+                at = part_of(k, u, 4 - d, 2 * side, 2)
+                last[k, u, 2 + side] = send(
+                    at, at, s_gat.at[u, 4 + k, side], r_gat.at[u, 4 + k, side], to(1 - k, d)
+                )
+    for u in range(2):
+        for k in range(2):
+            for side in range(2):
+                last[k, u, side].wait_send()
+                last[k, u, 2 + side].wait()
     out = keep(spread, grad_out, local.at[1])
-    done(sc)
+    sc.wait()
+    all_out[...] = gath[...]
     out.wait()
 
 
 def tail(
-    grads, weight, hid_own, gain, d_resid, pre, thr, n1, inner, cola, maga, uppera, early, both,
-    block, lower,
+    grads, weight, hidden, gain, d_resid, pre, thr, n1, inner, cola, maga, uppera, early, both,
+    block, lower, magd,
 ):
     rows, here, deep = grads.shape
-    piece, width = hid_own.shape
+    piece, width = d_resid.shape
     half = width // 2
-    mid = here // 2
+    mid = here // 4
+    sub = piece // 2
     _, bn, bw = block.shape
     n = 192
     en = 72
-    nc, nz = n // 2, n // 2 // Z
-    wx, wy = width // X, width // X // Y
+    nc = n // 2
+    wz, wx = width // Z, width // Z // X
     s = jax.ShapeDtypeStruct
     v = pltpu.VMEM
     return call(
         tail_kernel,
-        (s((rows, here, width), BF16), s((n, width), F32), s((bn, bw), F32), s((en, HD), F32)),
-        [VM] * 7 + [ANY] + [VM] * 8,
+        (s((rows, Y, piece, width), BF16), s((n, width), BF16), s((bn, bw), F32), s((en, HD), F32)),
+        [VM] * 2 + [ANY] + [VM] * 4 + [ANY] + [VM] * 9,
         (ANY, VM, VM, VM),
         [
             v((X, Y, piece, deep), BF16),
-            v((2, here, half), BF16),
-            v((2, 2, here, half), BF16),
-            v((2, 2, mid, half), F32),
-            v((2, 2, mid, half), BF16),
-            v((2, 2, here, half), BF16),
-            v((2, here, half), F32),
-            v((2, 3, piece, half), BF16),
-            v((2, 3, piece, half), BF16),
-            v((piece, width), F32),
-            v((rows, here, width), BF16),
+            v((2, 2, 2 * mid, half), BF16),
+            v((2, 2, 2, 2 * mid, half), BF16),
+            v((2, 2, 2, mid, half), F32),
+            v((2, 2, 2, mid, half), BF16),
+            v((2, 2, 2, 2 * mid, half), BF16),
+            v((2, 2, 2 * mid, half), F32),
+            v((2, 2, 3, sub, half), BF16),
+            v((2, 2, 3, sub, half), BF16),
+            v((2, sub, width), F32),
+            v((X, Y, piece, width), BF16),
             v((rows, here, width), BF16),
             v((rows * here, 48), BF16),
             v((n, width), F32),
+            v((piece, width), BF16),
+            v((n, width), BF16),
             v((nc, width), F32),
             v((nc, width), F32),
-            v((3, nz, width), F32),
-            v((nz, width), F32),
-            v((3, nz, wx), F32),
-            v((nz, wx), F32),
-            v((3, nz, wy), F32),
+            v((nc, width), BF16),
+            v((3, nc, wz), BF16),
+            v((nc, wz), F32),
+            v((3, nc, wx), F32),
+            v((Y, nc, wx), F32),
             v((3, bn, bw), F32),
             v((3, 16, HD), F32),
             v((bn, bw), F32),
             v((bn, bw), F32),
             v((en, HD), F32),
             v((en, HD), F32),
-            v((3, en, HD), F32),
-            v((3, bn, bw), F32),
-            dma(2, 6), dma(2, 6), dma(2, 3), dma(2, 3), dma(6, 3), dma(6, 3),
-            dma(14, 4), dma(14, 4), dma(2),
+            v((Z, en, HD), F32),
+            v((Z, bn, bw), F32),
+            dma(2, 2, 6), dma(2, 2, 6), dma(2, 2, 3), dma(2, 2, 3), dma(2, 6, 3), dma(2, 6, 3),
+            dma(13, 4), dma(13, 4), dma(3),
         ],
         3,
         2 * rows * here * deep * width,
         16 * 2**20,
     )(
-        grads, weight, hid_own, gain, d_resid, pre, thr, n1, inner, cola, maga, uppera, early, both,
-        block, lower,
-    )
+        grads, weight, hidden, gain, d_resid, pre, thr, n1, inner, cola, maga, uppera, early, both,
+        block, lower, magd,
+    )
+
+
+def widen_kernel(a_ref, b_ref, wide_out, same_out, narrow, wide, passed, loads, stores):
+    rows = a_ref.shape[0]
+    copies = [keep(a_ref.at[r], narrow.at[r], loads.at[0, r]) for r in range(rows)]
+    others = [keep(b_ref.at[r], passed.at[r], loads.at[1, r]) for r in range(rows)]
+    outs = []
+    for r in range(rows):
+        copies[r].wait()
+        wide[r] = narrow[r].astype(F32)
+        outs.append(keep(wide.at[r], wide_out.at[r], stores.at[0, r]))
+    for r in range(rows):
+        others[r].wait()
+        outs.append(keep(passed.at[r], same_out.at[r], stores.at[1, r]))
+    for copy in outs:
+        copy.wait()
+
+
+def widen(a, b):
+    parts = 16
+    many, width = a.shape[0] * a.shape[1] * a.shape[2] // parts, a.shape[3]
+    wide, same = pl.pallas_call(
+        widen_kernel,
+        out_shape=(
+            jax.ShapeDtypeStruct((parts, many, width), F32),
+            jax.ShapeDtypeStruct((parts, many, width), BF16),
+        ),
+        in_specs=[ANY, ANY],
+        out_specs=(ANY, ANY),
+        scratch_shapes=[
+            pltpu.VMEM((parts, many, width), BF16),
+            pltpu.VMEM((parts, many, width), F32),
+            pltpu.VMEM((parts, many, width), BF16),
+            dma(2, parts), dma(2, parts),
+        ],
+        compiler_params=pltpu.CompilerParams(vmem_limit_bytes=58 * 2**20),
+    )(a.reshape(parts, many, width), b.reshape(parts, many, width))
+    return wide.reshape(b.shape), same.reshape(b.shape)
 
 
 def on_device(
@@ -1152,11 +1360,8 @@
     rows, here, width = hidden.shape
     length = segments.shape[1]
     ff = reduce_frozen.shape[0]
-    piece = here // Y
     rank = output_lower.shape[1]
     ctx = lax.axis_index("ctx")
-    tp = lax.axis_index("tp")
-    y, x = tp // X, tp % X
     offset = ctx * here
 
     def left_factor(a):
@@ -1167,9 +1372,6 @@
         high, low = halves(a)
         return jnp.concatenate([high, low, high], axis=-2)
 
-    fw = jnp.concatenate(
-        [output_frozen, expand_frozen[0].T, expand_frozen[1].T, reduce_frozen], axis=0
-    )
     expand_upper_t = expand_upper.transpose(0, 2, 1)
     aw = left_factor(
         jnp.concatenate([output_lower, expand_upper_t[0], expand_upper_t[1], reduce_lower], axis=0)
@@ -1214,10 +1416,6 @@
     begin = begin_here.astype(jnp.int32)[:, :, None]
     gain_one = attention_gain.astype(F32)
     gain_two = feedforward_gain.astype(F32)
-
-    def take_row(a):
-        mine = lax.dynamic_index_in_dim(a, x, 0, keepdims=False)
-        return roll_blocks(mine.reshape(Y, piece, width), 0, y)
 
     (
         mixed_parts,
@@ -1236,7 +1434,7 @@
         inner_expand,
         inner_both,
         normed_one,
-        small_x,
+        small_own,
     ) = front(
         hidden,
         gain_one[None],
@@ -1245,7 +1443,9 @@
         ua,
         attend_magnitude,
         thin,
-        fw,
+        output_frozen,
+        expand_frozen.transpose(0, 2, 1),
+        reduce_frozen,
         aw,
         bw,
         expand_magnitude.reshape(2 * ff, 1),
@@ -1257,12 +1457,10 @@
         begin,
         key_tag,
     )
-    hid_own = take_row(hidden)[0]
-    cot_row = take_row(cotangent).reshape(here, width)
-    d_resid, block_own, d_mixed_parts, early, block_x, lower_out = feed(
-        mixed_parts, hid_own, gain_two[None], cot_row, weights_x, small_x, el, upper, mago, squares
-    )
-    grads_low, block_output = attend_back(
+    d_resid, resid, ff_own, ff_send, d_mixed_parts, early, block_x, lower_out = feed(
+        mixed_parts, hidden, gain_two[None], cotangent, weights_x, small_own, el, upper, mago, squares
+    )
+    grads_low, block_output, mag_down = attend_back(
         queries,
         all_pairs,
         d_mixed_parts,
@@ -1272,12 +1470,15 @@
         key_tag,
         cosine,
         sine_part,
-        block_own,
+        resid,
+        ff_own,
+        ff_send,
+        cotangent,
     )
     hidden_grad, everywhere, block_x, small_ctx = tail(
         grads_low,
         weight_attend,
-        hid_own,
+        hidden,
         gain_one[None],
         d_resid,
         pre,
@@ -1291,8 +1492,10 @@
         inner_both,
         block_x,
         lower_out,
-    )
-    hidden_grad = hidden_grad.astype(F32)
+        mag_down,
+    )
+    hidden_grad, block_output = widen(hidden_grad, block_output)
+    everywhere = everywhere.astype(F32)
     lower_out, local = small_ctx[:rank], small_ctx[rank:]
     late = adapter_scale * everywhere[7 * rank : 10 * rank]
     early = everywhere[: 7 * rank]

time: 343 us -> 303 us (0.88)
  Pallas kernels: 285 us -> 265 us
  other arithmetic: 28.5 us -> 17.7 us
  local copies, waits for them, and re-layouts: 18.9 us -> 11.4 us
    pallas_call x1, Pallas kernels: 81.8 us -> 63 us  [front(): call(front_kernel, (s((X, here, HD), BF16), s((rows, here, HD), F32), s((...]
    pallas_call x2 -> x3, Pallas kernels: 161 us -> 152 us  [the longest x1 76.5 us: feed(): call(feed_kernel, (s((piece, width), F32), s((piece, width), F32), s((pie...]
    pallas_call x1, Pallas kernels: 42.7 us -> 50 us  [attend_back(): call(attend_back_kernel, (jax.ShapeDtypeStruct((rows, here, 3 * HD), BF16...]
    unnamed x52 -> x47, local copies, waits for them, and re-layouts: 8.16 us -> 1.23 us
    convert_element_type x1, other arithmetic: 6.77 us -> 1.41 us  [on_device(): everywhere = everywhere.astype(F32)]
    concatenate x2 -> x0, other arithmetic: 3.87 us -> none  [the longest x1 2.53 us: on_device(): jnp.concatenate([output_frozen, expand_frozen[0].T, expand_frozen[1].T, r...]
where the time goes in v3:
time: 303 us; the launch traced here: 300 us
  Pallas kernels  265 us (87%)
  other arithmetic  17.7 us (6%)
  local copies, waits for them, and re-layouts  11.4 us (4%)
  matrix products  4.39 us (1%)
    pallas_call x1, Pallas kernels, feed(): call(feed_kernel, (s((piece, width), F32), s((piece, width), F32), s((pie...  76.5 us
    pallas_call x1, Pallas kernels, tail(): call(tail_kernel, (s((rows, Y, piece, width), BF16), s((n, width), BF16),...  67.2 us
    pallas_call x1, Pallas kernels, front(): call(front_kernel, (s((X, here, HD), BF16), s((rows, here, HD), F32), s((...  63 us
    pallas_call x1, Pallas kernels, attend_back(): call(attend_back_kernel, (jax.ShapeDtypeStruct((rows, here, 3 * HD), BF16...  50 us
    pallas_call x1, Pallas kernels, widen(): pl.pallas_call(widen_kernel, out_shape=(jax.ShapeDtypeStruct((parts, many...  8.15 us

profile of v3, /device:TPU:0, one launch (start us, length us, event | category | flops | bytes accessed | tf_op | source)
XLA Modules:
  0.0 299.7 jit_solution(12990293137747454169)
XLA Ops:
  0.7 0.7 constant_dynamic-slice_fusion
  1.4 0.9 convert_reduce_fusion
  2.5 3.0 %multiply_sine_fusion = (f32[4,256,128]{2,1,0:T(8,128)}, f32[4,256,128]{2,1,0:T(8,128)}) fusion(f32[128]{0:T(128)S(1)} %pad_maximum_fusion.9, f32[4,256]{1,0:T(4,128)S(1)} %get-tuple-element.123), kind=kLoop, calls=%fused_computation.15 | loop fusion | flops 131072 | bytes 1053184 | tf_op jit(solution)/shard_map/sin | solution.py:1413
  5.5 1.0 copy.98.begin_ref
  6.8 0.9 copy.96.aw_ref
  8.4 0.9 fusion.43
  10.3 0.7 copy-done.6
  11.1 1.6 maximum_maximum_fusion
  12.9 1.0 pad_maximum_fusion.bw_ref
  14.0 0.7 select_maximum_fusion.small_ref
  14.8 0.6 pad_maximum_fusion.8.mago_ref
  15.6 2.0 copy.95.la_ref
  17.6 0.6 pad_maximum_fusion.7.ua_ref
  18.2 0.6 broadcast_in_dim.48.tag_ref
  18.9 0.6 broadcast_in_dim.51
  19.5 1.0 reshape.109.mage_ref
  20.5 63.0 %shard_map.317 = (bf16[4,256,128]{2,1,0:T(8,128)(2,1)}, f32[4,256,128]{2,1,0:T(8,128)}, f32[4,256,1]{2,1,0:T(8,128)}, bf16[8,4,256,256]{3,2,1,0:T(8,128)(2,1)}, ...) custom-call(bf16[4,256,2048]{2,1,0:T(8,128)(2,1)} %hidden_ref.3, ...), custom_call_target="tpu_custom_call" | custom-call | flops 3221225472 | bytes 33554432 | tf_op jit(solution)/shard_map/pallas_call | solution.py:452
  83.5 0.7 pad_maximum_fusion.3.upper_ref
  84.8 76.5 %shard_map.318 = (f32[64,2048]{1,0:T(8,128)}, f32[64,2048]{1,0:T(8,128)}, f32[64,2048]{1,0:T(8,128)}, bf16[3,64,2048]{2,1,0:T(8,128)(2,1)}, bf16[4,256,128]{2,1,...) custom-call(bf16[4,256,128]{2,1,0:T(8,128)(2,1)} %get-tuple-element.50.mixed_ref, ...), custom_call_target="tpu_custom_call" | custom-call | flops 8858370048 | bytes 33554432 | tf_op jit(solution)/shard_map/pallas_call | solution.py:703
  161.3 50.0 %shard_map.319 = (bf16[4,256,384]{2,1,0:T(8,128)(2,1)}, bf16[4,256,2048]{2,1,0:T(8,128)(2,1)}, f32[8,2048]{1,0:T(8,128)}) custom-call(bf16[4,256,128]{2,1,0:T(8,128)(2,1)} %get-tuple-element.48.q_ref, bf16[8,4,256,256]{3,2,1,0:T(8,128)(2,1)} %get-tuple-element.49.kv_ref, bf16[4,256,128]{2,1,0:T(8,128)(2,1)} %get-tuple-element.54.dmix_ref, ...), custom_call_target="tpu_custom_call" | custom-call | flops 2684354560 | bytes 33554432 | tf_op jit(solution)/shard_map/pallas_call | solution.py:906
  211.3 67.2 %shard_map.320 = (bf16[4,4,64,2048]{3,2,1,0:T(8,128)(2,1)}, bf16[192,2048]{1,0:T(8,128)(2,1)}, f32[56,352]{1,0:T(8,128)}, f32[72,128]{1,0:T(8,128)}) custom-call(bf16[4,256,384]{2,1,0:T(8,128)(2,1)} %get-tuple-element.60.grads_ref, bf16[2048,384]{1,0:T(8,128)(2,1)} %get-tuple-element.61.weight_ref, bf16[4,256,2048]{2,1,0:T(8,128)(2,1)} %hidden_ref.3, ...), custom_call_target="tpu_custom_call" | custom-call | flops 1610612736 | bytes 16777216 | tf_op jit(solution)/shard_map/pallas_call | solution.py:1249
  278.6 1.4 convert_element_type.103
  281.1 1.9 fusion.3
  283.2 1.3 multiply_divide_fusion.1
  285.1 0.6 pad_maximum_fusion.6
  285.8 0.7 fusion.17
  287.3 0.8 fusion.7
  288.1 0.6 fusion.45
  288.7 8.1 %shard_map.321 = (f32[16,64,2048]{2,1,0:T(8,128)}, bf16[16,64,2048]{2,1,0:T(8,128)(2,1)}) custom-call(bf16[16,64,2048]{2,1,0:T(8,128)(2,1)} %bitcast.113, bf16[16,64,2048]{2,1,0:T(8,128)(2,1)} %bitcast.112), custom_call_target="tpu_custom_call" | custom-call | tf_op jit(solution)/shard_map/pallas_call | solution.py:1317
  296.8 0.8 slice_multiply_fusion
  297.6 0.7 slice_multiply_fusion.1
  298.3 0.6 slice.115
  (92 shorter events, 6.3 us)
Async XLA Ops:
  0.6 6.0 %copy-start.13 = (f32[2,16,352]{2,1,0:T(8,128)S(1)}, f32[2,16,352]{2,1,0:T(8,128)}, u32[]{:S(2)}) copy-start(f32[2,16,352]{2,1,0:T(8,128)} %param.38) | copy-start | bytes 135172
  0.7 6.0 %copy-start.11 = (f32[128,16]{0,1:T(8,128)S(1)}, f32[128,16]{0,1:T(8,128)}, u32[]{:S(2)}) copy-start(f32[128,16]{0,1:T(8,128)} %param.34) | copy-start | bytes 24580
  0.7 5.9 %copy-start.9 = (f32[352,16]{0,1:T(8,128)S(1)}, f32[352,16]{0,1:T(8,128)}, u32[]{:S(2)}) copy-start(f32[352,16]{0,1:T(8,128)} %param.40) | copy-start | bytes 67588
  0.7 7.0 %copy-start.4 = (f32[3,2048,16]{1,2,0:T(8,128)S(1)}, f32[3,2048,16]{1,2,0:T(8,128)}, u32[]{:S(2)}) copy-start(f32[3,2048,16]{1,2,0:T(8,128)} %param.31) | copy-start | bytes 1179652
  8.4 1.0 copy-start.5
  10.0 1.0 copy-start.6
  11.1 1.7 copy-start.2
  11.1 1.7 copy-start.3
  12.7 2.0 copy-start.16
  12.8 2.0 copy-start.17
  15.4 2.1 copy-start.10
  15.5 2.8 copy-start.15
  15.5 3.4 %copy-start.20 = (bf16[2048]{0:T(1024)(128)(2,1)S(1)}, bf16[2048]{0:T(1024)(128)(2,1)}, u32[]{:S(2)}) copy-start(bf16[2048]{0:T(1024)(128)(2,1)} %param.25) | copy-start | bytes 12292
  15.5 4.0 %copy-start.19 = (f32[2,352]{1,0:T(2,128)S(1)}, f32[2,352]{1,0:T(2,128)}, u32[]{:S(2)}) copy-start(f32[2,352]{1,0:T(2,128)} %param.39) | copy-start | bytes 8452
  20.5 63.7 %copy-start.21 = (bf16[2048]{0:T(1024)(128)(2,1)S(1)}, bf16[2048]{0:T(1024)(128)(2,1)}, u32[]{:S(2)}) copy-start(bf16[2048]{0:T(1024)(128)(2,1)} %param.26) | copy-start | bytes 12292
  278.6 1.4 copy-start.18
  278.6 2.0 copy-start
  280.6 2.4 copy-start.8
  280.6 4.0 %copy-start.7 = (f32[704,128]{1,0:T(8,128)S(1)}, f32[704,128]{1,0:T(8,128)}, u32[]{:S(2)}) copy-start(f32[704,128]{1,0:T(8,128)} %get-tuple-element.81) | copy-start | bytes 1081348
  283.0 2.1 copy-start.12
  284.6 1.9 copy-start.1
  285.1 2.2 copy-start.14

commit v4 on v3

--- a/solution.py
+++ b/solution.py
@@ -507,8 +507,8 @@
     mixed_ref, hidden_ref, gain_ref, cotangent_ref, weights_ref, small_ref, el_ref, upper_ref, mago_ref,
     sq_ref,
     resid_grad_out, resid_s, ff_own, ff_send, dmix_out, early_out, columns_out, lower_out,
-    out_w, gate_w, up_w, down_w, normed, low, act, dgate, dup, sends, recvs, acc, mags,
-    hid_ref, cot_ref,
+    out_w, gate_w, up_w, down_w, normed, low, act, dgate, dup, far, near, held, hop, came, acc, mags,
+    hid_ref, cot_ref, gate_s, up_s, dact_s,
     small_x, load, s_send, s_recv, local, sm_send, sm_recv, a_send, a_recv, b_send, b_recv, ws_send, ws_recv,
 ):
     z, core, y, x = place()
@@ -516,17 +516,22 @@
     piece = hid_ref.shape[0]
     here = cot_ref.shape[0]
     ff = gate_w.shape[0] // X
+    sub = piece // 2
+    many = here // 2
     cols = pl.ds(pl.multiple_of(core * (width // 2), width // 2), width // 2)
     down_rows = pl.ds(HD + 2 * ff, ff)
     tokens = pl.ds(pl.multiple_of(y * piece, piece), piece)
     loads = [[], [], [], [], [keep(hidden_ref.at[x, tokens], hid_ref, local.at[0])]]
-    for j in range(Y):
-        block = pl.ds(pl.multiple_of(((y + j) % Y) * piece, piece), piece)
-        loads[4].append(
-            keep(
-                cotangent_ref.at[x, block], cot_ref.at[pl.ds(j * piece, piece)], local.at[1 + j]
-            )
-        )
+    for u in range(2):
+        for j in range(Y):
+            first = ((y + j) % Y) * piece + u * sub
+            loads[4].append(
+                keep(
+                    cotangent_ref.at[x, pl.ds(pl.multiple_of(first, sub), sub)],
+                    cot_ref.at[pl.ds(u * many + j * sub, sub)],
+                    local.at[1 + u * Y + j],
+                )
+            )
     for w, (dst, start, size) in enumerate(((out_w, 0, HD), (gate_w, HD, ff), (up_w, HD + ff, ff))):
         for i in range(X):
             loads[w].append(
@@ -547,98 +552,199 @@
         there, a_send, a_recv, b_send, b_recv, ws_send, ws_recv, cols
     )
     sent = begin(0, weights_ref.at[0, down_rows, cols], 0, ff)
-    sm_copies = [
-        send(small_ref, small_x.at[d], sm_send.at[d - 1], sm_recv.at[d - 1], device(dx=d))
-        for d in NEAR_LAST
-    ]
 
     def loaded(w):
         for copy in loads[w]:
             copy.wait()
 
-    def start_scatter(k):
-        return [
-            send(
-                sends.at[k, d - 1], recvs.at[k, d - 1], s_send.at[k, d - 1], s_recv.at[k, d - 1],
-                device(dy=d),
-            )
-            for d in NEAR_LAST
-        ]
-
-    def put(k, part, start, size):
+    half = width // 2
+    cut_a, cut_b = pl.ds(0, half), pl.ds(half, half)
+    moves = {}
+
+    def put(k, u, part, start, size):
         at = slice(start, start + size)
-        acc[k, :, at] = part[:piece]
-        for d in range(1, Y):
-            sends[k, d - 1, :, at] = part[d * piece : (d + 1) * piece].astype(BF16)
-
-    def summed(k, copies):
-        for copy in copies:
-            copy.wait()
-        return acc[k] + (
-            recvs[k, 0].astype(F32) + recvs[k, 1].astype(F32) + recvs[k, 2].astype(F32)
+        acc[k, u * sub : (u + 1) * sub, at] = part[0:sub]
+        far[k, u, :, at] = part[2 * sub : 3 * sub].astype(BF16)
+        for side, block in enumerate((1, 3)):
+            value = part[block * sub : (block + 1) * sub]
+            if (start < half) == (side == 1):
+                near[k, u, side, :, at] = value.astype(BF16)
+            else:
+                inner = start % half
+                held[k, u, side, :, inner : inner + size] = value
+
+    def scatter_start(k, u):
+        for side, (cut, d) in enumerate(((cut_a, 1), (cut_b, 3))):
+            moves[k, u, side] = send(
+                far.at[k, u, :, cut], hop.at[k, u, side], s_send.at[k, u, side],
+                s_recv.at[k, u, side], device(dy=d),
+            )
+        for side, (cut, d) in enumerate(((cut_b, 1), (cut_a, 3))):
+            moves[k, u, 2 + side] = send(
+                near.at[k, u, side, :, cut], came.at[k, u, side, :, cut],
+                s_send.at[k, u, 2 + side], s_recv.at[k, u, 2 + side], device(dy=d),
+            )
+
+    def scatter_relay(k, u):
+        for side, (cut, d) in enumerate(((cut_a, 1), (cut_b, 3))):
+            moves[k, u, side].wait_recv()
+            near[k, u, side, :, side * half : (side + 1) * half] = (
+                held[k, u, side] + hop[k, u, side].astype(F32)
+            ).astype(BF16)
+            moves[k, u, 4 + side] = send(
+                near.at[k, u, side, :, cut], came.at[k, u, side, :, cut],
+                s_send.at[k, u, 4 + side], s_recv.at[k, u, 4 + side], device(dy=d),
+            )
+
+    def scatter_sum(k, u):
+        for index in range(2):
+            moves[k, u, index].wait_send()
+        for index in range(2, 6):
+            moves[k, u, index].wait()
+        return acc[k, u * sub : (u + 1) * sub] + (
+            came[k, u, 0].astype(F32) + came[k, u, 1].astype(F32)
         )
 
-    def start_gather(buffer, k):
-        return [
-            send(
-                buffer.at[pl.ds(0, piece)], buffer.at[pl.ds((Y - d) * piece, piece)],
-                s_send.at[k, d - 1], s_recv.at[k, d - 1], device(dy=d),
-            )
-            for d in NEAR_LAST
-        ]
+    def block_at(buffer, u, block, cut=slice(None)):
+        return buffer.at[pl.ds(u * many + block * sub, sub), cut]
+
+    def gather_start(buffer, k, u):
+        for side, (d, block) in enumerate(((1, 3), (3, 1))):
+            moves[k, u, side] = send(
+                block_at(buffer, u, 0), block_at(buffer, u, block), s_send.at[k, u, side],
+                s_recv.at[k, u, side], device(dy=d),
+            )
+
+    def gather_relay(buffer, k, u):
+        for side, (d, block, cut) in enumerate(((1, 3, cut_a), (3, 1, cut_b))):
+            moves[k, u, side].wait_recv()
+            moves[k, u, 2 + side] = send(
+                block_at(buffer, u, block, cut), block_at(buffer, u, 2, cut),
+                s_send.at[k, u, 2 + side], s_recv.at[k, u, 2 + side], device(dy=d),
+            )
+
+    def gather_wait(k, u):
+        for side in range(2):
+            moves[k, u, side].wait_send()
+            moves[k, u, 2 + side].wait()
 
     loaded(0)
-    mixed_cat = jnp.concatenate([mixed_ref[i] for i in range(X)], axis=1)
+    mixed_cat = jnp.concatenate(
+        [
+            jnp.concatenate(
+                [mixed_ref[i, b * piece + u * sub : b * piece + (u + 1) * sub] for i in range(X)],
+                axis=1,
+            )
+            for u in range(2)
+            for b in range(Y)
+        ],
+        axis=0,
+    )
     for start, size in tiles(width, 512):
-        put(0, dot32(mixed_cat, out_w[:, start : start + size], ((1,), (0,))), start, size)
-    copies = start_scatter(0)
+        at = slice(start, start + size)
+        part = dot32(mixed_cat, out_w[:, at], ((1,), (0,)))
+        for u in range(2):
+            put(0, u, part[u * many : (u + 1) * many], start, size)
+    for u in range(2):
+        scatter_start(0, u)
     ratios = mago_ref[...] / jnp.sqrt(sq_ref[...])
     upper_o = (upper_ref[0:16] * ratios[0:1]).astype(BF16)
     upper_d = (upper_ref[16:32] * ratios[1:2]).astype(BF16)
     loaded(4)
     through_down = dot32(cot_ref[...], upper_d, ((1,), (1,))).astype(BF16)
-    attended = summed(0, copies)
-    acc[0] = attended
     gain = gain_ref[...]
-    resid = hid_ref[...].astype(F32) + attended
-    inverse = lax.rsqrt(jnp.mean(resid * resid, axis=1, keepdims=True) + epsilon)
-    resid_s[...] = resid
-    normed[0:piece] = (resid * inverse * gain).astype(BF16)
-    copies = start_gather(normed, 3)
-    more = relay(0, sent, 0, ff)
+    for u in range(2):
+        scatter_relay(0, u)
+    for u in range(2):
+        own = slice(u * sub, (u + 1) * sub)
+        attended = scatter_sum(0, u)
+        acc[0, own] = attended
+        resid = hid_ref[own].astype(F32) + attended
+        inverse = lax.rsqrt(jnp.mean(resid * resid, axis=1, keepdims=True) + epsilon)
+        resid_s[own] = resid
+        normed[u * many : u * many + sub] = (resid * inverse * gain).astype(BF16)
+        gather_start(normed, 2, u)
+        if u == 0:
+            more = relay(0, sent, 0, ff)
+            sm_copies = [
+                send(small_ref, small_x.at[d], sm_send.at[d - 1], sm_recv.at[d - 1], device(dx=d))
+                for d in NEAR_LAST
+            ]
     loaded(1)
     loaded(2)
     loaded(3)
-    for copy in copies:
-        copy.wait()
-    far = relay_far(0, more, 0, ff)
-    finish(sent, more, far)
-    for start, size in tiles(X * ff, 256):
-        at = slice(start, start + size)
-        gate = dot32(normed[...], gate_w[at], ((1,), (1,)))
-        up = dot32(normed[...], up_w[at], ((1,), (1,)))
-        d_act = dot32(cot_ref[...], down_w[at], ((1,), (1,)))
-        sig = 1.0 / (1.0 + jnp.exp(-gate))
-        gated = gate * sig
-        act[:, at] = (gated * up).astype(BF16)
-        d_gate = (d_act * up * sig * (1.0 + gate * (1.0 - sig))).astype(BF16)
-        d_up = (d_act * gated).astype(BF16)
-        dgate[:, at] = d_gate
-        dup[:, at] = d_up
-        mags[0:1, at] = jnp.sum(d_gate.astype(F32) * gate, axis=0, keepdims=True)
-        mags[1:2, at] = jnp.sum(d_up.astype(F32) * up, axis=0, keepdims=True)
-    for start, size in tiles(width, 512):
-        at = slice(start, start + size)
-        part = dot32(dgate[...], gate_w[:, at], ((1,), (0,)))
-        part = part + dot32(dup[...], up_w[:, at], ((1,), (0,)))
-        put(1, part, start, size)
-    two_copies = start_scatter(1)
+    for u in range(2):
+        gather_relay(normed, 2, u)
+    for u in range(2):
+        rows = slice(u * many, (u + 1) * many)
+        gather_wait(2, u)
+        for start, size in tiles(X * ff, 256):
+            at = slice(start, start + size)
+            gate_s[:, at] = dot32(normed[rows], gate_w[at], ((1,), (1,)))
+            up_s[:, at] = dot32(normed[rows], up_w[at], ((1,), (1,)))
+        if u == 0:
+            more_far = relay_far(0, more, 0, ff)
+            finish(sent, more, more_far)
+            for start, size in tiles(X * ff, 256):
+                at = slice(start, start + size)
+                dact_s[:, at] = dot32(cot_ref[...], down_w[at], ((1,), (1,)))
+        else:
+            scatter_relay(1, 0)
+        for start, size in tiles(X * ff, 256):
+            at = slice(start, start + size)
+            gate, up, d_act = gate_s[:, at], up_s[:, at], dact_s[rows, at]
+            sig = 1.0 / (1.0 + jnp.exp(-gate))
+            gated = gate * sig
+            act[rows, at] = (gated * up).astype(BF16)
+            d_gate = (d_act * up * sig * (1.0 + gate * (1.0 - sig))).astype(BF16)
+            d_up = (d_act * gated).astype(BF16)
+            dgate[rows, at] = d_gate
+            dup[rows, at] = d_up
+            both = jnp.concatenate(
+                [
+                    jnp.sum(d_gate.astype(F32) * gate, axis=0, keepdims=True),
+                    jnp.sum(d_up.astype(F32) * up, axis=0, keepdims=True),
+                ],
+                axis=0,
+            )
+            mags[:, at] = mags[:, at] + both if u else both
+        for start, size in tiles(width, 512):
+            at = slice(start, start + size)
+            part = dot32(dgate[rows], gate_w[:, at], ((1,), (0,)))
+            part = part + dot32(dup[rows], up_w[:, at], ((1,), (0,)))
+            put(1, u, part, start, size)
+        scatter_start(1, u)
+
+    def residual(u):
+        own = slice(u * sub, (u + 1) * sub)
+        d_two = scatter_sum(1, u)
+        resid = resid_s[own]
+        inverse = lax.rsqrt(jnp.mean(resid * resid, axis=1, keepdims=True) + epsilon)
+        scaled = d_two * gain
+        mean = jnp.mean(resid * scaled, axis=1, keepdims=True)
+        d_resid = cot_ref[u * many : u * many + sub].astype(F32) + (
+            inverse * scaled - resid * (inverse * inverse * inverse) * mean
+        )
+        resid_grad_out[own] = d_resid
+        own_low = d_resid.astype(BF16)
+        low[u * many : u * many + sub] = own_low
+        gather_start(low, 3, u)
+        return jnp.sum(own_low.astype(F32) * acc[0, own], axis=0, keepdims=True)
+
+    mag_first = residual(0)
+    scatter_relay(1, 1)
     for start, size in tiles(width, 512):
         at = slice(start, start + size)
         part = dot32(act[...], down_w[:, at], ((1,), (0,)))
-        ff_own[:, at] = part[:piece]
-        for d in range(1, Y):
-            ff_send[d - 1, :, at] = part[d * piece : (d + 1) * piece].astype(BF16)
+        for u in range(2):
+            own = slice(u * sub, (u + 1) * sub)
+            ff_own[own, at] = part[u * many : u * many + sub]
+            for d in range(1, Y):
+                first = u * many + d * sub
+                ff_send[d - 1, own, at] = part[first : first + sub].astype(BF16)
+    mag_second = residual(1)
+    for u in range(2):
+        gather_relay(low, 3, u)
     for copy in sm_copies:
         copy.wait()
     small = jnp.concatenate([small_ref[0:ff]] + [small_x[i, 0:ff] for i in range(1, X)], axis=0)
@@ -668,26 +774,19 @@
         pull_up, up_w[...], ((1,), (0,))
     )
     early_out[48:64] = dot32(from_act, cot_ref[...], ((0,), (0,)))
-    d_two = summed(1, two_copies)
-    resid = resid_s[...]
-    inverse = lax.rsqrt(jnp.mean(resid * resid, axis=1, keepdims=True) + epsilon)
-    scaled = d_two * gain
-    cot_own = cot_ref[0:piece].astype(F32)
-    d_resid = cot_own + (
-        inverse * scaled
-        - resid * (inverse * inverse * inverse) * jnp.mean(resid * scaled, axis=1, keepdims=True)
-    )
-    resid_grad_out[...] = d_resid
-    own_low = d_resid.astype(BF16)
-    low[0:piece] = own_low
-    copies = start_gather(low, 4)
-    mag_out = jnp.sum(own_low.astype(F32) * acc[0], axis=0, keepdims=True)
-    early_out[64:80] = jnp.concatenate([mag_out, jnp.zeros((15, width), F32)], axis=0)
-    for copy in copies:
-        copy.wait()
+    early_out[64:80] = jnp.concatenate(
+        [mag_first + mag_second, jnp.zeros((15, width), F32)], axis=0
+    )
+    for u in range(2):
+        gather_wait(3, u)
     d_mixed = dot32(low[...], out_w[...], ((1,), (1,))).astype(BF16)
     for i in range(X):
-        dmix_out[i] = d_mixed[:, i * HD : (i + 1) * HD]
+        for u in range(2):
+            for b in range(Y):
+                first = u * many + b * sub
+                dmix_out[i, b * piece + u * sub : b * piece + (u + 1) * sub] = d_mixed[
+                    first : first + sub, i * HD : (i + 1) * HD
+                ]
     through_out = dot32(low[...], upper_o, ((1,), (1,))).astype(BF16)
     value = dot32(through_out, mixed_cat, ((0,), (0,)))
     for i in range(X):
@@ -724,14 +823,20 @@
             pltpu.VMEM((here, many), BF16),
             pltpu.VMEM((here, many), BF16),
             pltpu.VMEM((here, many), BF16),
-            pltpu.VMEM((2, Y - 1, piece, width), BF16),
-            pltpu.VMEM((2, Y - 1, piece, width), BF16),
+            pltpu.VMEM((2, 2, piece // 2, width), BF16),
+            pltpu.VMEM((2, 2, 2, piece // 2, width), BF16),
+            pltpu.VMEM((2, 2, 2, piece // 2, width // 2), F32),
+            pltpu.VMEM((2, 2, 2, piece // 2, width // 2), BF16),
+            pltpu.VMEM((2, 2, 2, piece // 2, width), BF16),
             pltpu.VMEM((2, piece, width), F32),
             pltpu.VMEM((2, many), F32),
             pltpu.VMEM((piece, width), BF16),
             pltpu.VMEM((here, width), BF16),
+            pltpu.VMEM((here // 2, many), F32),
+            pltpu.VMEM((here // 2, many), F32),
+            pltpu.VMEM((here, many), F32),
             pltpu.VMEM((X,) + small.shape, BF16),
-            dma(4, X), dma(5, 3), dma(5, 3), dma(1 + Y), dma(3), dma(3), dma(1, 2), dma(1, 2), dma(1, 2), dma(1, 2),
+            dma(4, X), dma(4, 2, 6), dma(4, 2, 6), dma(1 + 2 * Y), dma(3), dma(3), dma(1, 2), dma(1, 2), dma(1, 2), dma(1, 2),
             dma(1, 3), dma(1, 3),
         ],
         1,

time: 303 us -> 294 us (0.970)
  Pallas kernels: 265 us -> 256 us
    pallas_call x1, Pallas kernels: 76.5 us -> 68.3 us  [feed(): call(feed_kernel, (s((piece, width), F32), s((piece, width), F32), s((pie...]
where the time goes in v4:
time: 294 us; the launch traced here: 291 us
  Pallas kernels  256 us (87%)
  other arithmetic  17.7 us (6%)
  local copies, waits for them, and re-layouts  11.1 us (4%)
  matrix products  4.39 us (1%)
    pallas_call x1, Pallas kernels, feed(): call(feed_kernel, (s((piece, width), F32), s((piece, width), F32), s((pie...  68.3 us
    pallas_call x1, Pallas kernels, tail(): call(tail_kernel, (s((rows, Y, piece, width), BF16), s((n, width), BF16),...  67.7 us
    pallas_call x1, Pallas kernels, front(): call(front_kernel, (s((X, here, HD), BF16), s((rows, here, HD), F32), s((...  63 us
    pallas_call x1, Pallas kernels, attend_back(): call(attend_back_kernel, (jax.ShapeDtypeStruct((rows, here, 3 * HD), BF16...  49.2 us
    pallas_call x1, Pallas kernels, widen(): pl.pallas_call(widen_kernel, out_shape=(jax.ShapeDtypeStruct((parts, many...  8.15 us

profile of v4, /device:TPU:0, one launch (start us, length us, event | category | flops | bytes accessed | tf_op | source)
XLA Modules:
  0.0 291.0 jit_solution(8704368693949733587)
XLA Ops:
  0.7 0.7 constant_dynamic-slice_fusion
  1.4 0.9 convert_reduce_fusion
  2.5 3.0 %multiply_sine_fusion = (f32[4,256,128]{2,1,0:T(8,128)}, f32[4,256,128]{2,1,0:T(8,128)}) fusion(f32[128]{0:T(128)S(1)} %pad_maximum_fusion.9, f32[4,256]{1,0:T(4,128)S(1)} %get-tuple-element.123), kind=kLoop, calls=%fused_computation.15 | loop fusion | flops 131072 | bytes 1053184 | tf_op jit(solution)/shard_map/sin | solution.py:1518
  5.5 1.0 copy.98.begin_ref
  6.8 0.9 copy.96.aw_ref
  8.4 0.9 fusion.43
  10.3 0.7 copy-done.6
  11.1 1.6 maximum_maximum_fusion
  12.9 1.0 pad_maximum_fusion.bw_ref
  14.0 0.7 select_maximum_fusion.small_ref
  14.8 0.6 pad_maximum_fusion.8.mago_ref
  15.6 1.7 copy.95.la_ref
  17.3 0.6 pad_maximum_fusion.7.ua_ref
  17.9 0.6 broadcast_in_dim.48.tag_ref
  19.2 1.0 reshape.109.mage_ref
  20.2 63.0 %shard_map.317 = (bf16[4,256,128]{2,1,0:T(8,128)(2,1)}, f32[4,256,128]{2,1,0:T(8,128)}, f32[4,256,1]{2,1,0:T(8,128)}, bf16[8,4,256,256]{3,2,1,0:T(8,128)(2,1)}, ...) custom-call(bf16[4,256,2048]{2,1,0:T(8,128)(2,1)} %hidden_ref.3, ...), custom_call_target="tpu_custom_call" | custom-call | flops 3221225472 | bytes 33554432 | tf_op jit(solution)/shard_map/pallas_call | solution.py:452
  83.2 0.7 pad_maximum_fusion.3.upper_ref
  83.9 0.6 broadcast_in_dim.52
  84.5 68.3 %shard_map.318 = (f32[64,2048]{1,0:T(8,128)}, f32[64,2048]{1,0:T(8,128)}, f32[64,2048]{1,0:T(8,128)}, bf16[3,64,2048]{2,1,0:T(8,128)(2,1)}, bf16[4,256,128]{2,1,...) custom-call(bf16[4,256,128]{2,1,0:T(8,128)(2,1)} %get-tuple-element.50.mixed_ref, ...), custom_call_target="tpu_custom_call" | custom-call | flops 8858370048 | bytes 33554432 | tf_op jit(solution)/shard_map/pallas_call | solution.py:802
  152.8 49.2 %shard_map.319 = (bf16[4,256,384]{2,1,0:T(8,128)(2,1)}, bf16[4,256,2048]{2,1,0:T(8,128)(2,1)}, f32[8,2048]{1,0:T(8,128)}) custom-call(bf16[4,256,128]{2,1,0:T(8,128)(2,1)} %get-tuple-element.48.q_ref, bf16[8,4,256,256]{3,2,1,0:T(8,128)(2,1)} %get-tuple-element.49.kv_ref, bf16[4,256,128]{2,1,0:T(8,128)(2,1)} %get-tuple-element.54.dmix_ref, ...), custom_call_target="tpu_custom_call" | custom-call | flops 2684354560 | bytes 33554432 | tf_op jit(solution)/shard_map/pallas_call | solution.py:1011
  202.0 67.7 %shard_map.320 = (bf16[4,4,64,2048]{3,2,1,0:T(8,128)(2,1)}, bf16[192,2048]{1,0:T(8,128)(2,1)}, f32[56,352]{1,0:T(8,128)}, f32[72,128]{1,0:T(8,128)}) custom-call(bf16[4,256,384]{2,1,0:T(8,128)(2,1)} %get-tuple-element.60.grads_ref, bf16[2048,384]{1,0:T(8,128)(2,1)} %get-tuple-element.61.weight_ref, bf16[4,256,2048]{2,1,0:T(8,128)(2,1)} %hidden_ref.3, ...), custom_call_target="tpu_custom_call" | custom-call | flops 1610612736 | bytes 16777216 | tf_op jit(solution)/shard_map/pallas_call | solution.py:1354
  269.7 1.4 convert_element_type.103
  272.1 1.9 fusion.3
  274.3 1.3 multiply_divide_fusion.1
  276.2 0.6 pad_maximum_fusion.6
  276.8 0.7 fusion.17
  278.4 0.8 fusion.7
  279.1 0.6 fusion.45
  279.8 8.1 %shard_map.321 = (f32[16,64,2048]{2,1,0:T(8,128)}, bf16[16,64,2048]{2,1,0:T(8,128)(2,1)}) custom-call(bf16[16,64,2048]{2,1,0:T(8,128)(2,1)} %bitcast.113, bf16[16,64,2048]{2,1,0:T(8,128)(2,1)} %bitcast.112), custom_call_target="tpu_custom_call" | custom-call | tf_op jit(solution)/shard_map/pallas_call | solution.py:1422
  287.9 0.8 slice_multiply_fusion
  288.7 0.7 slice_multiply_fusion.1
  289.4 0.6 slice.115
  (92 shorter events, 6.3 us)
Async XLA Ops:
  0.6 6.0 %copy-start.13 = (f32[2,16,352]{2,1,0:T(8,128)S(1)}, f32[2,16,352]{2,1,0:T(8,128)}, u32[]{:S(2)}) copy-start(f32[2,16,352]{2,1,0:T(8,128)} %param.38) | copy-start | bytes 135172
  0.7 6.0 %copy-start.11 = (f32[128,16]{0,1:T(8,128)S(1)}, f32[128,16]{0,1:T(8,128)}, u32[]{:S(2)}) copy-start(f32[128,16]{0,1:T(8,128)} %param.34) | copy-start | bytes 24580
  0.7 5.9 %copy-start.9 = (f32[352,16]{0,1:T(8,128)S(1)}, f32[352,16]{0,1:T(8,128)}, u32[]{:S(2)}) copy-start(f32[352,16]{0,1:T(8,128)} %param.40) | copy-start | bytes 67588
  0.7 7.0 %copy-start.4 = (f32[3,2048,16]{1,2,0:T(8,128)S(1)}, f32[3,2048,16]{1,2,0:T(8,128)}, u32[]{:S(2)}) copy-start(f32[3,2048,16]{1,2,0:T(8,128)} %param.31) | copy-start | bytes 1179652
  8.4 1.0 copy-start.5
  10.0 1.0 copy-start.6
  11.1 1.7 copy-start.2
  11.1 1.7 copy-start.3
  12.7 2.0 copy-start.16
  12.8 2.0 copy-start.17
  15.4 1.8 copy-start.10
  15.5 2.5 copy-start.15
  15.5 3.1 %copy-start.20 = (bf16[2048]{0:T(1024)(128)(2,1)S(1)}, bf16[2048]{0:T(1024)(128)(2,1)}, u32[]{:S(2)}) copy-start(bf16[2048]{0:T(1024)(128)(2,1)} %param.25) | copy-start | bytes 12292
  15.5 3.7 %copy-start.19 = (f32[2,352]{1,0:T(2,128)S(1)}, f32[2,352]{1,0:T(2,128)}, u32[]{:S(2)}) copy-start(f32[2,352]{1,0:T(2,128)} %param.39) | copy-start | bytes 8452
  20.2 63.7 %copy-start.21 = (bf16[2048]{0:T(1024)(128)(2,1)S(1)}, bf16[2048]{0:T(1024)(128)(2,1)}, u32[]{:S(2)}) copy-start(bf16[2048]{0:T(1024)(128)(2,1)} %param.26) | copy-start | bytes 12292
  269.6 1.4 copy-start.18
  269.7 2.0 copy-start
  271.6 2.4 copy-start.8
  271.6 4.0 %copy-start.7 = (f32[704,128]{1,0:T(8,128)S(1)}, f32[704,128]{1,0:T(8,128)}, u32[]{:S(2)}) copy-start(f32[704,128]{1,0:T(8,128)} %get-tuple-element.81) | copy-start | bytes 1081348
  274.1 2.1 copy-start.12
  275.7 1.9 copy-start.1
  276.1 2.2 copy-start.14
